TPU v7x, 256 devices: a whole 4x4x8 slice. The times are simulated.
256 devices in a mesh: pair: 8 (over y, z_hi), row: 8 (over z_lo, core), col: 4 (over x).
Axes of the slice: x: 4, y: 4, z: 8 (z_hi: 2, z_lo: 4; z = z_hi * 4 + z_lo), core: 2. Of those that a mesh axis runs over, the one named last changes fastest.
Arguments:
- voxels: float32 [2, 15, 128, 640], P(None, None, ('pair', 'row'), 'col'), parts along dimension 2, may hold values from -6 to 6
- disparity: float32 [2, 128, 640], P(None, ('pair', 'row'), 'col'), parts along dimension 1, may hold values from 0 to 192
- hidden: bfloat16 [2, 128, 640, 128], P(None, ('pair', 'row'), 'col'), parts along dimension 1, may hold values from -1 to 1
- context: bfloat16 [2, 128, 640, 384], P(None, ('pair', 'row'), 'col'), parts along dimension 1, may hold values from -6 to 6
- embed_first: float32 [15, 256], replicated, may hold values from -1.5 to 1.5
- embed_bias: float32 [256], replicated, may hold values from -4 to 4
- embed_second: bfloat16 [256, 256], replicated, may hold values from -0.375 to 0.375
- motion_weight: float32 [36, 128], replicated, may hold values from -1 to 1
- motion_scale: float32 [128], replicated, may hold values from -4 to 4
- motion_bias: float32 [128], replicated, may hold values from -3 to 3
- gate_kernel: bfloat16 [3, 3, 256, 256], replicated, may hold values from -0.125 to 0.125
- candidate_kernel: bfloat16 [3, 3, 256, 128], replicated, may hold values from -0.125 to 0.125
- head_weight: bfloat16 [128], replicated, may hold values from -0.5 to 0.5
Outputs:
- new_hidden: bfloat16 [2, 128, 640, 128], P(None, ('pair', 'row'), 'col'), parts along dimension 1
- increment: float32 [2, 128, 640], P(None, ('pair', 'row'), 'col'), parts along dimension 1
There are 8 independent parts, one for each index of `pair`. A program takes and returns all parts, laid end to end along the dimension named above; an argument that names none is the same for every part. Nothing has to cross between parts.
All inputs are finite; a program needn't handle non-finite values.
Results may differ from a plain program's by a relative error of at most 0.0085.
Values may be sent and summed in bfloat16 or wider, within the bound.
No kernel may reach another device: no remote copies, remote signals or barrier semaphores. Data moves between devices by JAX's collectives and lax.ppermute only.
A program may use at most 128 MiB of HBM per device.

v0:
```python
import jax
import jax.numpy as jnp
import numpy as np
from jax import lax
from jax.experimental import pallas as pl
from jax.experimental.pallas import tpu as pltpu
from jax.sharding import PartitionSpec as P

BF = jnp.bfloat16
F32 = jnp.float32

ROWS = 2
TILE = 160
IMAGE = 640
PAD = 16
EXT = TILE + 2 * PAD
BINS = 15
UNITS = 128
NEAR = 48
FAR = 72
WINDOW = 512
LAST = FAR + 2 * TILE + NEAR - 1
TAPS = 9
LEVELS = 4
GROUP = 40
STARTS = (0, 17, 30, 41)
VMEM_LIMIT = 48 * 1024 * 1024


def tables():
    pool = np.zeros((128, 128), np.float32)
    firsts = (28, 12, 4, 0)
    counts = (17, 13, 11, 10)
    for level in range(LEVELS):
        width = 2**level
        for k in range(counts[level]):
            entry = firsts[level] + k
            pool[entry * width : (entry + 1) * width, STARTS[level] + k] = 1.0 / (16 * width)
    lane = np.arange(128)
    member = lane % GROUP
    used = (member < LEVELS * TAPS) & (lane < 3 * GROUP)
    level = np.where(used, member // TAPS, 0)
    first = np.where(used, np.take(np.array(STARTS), level) + member % TAPS, 0)
    scale = np.where(used, 0.5**level, 0.0)
    low = ((lane >= GROUP) & (lane < 2 * GROUP)).astype(np.float32)
    rows = np.zeros((8, 128), np.float32)
    rows[0], rows[1], rows[2] = first, scale, low
    return np.concatenate([pool, pool]).astype(jnp.bfloat16), rows


def split(value):
    high = value.astype(BF).astype(F32)
    return high, value - high


def silu_of_half(half):
    return half + half * jnp.tanh(half)


def sigmoid(value):
    return 0.5 * jnp.tanh(0.5 * value) + 0.5


def pack_kernel(vox, disp, hidden, context, own, right, left, far, down, up):
    col = lax.axis_index("col")
    row_at = lax.broadcasted_iota(jnp.int32, (8, 128), 0)
    parts = []
    edges_right, edges_left = [], []
    for v in range(2):
        for y in range(ROWS):
            high, low = split(vox[v, :, y, :])
            ones = jnp.ones((1, TILE), F32)
            block = jnp.concatenate([high, ones, low, ones], axis=0)
            parts.append(block)
            own[2 * v + y] = jnp.concatenate(
                [block, jnp.zeros((32, 256 - TILE), F32)], axis=1
            ).astype(BF)
            hid_last = pltpu.roll(hidden[v, y, 144:160, :].astype(F32)[8:16], 2, 0)
            con_last = pltpu.roll(context[v, y, 144:160, UNITS : 2 * UNITS].astype(F32)[8:16], 3, 0)
            hid_first = hidden[v, y, 0:16, :].astype(F32)[0:8]
            con_first = pltpu.roll(context[v, y, 0:16, UNITS : 2 * UNITS].astype(F32)[0:8], 2, 0)
            depth = disp[v, y : y + 1, :]
            d_last = pltpu.roll(jnp.broadcast_to(depth[:, 32:160], (8, 128)), 8, 1)
            d_first = jnp.broadcast_to(depth[:, 0:128], (8, 128))

            def edge(hid, con, dis):
                d_high, rest = split(dis)
                d_mid, d_low = split(rest)
                out = jnp.where(row_at < 2, hid, con)
                out = jnp.where(row_at == 3, d_high, out)
                out = jnp.where(row_at == 4, d_mid, out)
                return jnp.where(row_at >= 5, d_low, out)

            edges_right.append(edge(hid_last, con_last, d_last))
            edges_left.append(edge(hid_first, con_first, d_first))
            for target, con_row in ((down, ROWS - 1), (up, 0)):
                target[v, y] = hidden[v, y]
                if y == con_row:
                    target[v, ROWS] = context[v, y, :, UNITS : 2 * UNITS]
    blank = jnp.zeros((32, 256 - TILE - NEAR), F32)
    for y in range(ROWS):
        f0, f1 = parts[y], parts[ROWS + y]
        right[32 * y : 32 * y + 32, :] = jnp.concatenate(
            [f1, f0[:, TILE - NEAR :], blank], axis=1
        ).astype(BF)
        left[32 * y : 32 * y + 32, :] = jnp.concatenate([f0, f1[:, :NEAR], blank], axis=1).astype(BF)
        tail = jnp.concatenate([f1[:, TILE - FAR :], jnp.zeros((32, 128 - FAR), F32)], axis=1)
        far[32 * y : 32 * y + 32, :] = jnp.where(col < 2, tail, f0[:, :128]).astype(BF)
    for target, edges in ((right, edges_right), (left, edges_left)):
        target[64:80, :] = jnp.concatenate(
            [
                jnp.concatenate([edges[0], edges[1]], axis=0),
                jnp.concatenate([edges[2], edges[3]], axis=0),
            ],
            axis=1,
        ).astype(BF)


def weight_kernel(first, bias, second, motion, w1, w1t, w2t, mw):
    w_high, w_low = split(first[...] * 0.5)
    b_high, rest = split(bias[...] * 0.5)
    b_mid, b_low = split(rest)
    stacked = jnp.concatenate([w_high, b_high, w_high, b_mid, w_low, b_low], axis=0)
    w1[...] = stacked.astype(BF)
    w1t[...] = jnp.concatenate([stacked, jnp.zeros((80, 256), F32)], axis=0).T.astype(BF)
    w2t[...] = second[...].astype(F32).T.astype(BF)
    m_high, m_low = split(motion[...])
    gap = jnp.zeros((GROUP - LEVELS * TAPS, 128), F32)
    mw[...] = jnp.concatenate(
        [m_high, gap, m_high, gap, m_low, gap, jnp.zeros((8, 128), F32)], axis=0
    ).astype(BF)


def motion_kernel(
    own, from_left, from_right, from_far, disp, w1, w1t, w2, w2t, mw, scale, bias, pool, rows, out
):
    col = lax.axis_index("col")
    far_scale_left = jnp.where(col >= 2, 1.0, 0.0).astype(F32)
    far_scale_right = 1.0 - far_scale_left
    edge_left = from_left[64:80, :].astype(F32)
    edge_right = from_right[64:80, :].astype(F32)

    def edge_of(edges, v, y):
        return edges[8 * y : 8 * y + 8, 128 * v : 128 * v + 128]

    depth_rows = []
    for v in range(2):
        for y in range(ROWS):
            e_l, e_r = edge_of(edge_left, v, y), edge_of(edge_right, v, y)
            d_l = e_l[3:4] + e_l[4:5] + e_l[5:6]
            d_r = e_r[3:4] + e_r[4:5] + e_r[5:6]
            depth_rows.append(
                jnp.concatenate(
                    [
                        jnp.zeros((1, 8), F32),
                        d_l[:, :8],
                        disp[v, y : y + 1, :],
                        d_r[:, :8],
                        jnp.zeros((1, 72), F32),
                    ],
                    axis=1,
                )
            )
    depth_rows.append(jnp.zeros((4, 256), F32))
    depths = jnp.concatenate(depth_rows, axis=0).T

    first = rows[0:1, :].astype(jnp.int32)
    level_scale = rows[1:2, :]
    is_low = rows[2:3, :] > 0.5
    lane = lax.broadcasted_iota(jnp.int32, (EXT, 128), 1)
    pixel = lax.broadcasted_iota(jnp.int32, (EXT, 1), 0)
    column = pixel + (col * TILE - PAD)
    inside = (column >= 0) & (column < IMAGE)
    pixel = pixel.astype(F32)
    depth_scale = scale[...] * (1.0 / 192.0)

    def lookups(scores, depth, v):
        spot = (pixel - PAD if v == 0 else (EXT - 1 - PAD) - pixel) - depth
        eighth = jnp.floor(spot * 0.125)
        rest = spot - 8.0 * eighth
        start = (8.0 * eighth).astype(jnp.int32) + (FAR + TILE - 32)
        index = start + lane if v == 0 else (LAST - start) - lane
        block, place = index >> 7, index & 127
        near = jnp.zeros((EXT, 128), F32)
        for k in range(WINDOW // 128):
            taken = jnp.take_along_axis(
                scores[:, 128 * k : 128 * k + 128], place, axis=1, mode="promise_in_bounds"
            )
            near = jnp.where(block == k, taken, near)
        high, low = split(near)
        pooled = jnp.dot(
            jnp.concatenate([high.astype(BF), low.astype(BF)], axis=1),
            pool[...],
            preferred_element_type=F32,
        )
        at = rest * level_scale
        floor = jnp.floor(at)
        weight = at - floor
        index = floor.astype(jnp.int32) + first
        lower = jnp.take_along_axis(pooled, index, axis=1, mode="promise_in_bounds")
        upper = jnp.take_along_axis(pooled, index + 1, axis=1, mode="promise_in_bounds")
        return lower + weight * (upper - lower)

    for y in range(ROWS):
        left = from_left[32 * y : 32 * y + 32, :].astype(F32)
        right = from_right[32 * y : 32 * y + 32, :].astype(F32)
        far = from_far[32 * y : 32 * y + 32, :].astype(F32)[:, :FAR]
        f0 = own[y].astype(F32)[:, :TILE]
        f1 = own[ROWS + y].astype(F32)[:, :TILE]
        blank = jnp.zeros((32, WINDOW - 1 - LAST), F32)
        win1 = jnp.concatenate(
            [far * far_scale_left, left[:, :TILE], f1, right[:, TILE : TILE + NEAR], blank], axis=1
        )
        win0 = jnp.concatenate(
            [left[:, TILE : TILE + NEAR], f0, right[:, :TILE], far * far_scale_right, blank], axis=1
        )
        query0 = win0[:, NEAR - PAD : NEAR - PAD + EXT]
        query1 = win1[:, FAR + TILE - PAD : FAR + TILE - PAD + EXT]
        for v, query, window in ((0, query0, win1), (1, query1, win0)):
            stacked = jnp.concatenate([query, query[:16]], axis=0)
            stacked = jnp.concatenate(
                [
                    jnp.concatenate([stacked, jnp.zeros((48, 256 - EXT), F32)], axis=1),
                    jnp.zeros((80, 256), F32),
                ],
                axis=0,
            ).T.astype(BF)
            layer = silu_of_half(
                jnp.dot(stacked[:EXT, :48], w1[...], preferred_element_type=F32)
            ).astype(BF)
            features = jnp.dot(layer, w2[...], preferred_element_type=F32).astype(BF)
            stacked = jnp.concatenate([window, window[:16]], axis=0).astype(BF)
            layer = silu_of_half(
                jnp.dot(w1t[:, :48], stacked, preferred_element_type=F32)
            ).astype(BF)
            match = jnp.dot(w2t[...], layer, preferred_element_type=F32).astype(BF)
            scores = jnp.dot(features, match, preferred_element_type=F32)
            depth = depths[:EXT, 2 * v + y : 2 * v + y + 1]
            look = lookups(scores, depth, v)
            high, low = split(look)
            half = 0.5 * (
                jnp.dot(
                    jnp.where(is_low, low, high).astype(BF), mw[...], preferred_element_type=F32
                )
                + depth * depth_scale
                + bias[...]
            )
            value = jnp.where(inside, silu_of_half(half), 0.0)
            out[v, y] = jnp.concatenate(
                [edge_of(edge_left, v, y), value[8 : EXT - 8], edge_of(edge_right, v, y)], axis=0
            ).astype(BF)


def update_kernel(
    hidden, context, hc_up, hc_down, mot, mot_up, mot_down, gate_k, cand_k, head, new, inc, state, reset
):
    def mot_of(v, yy):
        if yy < 2:
            return mot_up[v, yy]
        if yy < 4:
            return mot[v, yy - 2]
        return mot_down[v, yy - 4]

    def widened(middle, value, shift_left, shift_right):
        ends_left = pltpu.roll(value[0:16].astype(F32), shift_left, 0).astype(BF)
        ends_right = pltpu.roll(value[EXT - 16 :].astype(F32), shift_right, 0).astype(BF)
        return jnp.concatenate([ends_left, middle, ends_right], axis=0)

    def spread(products, width, v):
        before, at, after = (products[:, width * b : width * b + width] for b in range(3))
        if v == 1:
            before, after = after, before
        return pltpu.roll(before, 1, 0) + at + pltpu.roll(after, EXT - 1, 0)

    gate_all = jnp.concatenate(
        [jnp.concatenate([gate_k[a, b] for a in range(3)], axis=0) for b in range(3)], axis=1
    )
    gate_reset = jnp.concatenate(
        [
            jnp.concatenate([gate_k[a, b, :, UNITS:] for a in range(3)], axis=0)
            for b in range(3)
        ],
        axis=1,
    )
    cand_all = jnp.concatenate(
        [jnp.concatenate([cand_k[a, b] for a in range(3)], axis=0) for b in range(3)], axis=1
    )
    head_rows = jnp.broadcast_to(head[...].astype(F32), (8, UNITS)).astype(BF)
    for v in range(2):
        for yy in range(6):
            if yy < 2:
                middle = hc_up[v, yy]
            elif yy < 4:
                middle = hidden[v, yy - 2]
            else:
                middle = hc_down[v, yy - 4]
            state[v, yy] = widened(middle, mot_of(v, yy), 14, 8)
        gates = [None, None]
        for yy in range(1, 5):
            stacked = jnp.concatenate(
                [piece for k in (yy - 1, yy, yy + 1) for piece in (state[v, k], mot_of(v, k))],
                axis=1,
            )
            if yy in (2, 3):
                terms = spread(
                    jnp.dot(stacked, gate_all, preferred_element_type=F32), 2 * UNITS, v
                )
                gates[yy - 2] = terms[PAD : PAD + TILE, :UNITS]
                terms = terms[:, UNITS:]
                own_context = context[v, yy - 2, :, UNITS : 2 * UNITS]
            else:
                terms = spread(jnp.dot(stacked, gate_reset, preferred_element_type=F32), UNITS, v)
                own_context = hc_up[v, ROWS] if yy == 1 else hc_down[v, ROWS]
            wide = widened(own_context, mot_of(v, yy), 13, 6)
            gate = sigmoid(terms + wide.astype(F32))
            reset[v, yy - 1] = (gate * state[v, yy].astype(F32)).astype(BF)
        for y in range(ROWS):
            stacked = jnp.concatenate(
                [piece for k in range(3) for piece in (reset[v, y + k], mot_of(v, y + 1 + k))],
                axis=1,
            )
            terms = spread(jnp.dot(stacked, cand_all, preferred_element_type=F32), UNITS, v)
            candidate = jnp.tanh(
                terms[PAD : PAD + TILE] + context[v, y, :, 2 * UNITS :].astype(F32)
            )
            update = sigmoid(gates[y] + context[v, y, :, :UNITS].astype(F32))
            old = hidden[v, y].astype(F32)
            fresh = ((1.0 - update) * old + update * candidate).astype(BF)
            new[v, y] = fresh
            inc[v, y : y + 1, :] = lax.dot_general(
                head_rows, fresh, (((1,), (1,)), ((), ())), preferred_element_type=F32
            )[0:1]


def call(kernel, outs, scratch=(), **cost):
    return pl.pallas_call(
        kernel,
        out_shape=[jax.ShapeDtypeStruct(shape, dtype) for shape, dtype in outs],
        scratch_shapes=list(scratch),
        compiler_params=pltpu.CompilerParams(vmem_limit_bytes=VMEM_LIMIT),
        cost_estimate=pl.CostEstimate(transcendentals=0, **cost),
    )


def local(
    voxels,
    disparity,
    hidden,
    context,
    embed_first,
    embed_bias,
    embed_second,
    motion_weight,
    motion_scale,
    motion_bias,
    gate_kernel,
    candidate_kernel,
    head_weight,
):
    cols = lax.axis_size("col")
    rows = lax.axis_size("row")
    onward = [(i, i + 1) for i in range(cols - 1)]
    back = [(i + 1, i) for i in range(cols - 1)]
    across = [(i, (i + 2) % cols) for i in range(cols)]
    downward = [(i, i + 1) for i in range(rows - 1)]
    upward = [(i + 1, i) for i in range(rows - 1)]
    pool, lane_rows = tables()

    own, right, left, far, down, up = call(
        pack_kernel,
        [
            ((4, 32, 256), BF),
            ((80, 256), BF),
            ((80, 256), BF),
            ((64, 128), BF),
            ((2, 3, TILE, UNITS), BF),
            ((2, 3, TILE, UNITS), BF),
        ],
        flops=10**6,
        bytes_accessed=2 * 10**6,
    )(voxels, disparity, hidden, context)
    from_left = lax.ppermute(right, "col", onward)
    from_right = lax.ppermute(left, "col", back)
    from_far = lax.ppermute(far, "col", across)
    hc_up = lax.ppermute(down, "row", downward)
    hc_down = lax.ppermute(up, "row", upward)
    w1, w1t, w2t, mw = call(
        weight_kernel,
        [((48, 256), BF), ((256, 128), BF), ((256, 256), BF), ((128, 128), BF)],
        flops=10**6,
        bytes_accessed=10**6,
    )(embed_first, embed_bias.reshape(1, -1), embed_second, motion_weight)
    (motion,) = call(
        motion_kernel,
        [((2, ROWS, EXT, UNITS), BF)],
        flops=10**9,
        bytes_accessed=10**6,
    )(
        own,
        from_left,
        from_right,
        from_far,
        disparity,
        w1,
        w1t,
        embed_second,
        w2t,
        mw,
        motion_scale.reshape(1, -1),
        motion_bias.reshape(1, -1),
        jnp.asarray(pool),
        jnp.asarray(lane_rows),
    )
    motion_up = lax.ppermute(motion, "row", downward)
    motion_down = lax.ppermute(motion, "row", upward)
    new_hidden, increment = call(
        update_kernel,
        [((2, ROWS, TILE, UNITS), BF), ((2, ROWS, TILE), F32)],
        scratch=[pltpu.VMEM((2, 6, EXT, UNITS), BF), pltpu.VMEM((2, 4, EXT, UNITS), BF)],
        flops=2 * 10**9,
        bytes_accessed=4 * 10**6,
    )(
        hidden,
        context,
        hc_up,
        hc_down,
        motion,
        motion_up,
        motion_down,
        gate_kernel,
        candidate_kernel,
        head_weight.reshape(1, -1),
    )
    return new_hidden, increment


def solution(mesh):
    band = ("pair", "row")
    in_specs = (
        P(None, None, band, "col"),
        P(None, band, "col"),
        P(None, band, "col", None),
        P(None, band, "col", None),
    ) + (P(),) * 9
    out_specs = (P(None, band, "col", None), P(None, band, "col"))
    return jax.shard_map(local, mesh=mesh, in_specs=in_specs, out_specs=out_specs, check_vma=False)
```

profile of v0, /device:TPU:1, one launch (start us, length us, event | category | flops | bytes accessed | tf_op | source)
XLA Modules:
  0.0 47.0 jit_solution(6082305717057614206)
XLA Ops:
  0.6 1.0 %copy-done = bf16[2,2,160,384]{3,2,1,0:T(8,128)(2,1)S(1)} copy-done((bf16[2,2,160,384]{3,2,1,0:T(8,128)(2,1)S(1)}, bf16[2,2,160,384]{3,2,1,0:T(8,128)(2,1)}, u32[]{:S(2)}) %copy-start) | copy-done | bytes 491544
  1.7 0.9 %copy-done.2 = bf16[2,2,160,128]{3,2,1,0:T(8,128)(2,1)S(1)} copy-done((bf16[2,2,160,128]{3,2,1,0:T(8,128)(2,1)S(1)}, bf16[2,2,160,128]{3,2,1,0:T(8,128)(2,1)}, u32[]{:S(2)}) %copy-start.2) | copy-done | bytes 163864
  2.6 0.8 %copy-done.6 = f32[2,15,2,160]{3,2,1,0:T(2,128)S(1)} copy-done((f32[2,15,2,160]{3,2,1,0:T(2,128)S(1)}, f32[2,15,2,160]{3,2,1,0:T(2,128)}, u32[]{:S(2)}) %copy-start.6) | copy-done | bytes 38424
  3.4 0.7 %copy-done.9 = f32[2,2,160]{2,1,0:T(2,128)S(1)} copy-done((f32[2,2,160]{2,1,0:T(2,128)S(1)}, f32[2,2,160]{2,1,0:T(2,128)}, u32[]{:S(2)}) %copy-start.9) | copy-done | bytes 2584
  4.4 3.9 %collective-permute-start.2 = (bf16[80,256]{1,0:T(8,128)(2,1)S(1)}, bf16[80,256]{1,0:T(8,128)(2,1)S(1)}, u32[]{:S(2)}, u32[]{:S(2)}) collective-permute-start(bf16[80,256]{1,0:T(8,128)(2,1)S(1)} %get-tuple-element.15), channel_id=1, source_target_pairs={{0,1},{1,2},{2,3},{4,5},{5,6},{6,7},{8,9},{9,10},{10,11},{12,13},{... | collective-permute-start | bytes 122888 | tf_op jit(solution)/shard_map/ppermute | solution.py:382
  8.3 1.3 %collective-permute-start.3 = (bf16[80,256]{1,0:T(8,128)(2,1)S(1)}, bf16[80,256]{1,0:T(8,128)(2,1)S(1)}, u32[]{:S(2)}, u32[]{:S(2)}) collective-permute-start(bf16[80,256]{1,0:T(8,128)(2,1)S(1)} %get-tuple-element.16), channel_id=1, source_target_pairs={{1,0},{2,1},{3,2},{5,4},{6,5},{7,6},{9,8},{10,9},{11,10},{13,12},{... | collective-permute-start | bytes 122888 | tf_op jit(solution)/shard_map/ppermute | solution.py:383
  9.6 3.7 %collective-permute-start.4 = (bf16[64,128]{1,0:T(8,128)(2,1)S(1)}, bf16[64,128]{1,0:T(8,128)(2,1)S(1)}, u32[]{:S(2)}, u32[]{:S(2)}) collective-permute-start(bf16[64,128]{1,0:T(8,128)(2,1)S(1)} %get-tuple-element.17), channel_id=1, source_target_pairs={{0,2},{1,3},{2,0},{3,1},{4,6},{5,7},{6,4},{7,5},{8,10},{9,11},{10,... | collective-permute-start | bytes 49160 | tf_op jit(solution)/shard_map/ppermute | solution.py:384
  13.3 4.9 %collective-permute-start = (bf16[2,3,160,128]{3,2,1,0:T(8,128)(2,1)S(1)}, bf16[2,3,160,128]{3,2,1,0:T(8,128)(2,1)S(1)}, u32[]{:S(2)}, u32[]{:S(2)}) collective-permute-start(bf16[2,3,160,128]{3,2,1,0:T(8,128)(2,1)S(1)} %get-tuple-element.12), channel_id=1, source_target_pairs={{0,4},{4,8},{8,12},{12,16},{16,20},{20,24},{24,28},{1,5},{5,9},{9,... | collective-permute-start | bytes 737288 | tf_op jit(solution)/shard_map/ppermute | solution.py:385
  18.3 1.9 %collective-permute-start.1 = (bf16[2,3,160,128]{3,2,1,0:T(8,128)(2,1)S(1)}, bf16[2,3,160,128]{3,2,1,0:T(8,128)(2,1)S(1)}, u32[]{:S(2)}, u32[]{:S(2)}) collective-permute-start(bf16[2,3,160,128]{3,2,1,0:T(8,128)(2,1)S(1)} %get-tuple-element.13), channel_id=1, source_target_pairs={{4,0},{8,4},{12,8},{16,12},{20,16},{24,20},{28,24},{5,1},{9,5},{13... | collective-permute-start | bytes 737288 | tf_op jit(solution)/shard_map/ppermute | solution.py:386
  20.2 0.9 %copy-done.4 = bf16[256,256]{1,0:T(8,128)(2,1)S(1)} copy-done((bf16[256,256]{1,0:T(8,128)(2,1)S(1)}, bf16[256,256]{1,0:T(8,128)(2,1)}, u32[]{:S(2)}) %copy-start.4) | copy-done | bytes 131096
  21.1 0.7 %copy-done.7 = f32[36,128]{1,0:T(8,128)S(1)} copy-done((f32[36,128]{1,0:T(8,128)S(1)}, f32[36,128]{1,0:T(8,128)}, u32[]{:S(2)}) %copy-start.7) | copy-done | bytes 18456
  21.8 0.7 %copy-done.8 = f32[15,256]{1,0:T(8,128)S(1)} copy-done((f32[15,256]{1,0:T(8,128)S(1)}, f32[15,256]{1,0:T(8,128)}, u32[]{:S(2)}) %copy-start.8) | copy-done | bytes 15384
  22.6 0.7 %copy-done.11 = f32[256]{0:T(256)S(1)} copy-done((f32[256]{0:T(256)S(1)}, f32[256]{0:T(256)}, u32[]{:S(2)}) %copy-start.11) | copy-done | bytes 1048
  23.4 0.9 %copy-done.5 = bf16[256,256]{1,0:T(8,128)(2,1)S(1)} copy-done((bf16[256,256]{1,0:T(8,128)(2,1)S(1)}, bf16[256,256]{1,0:T(8,128)(2,1)}, u32[]{:S(2)}) %copy-start.5) | copy-done | bytes 131096
  24.3 0.7 %copy-done.10 = f32[2,2,160]{2,1,0:T(2,128)S(1)} copy-done((f32[2,2,160]{2,1,0:T(2,128)S(1)}, f32[2,2,160]{2,1,0:T(2,128)}, u32[]{:S(2)}) %copy-start.10) | copy-done | bytes 2584
  25.0 0.7 %copy-done.14 = f32[128]{0:T(128)S(1)} copy-done((f32[128]{0:T(128)S(1)}, f32[128]{0:T(128)}, u32[]{:S(2)}) %copy-start.14) | copy-done | bytes 536
  26.3 0.8 %copy-done.17 = bf16[256,128]{1,0:T(8,128)(2,1)S(1)} copy-done((bf16[256,128]{1,0:T(8,128)(2,1)S(1)}, bf16[256,128]{1,0:T(8,128)(2,1)}, u32[]{:S(2)}) %copy-start.17) | copy-done | bytes 65560
  27.2 0.7 %copy-done.18 = f32[8,128]{1,0:T(8,128)S(1)} copy-done((f32[8,128]{1,0:T(8,128)S(1)}, f32[8,128]{1,0:T(8,128)}, u32[]{:S(2)}) %copy-start.18) | copy-done | bytes 4120
  27.9 4.9 %shard_map.160.mot = bf16[2,2,192,128]{3,2,1,0:T(8,128)(2,1)S(1)} custom-call(bf16[4,32,256]{2,1,0:T(8,128)(2,1)S(1)} %get-tuple-element.14.own, bf16[80,256]{1,0:T(8,128)(2,1)S(1)} %collective-permute-done.2.from_left, bf16[80,256]{1,0:T(8,128)(2,1)S(1)} %collective-permute-done.3.from_right, bf16[64,128]{1,0:T(8,128)(2,1)S(1)} %collective-permute-done.4.from_far, ...), custom_call_target="tpu_custom_call" | custom-call | flops 1000000000 | bytes 1000000 | tf_op jit(solution)/shard_map/pallas_call | solution.py:393
  32.7 3.6 %collective-permute-start.5 = (bf16[2,2,192,128]{3,2,1,0:T(8,128)(2,1)S(1)}, bf16[2,2,192,128]{3,2,1,0:T(8,128)(2,1)S(1)}, u32[]{:S(2)}, u32[]{:S(2)}) collective-permute-start(bf16[2,2,192,128]{3,2,1,0:T(8,128)(2,1)S(1)} %shard_map.160.mot), channel_id=1, source_target_pairs={{0,4},{4,8},{8,12},{12,16},{16,20},{20,24},{24,28},{1,5},{5,9},{9,... | collective-permute-start | bytes 589832 | tf_op jit(solution)/shard_map/ppermute | solution.py:414
  36.4 1.9 %collective-permute-start.6 = (bf16[2,2,192,128]{3,2,1,0:T(8,128)(2,1)S(1)}, bf16[2,2,192,128]{3,2,1,0:T(8,128)(2,1)S(1)}, u32[]{:S(2)}, u32[]{:S(2)}) collective-permute-start(bf16[2,2,192,128]{3,2,1,0:T(8,128)(2,1)S(1)} %shard_map.160.mot), channel_id=1, source_target_pairs={{4,0},{8,4},{12,8},{16,12},{20,16},{24,20},{28,24},{5,1},{9,5},{13... | collective-permute-start | bytes 589832 | tf_op jit(solution)/shard_map/ppermute | solution.py:415
  38.3 0.7 %collective-permute-done.5.mot_up = bf16[2,2,192,128]{3,2,1,0:T(8,128)(2,1)S(1)} collective-permute-done((bf16[2,2,192,128]{3,2,1,0:T(8,128)(2,1)S(1)}, bf16[2,2,192,128]{3,2,1,0:T(8,128)(2,1)S(1)}, u32[]{:S(2)}, u32[]{:S(2)}) %collective-permute-start.5) | collective-permute-done | bytes 196640 | tf_op jit(solution)/shard_map/ppermute | solution.py:414
  39.0 4.4 %collective-permute-done.6.mot_down = bf16[2,2,192,128]{3,2,1,0:T(8,128)(2,1)S(1)} collective-permute-done((bf16[2,2,192,128]{3,2,1,0:T(8,128)(2,1)S(1)}, bf16[2,2,192,128]{3,2,1,0:T(8,128)(2,1)S(1)}, u32[]{:S(2)}, u32[]{:S(2)}) %collective-permute-start.6) | collective-permute-done | bytes 196640 | tf_op jit(solution)/shard_map/ppermute | solution.py:415
  43.4 3.5 %shard_map.161 = (bf16[2,2,160,128]{3,2,1,0:T(8,128)(2,1)}, f32[2,2,160]{2,1,0:T(2,128)}) custom-call(bf16[2,2,160,128]{3,2,1,0:T(8,128)(2,1)S(1)} %copy-done.3, bf16[2,2,160,384]{3,2,1,0:T(8,128)(2,1)S(1)} %copy-done.1, bf16[2,3,160,128]{3,2,1,0:T(8,128)(2,1)S(1)} %collective-permute-done.hc_up, ...), custom_call_target="tpu_custom_call" | custom-call | flops 2000000000 | bytes 4000000 | tf_op jit(solution)/shard_map/pallas_call | solution.py:416
  (32 shorter events, 1.1 us)
Async XLA Ops:
  0.6 1.0 %copy-start = (bf16[2,2,160,384]{3,2,1,0:T(8,128)(2,1)S(1)}, bf16[2,2,160,384]{3,2,1,0:T(8,128)(2,1)}, u32[]{:S(2)}) copy-start(bf16[2,2,160,384]{3,2,1,0:T(8,128)(2,1)} %context.3) | copy-start | bytes 1474564
  1.7 0.9 %copy-start.2 = (bf16[2,2,160,128]{3,2,1,0:T(8,128)(2,1)S(1)}, bf16[2,2,160,128]{3,2,1,0:T(8,128)(2,1)}, u32[]{:S(2)}) copy-start(bf16[2,2,160,128]{3,2,1,0:T(8,128)(2,1)} %hidden.3) | copy-start | bytes 491524
  2.6 0.8 %copy-start.6 = (f32[2,15,2,160]{3,2,1,0:T(2,128)S(1)}, f32[2,15,2,160]{3,2,1,0:T(2,128)}, u32[]{:S(2)}) copy-start(f32[2,15,2,160]{3,2,1,0:T(2,128)} %vox.1) | copy-start | bytes 115204
  3.4 0.7 %copy-start.9 = (f32[2,2,160]{2,1,0:T(2,128)S(1)}, f32[2,2,160]{2,1,0:T(2,128)}, u32[]{:S(2)}) copy-start(f32[2,2,160]{2,1,0:T(2,128)} %disp.3) | copy-start | bytes 7684
  4.4 19.0 %collective-permute-start.2 = (bf16[80,256]{1,0:T(8,128)(2,1)S(1)}, bf16[80,256]{1,0:T(8,128)(2,1)S(1)}, u32[]{:S(2)}, u32[]{:S(2)}) collective-permute-start(bf16[80,256]{1,0:T(8,128)(2,1)S(1)} %get-tuple-element.15), channel_id=1, source_target_pairs={{0,1},{1,2},{2,3},{4,5},{5,6},{6,7},{8,9},{9,10},{10,11},{12,13},{... | collective-permute-start | bytes 122888 | tf_op jit(solution)/shard_map/ppermute | solution.py:382
  8.3 15.1 %collective-permute-start.3 = (bf16[80,256]{1,0:T(8,128)(2,1)S(1)}, bf16[80,256]{1,0:T(8,128)(2,1)S(1)}, u32[]{:S(2)}, u32[]{:S(2)}) collective-permute-start(bf16[80,256]{1,0:T(8,128)(2,1)S(1)} %get-tuple-element.16), channel_id=1, source_target_pairs={{1,0},{2,1},{3,2},{5,4},{6,5},{7,6},{9,8},{10,9},{11,10},{13,12},{... | collective-permute-start | bytes 122888 | tf_op jit(solution)/shard_map/ppermute | solution.py:383
  9.6 13.8 %collective-permute-start.4 = (bf16[64,128]{1,0:T(8,128)(2,1)S(1)}, bf16[64,128]{1,0:T(8,128)(2,1)S(1)}, u32[]{:S(2)}, u32[]{:S(2)}) collective-permute-start(bf16[64,128]{1,0:T(8,128)(2,1)S(1)} %get-tuple-element.17), channel_id=1, source_target_pairs={{0,2},{1,3},{2,0},{3,1},{4,6},{5,7},{6,4},{7,5},{8,10},{9,11},{10,... | collective-permute-start | bytes 49160 | tf_op jit(solution)/shard_map/ppermute | solution.py:384
  13.3 30.1 %collective-permute-start = (bf16[2,3,160,128]{3,2,1,0:T(8,128)(2,1)S(1)}, bf16[2,3,160,128]{3,2,1,0:T(8,128)(2,1)S(1)}, u32[]{:S(2)}, u32[]{:S(2)}) collective-permute-start(bf16[2,3,160,128]{3,2,1,0:T(8,128)(2,1)S(1)} %get-tuple-element.12), channel_id=1, source_target_pairs={{0,4},{4,8},{8,12},{12,16},{16,20},{20,24},{24,28},{1,5},{5,9},{9,... | collective-permute-start | bytes 737288 | tf_op jit(solution)/shard_map/ppermute | solution.py:385
  18.3 25.1 %collective-permute-start.1 = (bf16[2,3,160,128]{3,2,1,0:T(8,128)(2,1)S(1)}, bf16[2,3,160,128]{3,2,1,0:T(8,128)(2,1)S(1)}, u32[]{:S(2)}, u32[]{:S(2)}) collective-permute-start(bf16[2,3,160,128]{3,2,1,0:T(8,128)(2,1)S(1)} %get-tuple-element.13), channel_id=1, source_target_pairs={{4,0},{8,4},{12,8},{16,12},{20,16},{24,20},{28,24},{5,1},{9,5},{13... | collective-permute-start | bytes 737288 | tf_op jit(solution)/shard_map/ppermute | solution.py:386
  20.2 0.9 %copy-start.4 = (bf16[256,256]{1,0:T(8,128)(2,1)S(1)}, bf16[256,256]{1,0:T(8,128)(2,1)}, u32[]{:S(2)}) copy-start(bf16[256,256]{1,0:T(8,128)(2,1)} %w2.1) | copy-start | bytes 393220
  21.1 0.7 %copy-start.7 = (f32[36,128]{1,0:T(8,128)S(1)}, f32[36,128]{1,0:T(8,128)}, u32[]{:S(2)}) copy-start(f32[36,128]{1,0:T(8,128)} %motion.1) | copy-start | bytes 55300
  21.8 0.7 %copy-start.8 = (f32[15,256]{1,0:T(8,128)S(1)}, f32[15,256]{1,0:T(8,128)}, u32[]{:S(2)}) copy-start(f32[15,256]{1,0:T(8,128)} %first.1) | copy-start | bytes 46084
  22.6 0.7 %copy-start.11 = (f32[256]{0:T(256)S(1)}, f32[256]{0:T(256)}, u32[]{:S(2)}) copy-start(f32[256]{0:T(256)} %param.20) | copy-start | bytes 3076
  23.4 0.9 %copy-start.5 = (bf16[256,256]{1,0:T(8,128)(2,1)S(1)}, bf16[256,256]{1,0:T(8,128)(2,1)}, u32[]{:S(2)}) copy-start(bf16[256,256]{1,0:T(8,128)(2,1)} %w2.1) | copy-start | bytes 393220
  24.3 0.7 %copy-start.10 = (f32[2,2,160]{2,1,0:T(2,128)S(1)}, f32[2,2,160]{2,1,0:T(2,128)}, u32[]{:S(2)}) copy-start(f32[2,2,160]{2,1,0:T(2,128)} %disp.3) | copy-start | bytes 7684
  26.3 0.8 %copy-start.17 = (bf16[256,128]{1,0:T(8,128)(2,1)S(1)}, bf16[256,128]{1,0:T(8,128)(2,1)}, u32[]{:S(2)}) copy-start(bf16[256,128]{1,0:T(8,128)(2,1)} %constant.4.clone.pool) | copy-start | bytes 196612
  27.2 0.7 %copy-start.18 = (f32[8,128]{1,0:T(8,128)S(1)}, f32[8,128]{1,0:T(8,128)}, u32[]{:S(2)}) copy-start(f32[8,128]{1,0:T(8,128)} %constant.5.clone.rows) | copy-start | bytes 12292
  27.8 15.6 %copy-start.1 = (bf16[2,2,160,384]{3,2,1,0:T(8,128)(2,1)S(1)}, bf16[2,2,160,384]{3,2,1,0:T(8,128)(2,1)}, u32[]{:S(2)}) copy-start(bf16[2,2,160,384]{3,2,1,0:T(8,128)(2,1)} %context.3) | copy-start | bytes 1474564
  27.8 15.6 %copy-start.3 = (bf16[2,2,160,128]{3,2,1,0:T(8,128)(2,1)S(1)}, bf16[2,2,160,128]{3,2,1,0:T(8,128)(2,1)}, u32[]{:S(2)}) copy-start(bf16[2,2,160,128]{3,2,1,0:T(8,128)(2,1)} %hidden.3) | copy-start | bytes 491524
  27.9 15.6 %copy-start.12 = (bf16[3,3,256,256]{3,2,1,0:T(8,128)(2,1)S(1)}, bf16[3,3,256,256]{3,2,1,0:T(8,128)(2,1)}, u32[]{:S(2)}) copy-start(bf16[3,3,256,256]{3,2,1,0:T(8,128)(2,1)} %gate_k.1) | copy-start | bytes 3538948
  27.9 15.6 %copy-start.13 = (bf16[3,3,256,128]{3,2,1,0:T(8,128)(2,1)S(1)}, bf16[3,3,256,128]{3,2,1,0:T(8,128)(2,1)}, u32[]{:S(2)}) copy-start(bf16[3,3,256,128]{3,2,1,0:T(8,128)(2,1)} %cand_k.1) | copy-start | bytes 1769476
  27.9 15.6 %copy-start.16 = (bf16[128]{0:T(256)(128)(2,1)S(1)}, bf16[128]{0:T(256)(128)(2,1)}, u32[]{:S(2)}) copy-start(bf16[128]{0:T(256)(128)(2,1)} %param.27) | copy-start | bytes 772
  32.7 6.2 %collective-permute-start.5 = (bf16[2,2,192,128]{3,2,1,0:T(8,128)(2,1)S(1)}, bf16[2,2,192,128]{3,2,1,0:T(8,128)(2,1)S(1)}, u32[]{:S(2)}, u32[]{:S(2)}) collective-permute-start(bf16[2,2,192,128]{3,2,1,0:T(8,128)(2,1)S(1)} %shard_map.160.mot), channel_id=1, source_target_pairs={{0,4},{4,8},{8,12},{12,16},{16,20},{20,24},{24,28},{1,5},{5,9},{9,... | collective-permute-start | bytes 589832 | tf_op jit(solution)/shard_map/ppermute | solution.py:414
  36.4 7.0 %collective-permute-start.6 = (bf16[2,2,192,128]{3,2,1,0:T(8,128)(2,1)S(1)}, bf16[2,2,192,128]{3,2,1,0:T(8,128)(2,1)S(1)}, u32[]{:S(2)}, u32[]{:S(2)}) collective-permute-start(bf16[2,2,192,128]{3,2,1,0:T(8,128)(2,1)S(1)} %shard_map.160.mot), channel_id=1, source_target_pairs={{4,0},{8,4},{12,8},{16,12},{20,16},{24,20},{28,24},{5,1},{9,5},{13... | collective-permute-start | bytes 589832 | tf_op jit(solution)/shard_map/ppermute | solution.py:415
  (2 other events, 1.3 us)
where the time goes:
time: 47.7 us; the launch traced here: 47 us
  starting transfers between devices  21.4 us (45%)
  local copies, waits for them, and re-layouts  10.9 us (23%)
  Pallas kernels  8.84 us (19%)
  waiting for transfers between devices  5.07 us (11%)
  between operations  0.8 us (2%)
    unnamed x38, local copies, waits for them, and re-layouts  10.9 us
    ppermute x1, starting transfers between devices, local(): hc_up = lax.ppermute(down, 'row', downward)  4.93 us
    pallas_call x1, Pallas kernels, local(): call(motion_kernel, [((2, ROWS, EXT, UNITS), BF)], flops=10 ** 9, bytes_a...  4.87 us
    ppermute x1, waiting for transfers between devices, local(): motion_down = lax.ppermute(motion, 'row', upward)  4.4 us
    ppermute x1, starting transfers between devices, local(): from_left = lax.ppermute(right, 'col', onward)  3.95 us
    ppermute x1, starting transfers between devices, local(): from_far = lax.ppermute(far, 'col', across)  3.7 us
    ppermute x1, starting transfers between devices, local(): motion_up = lax.ppermute(motion, 'row', downward)  3.65 us
    pallas_call x1, Pallas kernels, local(): call(update_kernel, [((2, ROWS, TILE, UNITS), BF), ((2, ROWS, TILE), F32)...  3.55 us
  transfers between devices with their start and end apart: 7, of which 2 were waited for; matrix products, arithmetic and copies ran while one was open for 0% of the time, Pallas kernels for 11%

commit v1 on v0

--- a/solution.py
+++ b/solution.py
@@ -61,7 +61,65 @@
     return 0.5 * jnp.tanh(0.5 * value) + 0.5
 
 
-def pack_kernel(vox, disp, hidden, context, own, right, left, far, down, up):
+def pack_kernel(
+    vox_h,
+    disp_h,
+    hidden_h,
+    context_h,
+    first_h,
+    bias_h,
+    second_h,
+    motion_h,
+    scale_h,
+    mbias_h,
+    pool_h,
+    rows_h,
+    own,
+    right,
+    left,
+    far,
+    down,
+    up,
+    w1,
+    w1t,
+    w2,
+    w2t,
+    mw,
+    pool,
+    rows,
+    scale,
+    mbias,
+    disp,
+    vox,
+    first,
+    bias,
+    motion,
+    sems,
+):
+    pairs = [(vox_h, vox), (disp_h, disp)]
+    for v in range(2):
+        pairs += [
+            (hidden_h.at[v], down.at[v, 0:ROWS]),
+            (hidden_h.at[v], up.at[v, 0:ROWS]),
+            (context_h.at[v, ROWS - 1, :, UNITS : 2 * UNITS], down.at[v, ROWS]),
+            (context_h.at[v, 0, :, UNITS : 2 * UNITS], up.at[v, ROWS]),
+        ]
+    data = len(pairs)
+    pairs += [
+        (first_h, first),
+        (bias_h, bias),
+        (second_h, w2),
+        (motion_h, motion),
+        (scale_h, scale),
+        (mbias_h, mbias),
+        (pool_h, pool),
+        (rows_h, rows),
+    ]
+    copies = [pltpu.make_async_copy(a, b, sems.at[k]) for k, (a, b) in enumerate(pairs)]
+    for copy in copies:
+        copy.start()
+    for copy in copies[:data]:
+        copy.wait()
     col = lax.axis_index("col")
     row_at = lax.broadcasted_iota(jnp.int32, (8, 128), 0)
     parts = []
@@ -75,10 +133,11 @@
             own[2 * v + y] = jnp.concatenate(
                 [block, jnp.zeros((32, 256 - TILE), F32)], axis=1
             ).astype(BF)
-            hid_last = pltpu.roll(hidden[v, y, 144:160, :].astype(F32)[8:16], 2, 0)
-            con_last = pltpu.roll(context[v, y, 144:160, UNITS : 2 * UNITS].astype(F32)[8:16], 3, 0)
-            hid_first = hidden[v, y, 0:16, :].astype(F32)[0:8]
-            con_first = pltpu.roll(context[v, y, 0:16, UNITS : 2 * UNITS].astype(F32)[0:8], 2, 0)
+            con = (up, down)[y]
+            hid_last = pltpu.roll(down[v, y, 144:160, :].astype(F32)[8:16], 2, 0)
+            con_last = pltpu.roll(con[v, ROWS, 144:160, :].astype(F32)[8:16], 3, 0)
+            hid_first = down[v, y, 0:16, :].astype(F32)[0:8]
+            con_first = pltpu.roll(con[v, ROWS, 0:16, :].astype(F32)[0:8], 2, 0)
             depth = disp[v, y : y + 1, :]
             d_last = pltpu.roll(jnp.broadcast_to(depth[:, 32:160], (8, 128)), 8, 1)
             d_first = jnp.broadcast_to(depth[:, 0:128], (8, 128))
@@ -93,10 +152,6 @@
 
             edges_right.append(edge(hid_last, con_last, d_last))
             edges_left.append(edge(hid_first, con_first, d_first))
-            for target, con_row in ((down, ROWS - 1), (up, 0)):
-                target[v, y] = hidden[v, y]
-                if y == con_row:
-                    target[v, ROWS] = context[v, y, :, UNITS : 2 * UNITS]
     blank = jnp.zeros((32, 256 - TILE - NEAR), F32)
     for y in range(ROWS):
         f0, f1 = parts[y], parts[ROWS + y]
@@ -114,16 +169,15 @@
             ],
             axis=1,
         ).astype(BF)
-
-
-def weight_kernel(first, bias, second, motion, w1, w1t, w2t, mw):
+    for copy in copies[data:]:
+        copy.wait()
     w_high, w_low = split(first[...] * 0.5)
     b_high, rest = split(bias[...] * 0.5)
     b_mid, b_low = split(rest)
     stacked = jnp.concatenate([w_high, b_high, w_high, b_mid, w_low, b_low], axis=0)
     w1[...] = stacked.astype(BF)
     w1t[...] = jnp.concatenate([stacked, jnp.zeros((80, 256), F32)], axis=0).T.astype(BF)
-    w2t[...] = second[...].astype(F32).T.astype(BF)
+    w2t[...] = w2[...].astype(F32).T.astype(BF)
     m_high, m_low = split(motion[...])
     gap = jnp.zeros((GROUP - LEVELS * TAPS, 128), F32)
     mw[...] = jnp.concatenate(
@@ -332,9 +386,10 @@
             )[0:1]
 
 
-def call(kernel, outs, scratch=(), **cost):
+def call(kernel, outs, in_specs=None, scratch=(), **cost):
     return pl.pallas_call(
         kernel,
+        **({} if in_specs is None else {"in_specs": in_specs}),
         out_shape=[jax.ShapeDtypeStruct(shape, dtype) for shape, dtype in outs],
         scratch_shapes=list(scratch),
         compiler_params=pltpu.CompilerParams(vmem_limit_bytes=VMEM_LIMIT),
@@ -366,51 +421,66 @@
     upward = [(i + 1, i) for i in range(rows - 1)]
     pool, lane_rows = tables()
 
-    own, right, left, far, down, up = call(
+    (own, right, left, far, down, up, w1, w1t, w2, w2t, mw, pool, lane_rows, scale, bias, disp) = call(
         pack_kernel,
         [
             ((4, 32, 256), BF),
             ((80, 256), BF),
             ((80, 256), BF),
             ((64, 128), BF),
-            ((2, 3, TILE, UNITS), BF),
-            ((2, 3, TILE, UNITS), BF),
+            ((2, ROWS + 1, TILE, UNITS), BF),
+            ((2, ROWS + 1, TILE, UNITS), BF),
+            ((48, 256), BF),
+            ((256, 128), BF),
+            ((256, 256), BF),
+            ((256, 256), BF),
+            ((128, 128), BF),
+            ((256, 128), BF),
+            ((8, 128), F32),
+            ((1, 128), F32),
+            ((1, 128), F32),
+            ((2, ROWS, TILE), F32),
+        ],
+        in_specs=[pl.BlockSpec(memory_space=pltpu.MemorySpace.HBM)] * 12,
+        scratch=[
+            pltpu.VMEM((2, BINS, ROWS, TILE), F32),
+            pltpu.VMEM((BINS, 256), F32),
+            pltpu.VMEM((1, 256), F32),
+            pltpu.VMEM((LEVELS * TAPS, 128), F32),
+            pltpu.SemaphoreType.DMA((18,)),
         ],
         flops=10**6,
         bytes_accessed=2 * 10**6,
-    )(voxels, disparity, hidden, context)
+    )(
+        *(
+            pltpu.with_memory_space_constraint(x, pltpu.MemorySpace.HBM)
+            for x in (
+                voxels,
+                disparity,
+                hidden,
+                context,
+                embed_first,
+                embed_bias.reshape(1, -1),
+                embed_second,
+                motion_weight,
+                motion_scale.reshape(1, -1),
+                motion_bias.reshape(1, -1),
+                jnp.asarray(pool),
+                jnp.asarray(lane_rows),
+            )
+        )
+    )
     from_left = lax.ppermute(right, "col", onward)
     from_right = lax.ppermute(left, "col", back)
     from_far = lax.ppermute(far, "col", across)
     hc_up = lax.ppermute(down, "row", downward)
     hc_down = lax.ppermute(up, "row", upward)
-    w1, w1t, w2t, mw = call(
-        weight_kernel,
-        [((48, 256), BF), ((256, 128), BF), ((256, 256), BF), ((128, 128), BF)],
-        flops=10**6,
-        bytes_accessed=10**6,
-    )(embed_first, embed_bias.reshape(1, -1), embed_second, motion_weight)
     (motion,) = call(
         motion_kernel,
         [((2, ROWS, EXT, UNITS), BF)],
         flops=10**9,
         bytes_accessed=10**6,
-    )(
-        own,
-        from_left,
-        from_right,
-        from_far,
-        disparity,
-        w1,
-        w1t,
-        embed_second,
-        w2t,
-        mw,
-        motion_scale.reshape(1, -1),
-        motion_bias.reshape(1, -1),
-        jnp.asarray(pool),
-        jnp.asarray(lane_rows),
-    )
+    )(own, from_left, from_right, from_far, disp, w1, w1t, w2, w2t, mw, scale, bias, pool, lane_rows)
     motion_up = lax.ppermute(motion, "row", downward)
     motion_down = lax.ppermute(motion, "row", upward)
     new_hidden, increment = call(

time: 47.7 us -> 35.1 us (0.74)
  local copies, waits for them, and re-layouts: 10.9 us -> 0.03 us
  waiting for transfers between devices: 5.07 us -> 2.61 us
  Pallas kernels: 8.84 us -> 10.1 us
    unnamed x38 -> x10, local copies, waits for them, and re-layouts: 10.9 us -> 0.03 us
    ppermute x1, waiting for transfers between devices: 4.4 us -> 1.41 us  [local(): motion_down = lax.ppermute(motion, 'row', upward)]
    pallas_call x1, Pallas kernels: 0.27 us -> 1.65 us  [local(): call(pack_kernel, [((4, 32, 256), BF), ((80, 256), BF), ((80, 256), BF),...]
    ppermute x1, waiting for transfers between devices: 0.66 us -> 1.18 us  [local(): motion_up = lax.ppermute(motion, 'row', downward)]
  transfers between devices with their start and end apart: 7 -> 7, of which waited for: 2 -> 2; matrix products, arithmetic and copies ran while one was open for 0% -> 0% of each run, Pallas kernels for 11% -> 14%
where the time goes in v1:
time: 35.1 us; the launch traced here: 34.9 us
  starting transfers between devices  21.4 us (61%)
  Pallas kernels  10.1 us (29%)
  waiting for transfers between devices  2.61 us (7%)
  between operations  0.8 us (2%)
    ppermute x1, starting transfers between devices, local(): hc_up = lax.ppermute(down, 'row', downward)  4.93 us
    pallas_call x1, Pallas kernels, local(): call(motion_kernel, [((2, ROWS, EXT, UNITS), BF)], flops=10 ** 9, bytes_a...  4.88 us
    ppermute x1, starting transfers between devices, local(): from_left = lax.ppermute(right, 'col', onward)  3.95 us
    ppermute x1, starting transfers between devices, local(): from_far = lax.ppermute(far, 'col', across)  3.7 us
    ppermute x1, starting transfers between devices, local(): motion_up = lax.ppermute(motion, 'row', downward)  3.65 us
    pallas_call x1, Pallas kernels, local(): call(update_kernel, [((2, ROWS, TILE, UNITS), BF), ((2, ROWS, TILE), F32)...  3.54 us
    ppermute x1, starting transfers between devices, local(): hc_down = lax.ppermute(up, 'row', upward)  1.92 us
    ppermute x1, starting transfers between devices, local(): motion_down = lax.ppermute(motion, 'row', upward)  1.92 us
  transfers between devices with their start and end apart: 7, of which 2 were waited for; matrix products, arithmetic and copies ran while one was open for 0% of the time, Pallas kernels for 14%

profile of v1, /device:TPU:1, one launch (start us, length us, event | category | flops | bytes accessed | tf_op | source)
XLA Modules:
  0.0 34.9 jit_solution(17030139034166219582)
XLA Ops:
  0.6 1.7 %shard_map.158 = (bf16[4,32,256]{2,1,0:T(8,128)(2,1)S(1)}, bf16[80,256]{1,0:T(8,128)(2,1)S(1)}, bf16[80,256]{1,0:T(8,128)(2,1)S(1)}, bf16[64,128]{1,0:T(8,128)(2...) custom-call(f32[2,15,2,160]{3,2,1,0:T(2,128)} %vox_h.1, ...), custom_call_target="tpu_custom_call" | custom-call | flops 1000000 | bytes 2000000 | tf_op jit(solution)/shard_map/pallas_call | solution.py:424
  2.3 3.9 %collective-permute-start.2 = (bf16[80,256]{1,0:T(8,128)(2,1)S(1)}, bf16[80,256]{1,0:T(8,128)(2,1)S(1)}, u32[]{:S(2)}, u32[]{:S(2)}) collective-permute-start(bf16[80,256]{1,0:T(8,128)(2,1)S(1)} %get-tuple-element.21), channel_id=1, source_target_pairs={{0,1},{1,2},{2,3},{4,5},{5,6},{6,7},{8,9},{9,10},{10,11},{12,13},{... | collective-permute-start | bytes 122888 | tf_op jit(solution)/shard_map/ppermute | solution.py:473
  6.2 1.3 %collective-permute-start.3 = (bf16[80,256]{1,0:T(8,128)(2,1)S(1)}, bf16[80,256]{1,0:T(8,128)(2,1)S(1)}, u32[]{:S(2)}, u32[]{:S(2)}) collective-permute-start(bf16[80,256]{1,0:T(8,128)(2,1)S(1)} %get-tuple-element.22), channel_id=1, source_target_pairs={{1,0},{2,1},{3,2},{5,4},{6,5},{7,6},{9,8},{10,9},{11,10},{13,12},{... | collective-permute-start | bytes 122888 | tf_op jit(solution)/shard_map/ppermute | solution.py:474
  7.5 3.7 %collective-permute-start.4 = (bf16[64,128]{1,0:T(8,128)(2,1)S(1)}, bf16[64,128]{1,0:T(8,128)(2,1)S(1)}, u32[]{:S(2)}, u32[]{:S(2)}) collective-permute-start(bf16[64,128]{1,0:T(8,128)(2,1)S(1)} %get-tuple-element.23), channel_id=1, source_target_pairs={{0,2},{1,3},{2,0},{3,1},{4,6},{5,7},{6,4},{7,5},{8,10},{9,11},{10,... | collective-permute-start | bytes 49160 | tf_op jit(solution)/shard_map/ppermute | solution.py:475
  11.2 4.9 %collective-permute-start = (bf16[2,3,160,128]{3,2,1,0:T(8,128)(2,1)S(1)}, bf16[2,3,160,128]{3,2,1,0:T(8,128)(2,1)S(1)}, u32[]{:S(2)}, u32[]{:S(2)}) collective-permute-start(bf16[2,3,160,128]{3,2,1,0:T(8,128)(2,1)S(1)} %get-tuple-element.18), channel_id=1, source_target_pairs={{0,4},{4,8},{8,12},{12,16},{16,20},{20,24},{24,28},{1,5},{5,9},{9,... | collective-permute-start | bytes 737288 | tf_op jit(solution)/shard_map/ppermute | solution.py:476
  16.2 1.9 %collective-permute-start.1 = (bf16[2,3,160,128]{3,2,1,0:T(8,128)(2,1)S(1)}, bf16[2,3,160,128]{3,2,1,0:T(8,128)(2,1)S(1)}, u32[]{:S(2)}, u32[]{:S(2)}) collective-permute-start(bf16[2,3,160,128]{3,2,1,0:T(8,128)(2,1)S(1)} %get-tuple-element.19), channel_id=1, source_target_pairs={{4,0},{8,4},{12,8},{16,12},{20,16},{24,20},{28,24},{5,1},{9,5},{13... | collective-permute-start | bytes 737288 | tf_op jit(solution)/shard_map/ppermute | solution.py:477
  18.1 0.0 collective-permute-done.4.from_far
  18.1 0.0 collective-permute-done.2.from_left
  18.1 0.0 collective-permute-done.3.from_right
  18.2 0.0 copy-start
  18.2 0.0 copy-start.1
  18.2 0.0 copy-start.2
  18.2 0.0 copy-start.3
  18.2 0.0 copy-start.4
  18.2 4.9 %shard_map.159.mot = bf16[2,2,192,128]{3,2,1,0:T(8,128)(2,1)S(1)} custom-call(bf16[4,32,256]{2,1,0:T(8,128)(2,1)S(1)} %get-tuple-element.20.own, bf16[80,256]{1,0:T(8,128)(2,1)S(1)} %collective-permute-done.2.from_left, bf16[80,256]{1,0:T(8,128)(2,1)S(1)} %collective-permute-done.3.from_right, bf16[64,128]{1,0:T(8,128)(2,1)S(1)} %collective-permute-done.4.from_far, ...), custom_call_target="tpu_custom_call" | custom-call | flops 1000000000 | bytes 1000000 | tf_op jit(solution)/shard_map/pallas_call | solution.py:478
  23.1 1.9 %collective-permute-start.6 = (bf16[2,2,192,128]{3,2,1,0:T(8,128)(2,1)S(1)}, bf16[2,2,192,128]{3,2,1,0:T(8,128)(2,1)S(1)}, u32[]{:S(2)}, u32[]{:S(2)}) collective-permute-start(bf16[2,2,192,128]{3,2,1,0:T(8,128)(2,1)S(1)} %shard_map.159.mot), channel_id=1, source_target_pairs={{4,0},{8,4},{12,8},{16,12},{20,16},{24,20},{28,24},{5,1},{9,5},{13... | collective-permute-start | bytes 589832 | tf_op jit(solution)/shard_map/ppermute | solution.py:485
  25.0 3.6 %collective-permute-start.5 = (bf16[2,2,192,128]{3,2,1,0:T(8,128)(2,1)S(1)}, bf16[2,2,192,128]{3,2,1,0:T(8,128)(2,1)S(1)}, u32[]{:S(2)}, u32[]{:S(2)}) collective-permute-start(bf16[2,2,192,128]{3,2,1,0:T(8,128)(2,1)S(1)} %shard_map.159.mot), channel_id=1, source_target_pairs={{0,4},{4,8},{8,12},{12,16},{16,20},{20,24},{24,28},{1,5},{5,9},{9,... | collective-permute-start | bytes 589832 | tf_op jit(solution)/shard_map/ppermute | solution.py:484
  28.7 1.4 %collective-permute-done.6.mot_down = bf16[2,2,192,128]{3,2,1,0:T(8,128)(2,1)S(1)} collective-permute-done((bf16[2,2,192,128]{3,2,1,0:T(8,128)(2,1)S(1)}, bf16[2,2,192,128]{3,2,1,0:T(8,128)(2,1)S(1)}, u32[]{:S(2)}, u32[]{:S(2)}) %collective-permute-start.6) | collective-permute-done | bytes 196640 | tf_op jit(solution)/shard_map/ppermute | solution.py:485
  30.1 1.2 %collective-permute-done.5.mot_up = bf16[2,2,192,128]{3,2,1,0:T(8,128)(2,1)S(1)} collective-permute-done((bf16[2,2,192,128]{3,2,1,0:T(8,128)(2,1)S(1)}, bf16[2,2,192,128]{3,2,1,0:T(8,128)(2,1)S(1)}, u32[]{:S(2)}, u32[]{:S(2)}) %collective-permute-start.5) | collective-permute-done | bytes 196640 | tf_op jit(solution)/shard_map/ppermute | solution.py:484
  31.3 0.0 collective-permute-done.hc_up
  31.3 0.0 collective-permute-done.1.hc_down
  31.3 0.0 copy-done
  31.3 0.0 copy-done.1
  31.3 3.5 %shard_map.160 = (bf16[2,2,160,128]{3,2,1,0:T(8,128)(2,1)}, f32[2,2,160]{2,1,0:T(2,128)}) custom-call(bf16[2,2,160,128]{3,2,1,0:T(8,128)(2,1)S(1)} %copy-done.1, bf16[2,2,160,384]{3,2,1,0:T(8,128)(2,1)S(1)} %copy-done, bf16[2,3,160,128]{3,2,1,0:T(8,128)(2,1)S(1)} %collective-permute-done.hc_up, bf16[2,3,160,128]{3,2,1,0:T(8,128)(2,1)S(1)} %collective-permute-done.1.hc_down, ...), custom_call_target="tpu_custom_call" | custom-call | flops 2000000000 | bytes 4000000 | tf_op jit(solution)/shard_map/pallas_call | solution.py:486
  (3 shorter events, 0.0 us)
Async XLA Ops:
  2.3 15.8 %collective-permute-start.2 = (bf16[80,256]{1,0:T(8,128)(2,1)S(1)}, bf16[80,256]{1,0:T(8,128)(2,1)S(1)}, u32[]{:S(2)}, u32[]{:S(2)}) collective-permute-start(bf16[80,256]{1,0:T(8,128)(2,1)S(1)} %get-tuple-element.21), channel_id=1, source_target_pairs={{0,1},{1,2},{2,3},{4,5},{5,6},{6,7},{8,9},{9,10},{10,11},{12,13},{... | collective-permute-start | bytes 122888 | tf_op jit(solution)/shard_map/ppermute | solution.py:473
  6.2 11.9 %collective-permute-start.3 = (bf16[80,256]{1,0:T(8,128)(2,1)S(1)}, bf16[80,256]{1,0:T(8,128)(2,1)S(1)}, u32[]{:S(2)}, u32[]{:S(2)}) collective-permute-start(bf16[80,256]{1,0:T(8,128)(2,1)S(1)} %get-tuple-element.22), channel_id=1, source_target_pairs={{1,0},{2,1},{3,2},{5,4},{6,5},{7,6},{9,8},{10,9},{11,10},{13,12},{... | collective-permute-start | bytes 122888 | tf_op jit(solution)/shard_map/ppermute | solution.py:474
  7.5 10.6 %collective-permute-start.4 = (bf16[64,128]{1,0:T(8,128)(2,1)S(1)}, bf16[64,128]{1,0:T(8,128)(2,1)S(1)}, u32[]{:S(2)}, u32[]{:S(2)}) collective-permute-start(bf16[64,128]{1,0:T(8,128)(2,1)S(1)} %get-tuple-element.23), channel_id=1, source_target_pairs={{0,2},{1,3},{2,0},{3,1},{4,6},{5,7},{6,4},{7,5},{8,10},{9,11},{10,... | collective-permute-start | bytes 49160 | tf_op jit(solution)/shard_map/ppermute | solution.py:475
  11.2 20.0 %collective-permute-start = (bf16[2,3,160,128]{3,2,1,0:T(8,128)(2,1)S(1)}, bf16[2,3,160,128]{3,2,1,0:T(8,128)(2,1)S(1)}, u32[]{:S(2)}, u32[]{:S(2)}) collective-permute-start(bf16[2,3,160,128]{3,2,1,0:T(8,128)(2,1)S(1)} %get-tuple-element.18), channel_id=1, source_target_pairs={{0,4},{4,8},{8,12},{12,16},{16,20},{20,24},{24,28},{1,5},{5,9},{9,... | collective-permute-start | bytes 737288 | tf_op jit(solution)/shard_map/ppermute | solution.py:476
  16.2 15.1 %collective-permute-start.1 = (bf16[2,3,160,128]{3,2,1,0:T(8,128)(2,1)S(1)}, bf16[2,3,160,128]{3,2,1,0:T(8,128)(2,1)S(1)}, u32[]{:S(2)}, u32[]{:S(2)}) collective-permute-start(bf16[2,3,160,128]{3,2,1,0:T(8,128)(2,1)S(1)} %get-tuple-element.19), channel_id=1, source_target_pairs={{4,0},{8,4},{12,8},{16,12},{20,16},{24,20},{28,24},{5,1},{9,5},{13... | collective-permute-start | bytes 737288 | tf_op jit(solution)/shard_map/ppermute | solution.py:477
  18.2 13.1 %copy-start = (bf16[2,2,160,384]{3,2,1,0:T(8,128)(2,1)S(1)}, bf16[2,2,160,384]{3,2,1,0:T(8,128)(2,1)}, u32[]{:S(2)}) copy-start(bf16[2,2,160,384]{3,2,1,0:T(8,128)(2,1)} %context.1) | copy-start | bytes 1474564
  18.2 13.1 %copy-start.1 = (bf16[2,2,160,128]{3,2,1,0:T(8,128)(2,1)S(1)}, bf16[2,2,160,128]{3,2,1,0:T(8,128)(2,1)}, u32[]{:S(2)}) copy-start(bf16[2,2,160,128]{3,2,1,0:T(8,128)(2,1)} %hidden.1) | copy-start | bytes 491524
  18.2 13.1 %copy-start.2 = (bf16[3,3,256,256]{3,2,1,0:T(8,128)(2,1)S(1)}, bf16[3,3,256,256]{3,2,1,0:T(8,128)(2,1)}, u32[]{:S(2)}) copy-start(bf16[3,3,256,256]{3,2,1,0:T(8,128)(2,1)} %gate_k.1) | copy-start | bytes 3538948
  18.2 13.1 %copy-start.3 = (bf16[3,3,256,128]{3,2,1,0:T(8,128)(2,1)S(1)}, bf16[3,3,256,128]{3,2,1,0:T(8,128)(2,1)}, u32[]{:S(2)}) copy-start(bf16[3,3,256,128]{3,2,1,0:T(8,128)(2,1)} %cand_k.1) | copy-start | bytes 1769476
  18.2 13.1 %copy-start.4 = (bf16[128]{0:T(256)(128)(2,1)S(1)}, bf16[128]{0:T(256)(128)(2,1)}, u32[]{:S(2)}) copy-start(bf16[128]{0:T(256)(128)(2,1)} %param.27) | copy-start | bytes 772
  23.1 7.0 %collective-permute-start.6 = (bf16[2,2,192,128]{3,2,1,0:T(8,128)(2,1)S(1)}, bf16[2,2,192,128]{3,2,1,0:T(8,128)(2,1)S(1)}, u32[]{:S(2)}, u32[]{:S(2)}) collective-permute-start(bf16[2,2,192,128]{3,2,1,0:T(8,128)(2,1)S(1)} %shard_map.159.mot), channel_id=1, source_target_pairs={{4,0},{8,4},{12,8},{16,12},{20,16},{24,20},{28,24},{5,1},{9,5},{13... | collective-permute-start | bytes 589832 | tf_op jit(solution)/shard_map/ppermute | solution.py:485
  25.0 6.2 %collective-permute-start.5 = (bf16[2,2,192,128]{3,2,1,0:T(8,128)(2,1)S(1)}, bf16[2,2,192,128]{3,2,1,0:T(8,128)(2,1)S(1)}, u32[]{:S(2)}, u32[]{:S(2)}) collective-permute-start(bf16[2,2,192,128]{3,2,1,0:T(8,128)(2,1)S(1)} %shard_map.159.mot), channel_id=1, source_target_pairs={{0,4},{4,8},{8,12},{12,16},{16,20},{20,24},{24,28},{1,5},{5,9},{9,... | collective-permute-start | bytes 589832 | tf_op jit(solution)/shard_map/ppermute | solution.py:484

commit v2 on v1

v2 whole, which is shorter than its diff:
```python
import functools

import jax
import jax.numpy as jnp
import numpy as np
from jax import lax
from jax.experimental import pallas as pl
from jax.experimental.pallas import tpu as pltpu
from jax.sharding import PartitionSpec as P

BF = jnp.bfloat16
F32 = jnp.float32

ROWS = 2
TILE = 160
IMAGE = 640
PAD = 16
EXT = TILE + 2 * PAD
BINS = 15
UNITS = 128
NEAR = 48
FAR = 72
WINDOW = 512
LAST = FAR + 2 * TILE + NEAR - 1
TAPS = 9
LEVELS = 4
GROUP = 40
STARTS = (0, 17, 30, 41)
VMEM_LIMIT = 48 * 1024 * 1024


def tables():
    pool = np.zeros((128, 128), np.float32)
    firsts = (28, 12, 4, 0)
    counts = (17, 13, 11, 10)
    for level in range(LEVELS):
        width = 2**level
        for k in range(counts[level]):
            entry = firsts[level] + k
            pool[entry * width : (entry + 1) * width, STARTS[level] + k] = 1.0 / (16 * width)
    lane = np.arange(128)
    member = lane % GROUP
    used = (member < LEVELS * TAPS) & (lane < 3 * GROUP)
    level = np.where(used, member // TAPS, 0)
    first = np.where(used, np.take(np.array(STARTS), level) + member % TAPS, 0)
    scale = np.where(used, 0.5**level, 0.0)
    low = ((lane >= GROUP) & (lane < 2 * GROUP)).astype(np.float32)
    rows = np.zeros((8, 128), np.float32)
    rows[0], rows[1], rows[2] = first, scale, low
    return np.concatenate([pool, pool]).astype(jnp.bfloat16), rows


def split(value):
    high = value.astype(BF).astype(F32)
    return high, value - high


def silu_of_half(half):
    return half + half * jnp.tanh(half)


def sigmoid(value):
    return 0.5 * jnp.tanh(0.5 * value) + 0.5


def pack_kernel(
    vox_h,
    disp_h,
    hidden_h,
    context_h,
    first_h,
    bias_h,
    second_h,
    motion_h,
    scale_h,
    mbias_h,
    pool_h,
    rows_h,
    own,
    odd_out,
    even_out,
    far,
    hid,
    con,
    w1,
    w1t,
    w2,
    w2t,
    mw,
    pool,
    rows,
    scale,
    mbias,
    disp,
    vox,
    first,
    bias,
    motion,
    sems,
):
    pairs = [
        (vox_h, vox),
        (disp_h, disp),
        (hidden_h, hid),
        (context_h.at[:, :, :, UNITS : 2 * UNITS], con),
    ]
    data = len(pairs)
    pairs += [
        (first_h, first),
        (bias_h, bias),
        (second_h, w2),
        (motion_h, motion),
        (scale_h, scale),
        (mbias_h, mbias),
        (pool_h, pool),
        (rows_h, rows),
    ]
    copies = [pltpu.make_async_copy(a, b, sems.at[k]) for k, (a, b) in enumerate(pairs)]
    for copy in copies:
        copy.start()
    for copy in copies[:data]:
        copy.wait()
    col = lax.axis_index("col")
    is_even = col % 2 == 0
    row_at = lax.broadcasted_iota(jnp.int32, (8, 128), 0)
    parts = []
    edges_right, edges_left = [], []
    for v in range(2):
        for y in range(ROWS):
            high, low = split(vox[v, :, y, :])
            ones = jnp.ones((1, TILE), F32)
            block = jnp.concatenate([high, ones, low, ones], axis=0)
            parts.append(block)
            own[2 * v + y] = jnp.concatenate(
                [block, jnp.zeros((32, 256 - TILE), F32)], axis=1
            ).astype(BF)
            hid_last = pltpu.roll(hid[v, y, 144:160, :].astype(F32)[8:16], 2, 0)
            con_last = pltpu.roll(con[v, y, 144:160, :].astype(F32)[8:16], 3, 0)
            hid_first = hid[v, y, 0:16, :].astype(F32)[0:8]
            con_first = pltpu.roll(con[v, y, 0:16, :].astype(F32)[0:8], 2, 0)
            depth = disp[v, y : y + 1, :]
            d_last = pltpu.roll(jnp.broadcast_to(depth[:, 32:160], (8, 128)), 8, 1)
            d_first = jnp.broadcast_to(depth[:, 0:128], (8, 128))

            def edge(hid, con, dis):
                d_high, rest = split(dis)
                d_mid, d_low = split(rest)
                out = jnp.where(row_at < 2, hid, con)
                out = jnp.where(row_at == 3, d_high, out)
                out = jnp.where(row_at == 4, d_mid, out)
                return jnp.where(row_at >= 5, d_low, out)

            edges_right.append(edge(hid_last, con_last, d_last))
            edges_left.append(edge(hid_first, con_first, d_first))

    def emit(at, to_right, to_left):
        odd_out[at, :] = jnp.where(is_even, to_right, to_left).astype(BF)
        even_out[at, :] = jnp.where(is_even, to_left, to_right).astype(BF)

    blank = jnp.zeros((32, 256 - TILE - NEAR), F32)
    for y in range(ROWS):
        f0, f1 = parts[y], parts[ROWS + y]
        rows_at = pl.ds(32 * y, 32)
        emit(
            rows_at,
            jnp.concatenate([f1, f0[:, TILE - NEAR :], blank], axis=1),
            jnp.concatenate([f0, f1[:, :NEAR], blank], axis=1),
        )
        tail = jnp.concatenate([f1[:, TILE - FAR :], jnp.zeros((32, 128 - FAR), F32)], axis=1)
        far[rows_at, :] = jnp.where(col < 2, tail, f0[:, :128]).astype(BF)

    def gathered(edges):
        return jnp.concatenate(
            [
                jnp.concatenate([edges[0], edges[1]], axis=0),
                jnp.concatenate([edges[2], edges[3]], axis=0),
            ],
            axis=1,
        )

    emit(pl.ds(64, 16), gathered(edges_right), gathered(edges_left))
    for copy in copies[data:]:
        copy.wait()
    w_high, w_low = split(first[...] * 0.5)
    b_high, rest = split(bias[...] * 0.5)
    b_mid, b_low = split(rest)
    stacked = jnp.concatenate([w_high, b_high, w_high, b_mid, w_low, b_low], axis=0)
    w1[...] = stacked.astype(BF)
    w1t[...] = jnp.concatenate([stacked, jnp.zeros((80, 256), F32)], axis=0).T.astype(BF)
    w2t[...] = w2[...].astype(F32).T.astype(BF)
    m_high, m_low = split(motion[...])
    gap = jnp.zeros((GROUP - LEVELS * TAPS, 128), F32)
    mw[...] = jnp.concatenate(
        [m_high, gap, m_high, gap, m_low, gap, jnp.zeros((8, 128), F32)], axis=0
    ).astype(BF)


def motion_kernel(
    v,
    own,
    odd_in,
    even_in,
    far_in,
    hid,
    con,
    disp,
    w1,
    w1t,
    w2,
    w2t,
    mw,
    scale,
    bias,
    pool,
    rows,
    chip_out,
    link_out,
):
    col = lax.axis_index("col")
    is_even = col % 2 == 0
    row_even = lax.axis_index("row") % 2 == 0

    def received(at, lanes):
        first, second = odd_in[at, lanes].astype(F32), even_in[at, lanes].astype(F32)
        left = jnp.where(col > 0, jnp.where(is_even, second, first), 0.0)
        right = jnp.where(col < 3, jnp.where(is_even, first, second), 0.0)
        return left, right

    lanes = pl.ds(128 * v, 128)
    edge_left, edge_right = received(pl.ds(64, 16), lanes)
    edges = [
        (edge_left[8 * y : 8 * y + 8], edge_right[8 * y : 8 * y + 8]) for y in range(ROWS)
    ]
    depth_rows = []
    for y in range(ROWS):
        e_l, e_r = edges[y]
        d_l = e_l[3:4] + e_l[4:5] + e_l[5:6]
        d_r = e_r[3:4] + e_r[4:5] + e_r[5:6]
        depth_rows.append(
            jnp.concatenate(
                [
                    jnp.zeros((1, 8), F32),
                    d_l[:, :8],
                    disp[v, y : y + 1, :],
                    d_r[:, :8],
                    jnp.zeros((1, 72), F32),
                ],
                axis=1,
            )
        )
    depth_rows.append(jnp.zeros((8 - ROWS, 256), F32))
    depths = jnp.concatenate(depth_rows, axis=0).T

    first = rows[0:1, :].astype(jnp.int32)
    level_scale = rows[1:2, :]
    is_low = rows[2:3, :] > 0.5
    lane = lax.broadcasted_iota(jnp.int32, (EXT, 128), 1)
    pixel = lax.broadcasted_iota(jnp.int32, (EXT, 1), 0)
    column = pixel + (col * TILE - PAD)
    inside = (column >= 0) & (column < IMAGE)
    pixel = pixel.astype(F32)
    depth_scale = scale[...] * (1.0 / 192.0)

    def lookups(scores, depth):
        spot = (pixel - PAD if v == 0 else (EXT - 1 - PAD) - pixel) - depth
        eighth = jnp.floor(spot * 0.125)
        rest = spot - 8.0 * eighth
        start = (8.0 * eighth).astype(jnp.int32) + (FAR + TILE - 32)
        index = start + lane if v == 0 else (LAST - start) - lane
        block, place = index >> 7, index & 127
        near = jnp.zeros((EXT, 128), F32)
        for k in range(WINDOW // 128):
            taken = jnp.take_along_axis(
                scores[:, 128 * k : 128 * k + 128], place, axis=1, mode="promise_in_bounds"
            )
            near = jnp.where(block == k, taken, near)
        high, low = split(near)
        pooled = jnp.dot(
            jnp.concatenate([high.astype(BF), low.astype(BF)], axis=1),
            pool[...],
            preferred_element_type=F32,
        )
        at = rest * level_scale
        floor = jnp.floor(at)
        weight = at - floor
        index = floor.astype(jnp.int32) + first
        lower = jnp.take_along_axis(pooled, index, axis=1, mode="promise_in_bounds")
        upper = jnp.take_along_axis(pooled, index + 1, axis=1, mode="promise_in_bounds")
        return lower + weight * (upper - lower)

    for y in range(ROWS):
        e_l, e_r = edges[y]
        pad8 = jnp.zeros((8, 128), F32)
        for k, value, to_last, to_first in ((y, hid, 6, 0), (2, con, 5, 6)):
            before = jnp.concatenate([pad8, pltpu.roll(e_l, to_last, 0)], axis=0).astype(BF)
            after = pltpu.roll(e_r, to_first, 0) if to_first else e_r
            after = jnp.concatenate([after, pad8], axis=0).astype(BF)
            if k == 2:

                @pl.when(row_even == (y == 1))
                def _(before=before, after=after):
                    chip_out[2, 0:PAD] = before
                    chip_out[2, PAD : PAD + TILE] = con[v, y]
                    chip_out[2, PAD + TILE :] = after

                @pl.when(row_even == (y == 0))
                def _(before=before, after=after):
                    link_out[2, 0:PAD] = before
                    link_out[2, PAD : PAD + TILE] = con[v, y]
                    link_out[2, PAD + TILE :] = after

            else:
                for target in (chip_out, link_out):
                    target[k, 0:PAD] = before
                    target[k, PAD : PAD + TILE] = value[v, y]
                    target[k, PAD + TILE :] = after
    for y in range(ROWS):
        left, right = received(pl.ds(32 * y, 32), slice(None))
        far = far_in[32 * y : 32 * y + 32, :].astype(F32)[:, :FAR]
        mine, other = own[ROWS * v + y].astype(F32), own[ROWS * (1 - v) + y].astype(F32)[:, :TILE]
        blank = jnp.zeros((32, WINDOW - 1 - LAST), F32)
        if v == 0:
            far = jnp.where(col >= 2, far, 0.0)
            pieces = [far, left[:, :TILE], other, right[:, TILE : TILE + NEAR], blank]
            ends = (left[:, TILE + NEAR - PAD : TILE + NEAR], right[:, :PAD])
        else:
            far = jnp.where(col < 2, far, 0.0)
            pieces = [left[:, TILE : TILE + NEAR], other, right[:, :TILE], far, blank]
            ends = (left[:, TILE - PAD : TILE], right[:, TILE : TILE + PAD])
        window = jnp.concatenate(pieces, axis=1)
        query = jnp.concatenate([ends[0], mine[:, :TILE], ends[1]], axis=1)
        stacked = jnp.concatenate([query, query[:16]], axis=0)
        stacked = jnp.concatenate(
            [
                jnp.concatenate([stacked, jnp.zeros((48, 256 - EXT), F32)], axis=1),
                jnp.zeros((80, 256), F32),
            ],
            axis=0,
        ).T.astype(BF)
        layer = silu_of_half(
            jnp.dot(stacked[:EXT, :48], w1[...], preferred_element_type=F32)
        ).astype(BF)
        features = jnp.dot(layer, w2[...], preferred_element_type=F32).astype(BF)
        stacked = jnp.concatenate([window, window[:16]], axis=0).astype(BF)
        layer = silu_of_half(
            jnp.dot(w1t[:, :48], stacked, preferred_element_type=F32)
        ).astype(BF)
        match = jnp.dot(w2t[...], layer, preferred_element_type=F32).astype(BF)
        scores = jnp.dot(features, match, preferred_element_type=F32)
        depth = depths[:EXT, y : y + 1]
        look = lookups(scores, depth)
        high, low = split(look)
        half = 0.5 * (
            jnp.dot(jnp.where(is_low, low, high).astype(BF), mw[...], preferred_element_type=F32)
            + depth * depth_scale
            + bias[...]
        )
        value = jnp.where(inside, silu_of_half(half), 0.0).astype(BF)
        chip_out[3 + y] = value
        link_out[3 + y] = value


def update_kernel(
    v,
    hidden,
    context,
    chip_own,
    link_own,
    chip_in,
    link_in,
    gate_k,
    cand_k,
    head,
    *refs,
):
    if v == 1:
        new_before, inc_before, new, inc, halo, reset = refs
        new[0] = new_before[...]
        inc[0] = inc_before[...]
        new, inc = new.at[1], inc.at[1]
    else:
        new, inc, halo, reset = refs
    row = lax.axis_index("row")
    row_even = row % 2 == 0
    last = lax.axis_size("row") - 1
    blank = jnp.zeros((5, EXT, UNITS), BF)

    @pl.when(row_even)
    def _():
        halo[0] = jnp.where(row > 0, link_in[...], blank)
        halo[1] = chip_in[...]

    @pl.when(jnp.logical_not(row_even))
    def _():
        halo[0] = chip_in[...]
        halo[1] = jnp.where(row < last, link_in[...], blank)

    def pick(k, yy):
        if yy < 2:
            return halo[0, k + yy]
        if yy < 4:
            return chip_own[k + yy - 2]
        return halo[1, k + yy - 4]

    def con_of(yy):
        if yy == 1:
            return halo[0, 2]
        if yy == 4:
            return halo[1, 2]
        near, far = chip_own[2].astype(F32), link_own[2].astype(F32)
        return jnp.where(row_even == (yy == 3), near, far)

    def spread(products, width):
        before, at, after = (products[:, width * b : width * b + width] for b in range(3))
        if v == 1:
            before, after = after, before
        return pltpu.roll(before, 1, 0) + at + pltpu.roll(after, EXT - 1, 0)

    gate_all = jnp.concatenate(
        [jnp.concatenate([gate_k[a, b] for a in range(3)], axis=0) for b in range(3)], axis=1
    )
    gate_reset = jnp.concatenate(
        [
            jnp.concatenate([gate_k[a, b, :, UNITS:] for a in range(3)], axis=0)
            for b in range(3)
        ],
        axis=1,
    )
    cand_all = jnp.concatenate(
        [jnp.concatenate([cand_k[a, b] for a in range(3)], axis=0) for b in range(3)], axis=1
    )
    head_rows = jnp.broadcast_to(head[...].astype(F32), (8, UNITS)).astype(BF)
    gates = [None, None]
    for yy in range(1, 5):
        stacked = jnp.concatenate(
            [piece for k in (yy - 1, yy, yy + 1) for piece in (pick(0, k), pick(3, k))], axis=1
        )
        if yy in (2, 3):
            terms = spread(jnp.dot(stacked, gate_all, preferred_element_type=F32), 2 * UNITS)
            gates[yy - 2] = terms[PAD : PAD + TILE, :UNITS]
            terms = terms[:, UNITS:]
        else:
            terms = spread(jnp.dot(stacked, gate_reset, preferred_element_type=F32), UNITS)
        gate = sigmoid(terms + con_of(yy).astype(F32))
        reset[yy - 1] = (gate * pick(0, yy).astype(F32)).astype(BF)
    for y in range(ROWS):
        stacked = jnp.concatenate(
            [piece for k in range(3) for piece in (reset[y + k], pick(3, y + 1 + k))], axis=1
        )
        terms = spread(jnp.dot(stacked, cand_all, preferred_element_type=F32), UNITS)
        candidate = jnp.tanh(terms[PAD : PAD + TILE] + context[v, y, :, 2 * UNITS :].astype(F32))
        update = sigmoid(gates[y] + context[v, y, :, :UNITS].astype(F32))
        old = hidden[v, y].astype(F32)
        fresh = ((1.0 - update) * old + update * candidate).astype(BF)
        new[y] = fresh
        inc[y : y + 1, :] = lax.dot_general(
            head_rows, fresh, (((1,), (1,)), ((), ())), preferred_element_type=F32
        )[0:1]


def call(kernel, outs, in_specs=None, scratch=(), **cost):
    return pl.pallas_call(
        kernel,
        **({} if in_specs is None else {"in_specs": in_specs}),
        out_shape=[jax.ShapeDtypeStruct(shape, dtype) for shape, dtype in outs],
        scratch_shapes=list(scratch),
        compiler_params=pltpu.CompilerParams(vmem_limit_bytes=VMEM_LIMIT),
        cost_estimate=pl.CostEstimate(transcendentals=0, **cost),
    )


def local(
    voxels,
    disparity,
    hidden,
    context,
    embed_first,
    embed_bias,
    embed_second,
    motion_weight,
    motion_scale,
    motion_bias,
    gate_kernel,
    candidate_kernel,
    head_weight,
):
    cols = lax.axis_size("col")
    rows = lax.axis_size("row")
    odd = [(i, i ^ 1) for i in range(cols)]
    even = [(i, (cols - 1) - i) for i in range(cols)]
    across = [(i, (i + 2) % cols) for i in range(cols)]
    chip = [(i, i ^ 1) for i in range(rows)]
    link = [(0, 0), (rows - 1, rows - 1)]
    link += [(i, ((i + 1) ^ 1) - 1) for i in range(1, rows - 1)]
    pool, lane_rows = tables()

    (own, odd_out, even_out, far, hid, con, w1, w1t, w2, w2t, mw, pool, lane_rows, scale, bias, disp) = call(
        pack_kernel,
        [
            ((4, 32, 256), BF),
            ((80, 256), BF),
            ((80, 256), BF),
            ((64, 128), BF),
            ((2, ROWS, TILE, UNITS), BF),
            ((2, ROWS, TILE, UNITS), BF),
            ((48, 256), BF),
            ((256, 128), BF),
            ((256, 256), BF),
            ((256, 256), BF),
            ((128, 128), BF),
            ((256, 128), BF),
            ((8, 128), F32),
            ((1, 128), F32),
            ((1, 128), F32),
            ((2, ROWS, TILE), F32),
        ],
        in_specs=[pl.BlockSpec(memory_space=pltpu.MemorySpace.HBM)] * 12,
        scratch=[
            pltpu.VMEM((2, BINS, ROWS, TILE), F32),
            pltpu.VMEM((BINS, 256), F32),
            pltpu.VMEM((1, 256), F32),
            pltpu.VMEM((LEVELS * TAPS, 128), F32),
            pltpu.SemaphoreType.DMA((12,)),
        ],
        flops=10**6,
        bytes_accessed=2 * 10**6,
    )(
        *(
            pltpu.with_memory_space_constraint(x, pltpu.MemorySpace.HBM)
            for x in (
                voxels,
                disparity,
                hidden,
                context,
                embed_first,
                embed_bias.reshape(1, -1),
                embed_second,
                motion_weight,
                motion_scale.reshape(1, -1),
                motion_bias.reshape(1, -1),
                jnp.asarray(pool),
                jnp.asarray(lane_rows),
            )
        )
    )
    odd_in = lax.ppermute(odd_out, "col", odd)
    even_in = lax.ppermute(even_out, "col", even)
    far_in = lax.ppermute(far, "col", across)
    halos = []
    for v in range(2):
        chip_out, link_out = call(
            functools.partial(motion_kernel, v),
            [((5, EXT, UNITS), BF)] * 2,
            flops=5 * 10**8,
            bytes_accessed=10**6,
        )(own, odd_in, even_in, far_in, hid, con, disp, w1, w1t, w2, w2t, mw, scale, bias, pool, lane_rows)
        link_in = lax.ppermute(link_out, "row", link)
        chip_in = lax.ppermute(chip_out, "row", chip)
        halos.append((chip_out, link_out, chip_in, link_in))
    done = ()
    for v in range(2):
        lead = (2,) * v
        done = call(
            functools.partial(update_kernel, v),
            [(lead + (ROWS, TILE, UNITS), BF), (lead + (ROWS, TILE), F32)],
            scratch=[pltpu.VMEM((2, 5, EXT, UNITS), BF), pltpu.VMEM((4, EXT, UNITS), BF)],
            flops=10**9,
            bytes_accessed=4 * 10**6,
        )(
            hidden,
            context,
            *halos[v],
            gate_kernel,
            candidate_kernel,
            head_weight.reshape(1, -1),
            *done,
        )
    return tuple(done)


def solution(mesh):
    band = ("pair", "row")
    in_specs = (
        P(None, None, band, "col"),
        P(None, band, "col"),
        P(None, band, "col", None),
        P(None, band, "col", None),
    ) + (P(),) * 9
    out_specs = (P(None, band, "col", None), P(None, band, "col"))
    return jax.shard_map(local, mesh=mesh, in_specs=in_specs, out_specs=out_specs, check_vma=False)
```

time: 35.1 us -> 32.3 us (0.920)
  starting transfers between devices: 21.4 us -> 14.6 us
  waiting for transfers between devices: 2.61 us -> 5.68 us
  Pallas kernels: 10.1 us -> 11.1 us
    ppermute x7, starting transfers between devices: 21.4 us -> 14.6 us  [the longest x2 7.49 us: local(): link_in = lax.ppermute(link_out, 'row', link)]
    ppermute x7, waiting for transfers between devices: 2.61 us -> 5.68 us  [the longest x1 3.55 us: local(): far_in = lax.ppermute(far, 'col', across)]
    pallas_call x2 -> x4, Pallas kernels: 8.42 us -> 9.55 us  [the longest x2 5.6 us: local(): call(functools.partial(motion_kernel, v), [((5, EXT, UNITS), BF)] * 2, fl...]
where the time goes in v2:
time: 32.3 us; the launch traced here: 32.1 us
  starting transfers between devices  14.6 us (45%)
  Pallas kernels  11.1 us (34%)
  waiting for transfers between devices  5.68 us (18%)
  between operations  0.78 us (2%)
    ppermute x2, starting transfers between devices, local(): link_in = lax.ppermute(link_out, 'row', link)  7.49 us
    pallas_call x2, Pallas kernels, local(): call(functools.partial(motion_kernel, v), [((5, EXT, UNITS), BF)] * 2, fl...  5.6 us
    pallas_call x2, Pallas kernels, local(): call(functools.partial(update_kernel, v), [(lead + (ROWS, TILE, UNITS), B...  3.95 us
    ppermute x1, waiting for transfers between devices, local(): far_in = lax.ppermute(far, 'col', across)  3.55 us
    ppermute x2, starting transfers between devices, local(): chip_in = lax.ppermute(chip_out, 'row', chip)  2.48 us
    ppermute x1, starting transfers between devices, local(): odd_in = lax.ppermute(odd_out, 'col', odd)  2.13 us
    ppermute x2, waiting for transfers between devices, local(): link_in = lax.ppermute(link_out, 'row', link)  2.12 us
    ppermute x1, starting transfers between devices, local(): even_in = lax.ppermute(even_out, 'col', even)  1.82 us
  transfers between devices with their start and end apart: 7, of which 2 were waited for; matrix products, arithmetic and copies ran while one was open for 0% of the time, Pallas kernels for 14%

profile of v2, /device:TPU:1, one launch (start us, length us, event | category | flops | bytes accessed | tf_op | source)
XLA Modules:
  0.0 32.1 jit_solution(14856258416867388791)
XLA Ops:
  0.6 1.5 %shard_map.158 = (bf16[4,32,256]{2,1,0:T(8,128)(2,1)S(1)}, bf16[80,256]{1,0:T(8,128)(2,1)S(1)}, bf16[80,256]{1,0:T(8,128)(2,1)S(1)}, bf16[64,128]{1,0:T(8,128)(2...) custom-call(f32[2,15,2,160]{3,2,1,0:T(2,128)} %vox_h.1, ...), custom_call_target="tpu_custom_call" | custom-call | flops 1000000 | bytes 2000000 | tf_op jit(solution)/shard_map/pallas_call | solution.py:497
  2.2 2.1 %collective-permute-start = (bf16[80,256]{1,0:T(8,128)(2,1)S(1)}, bf16[80,256]{1,0:T(8,128)(2,1)S(1)}, u32[]{:S(2)}, u32[]{:S(2)}) collective-permute-start(bf16[80,256]{1,0:T(8,128)(2,1)S(1)} %get-tuple-element.25), channel_id=1, source_target_pairs={{0,1},{1,0},{2,3},{3,2},{4,5},{5,4},{6,7},{7,6},{8,9},{9,8},{10,11... | collective-permute-start | bytes 122888 | tf_op jit(solution)/shard_map/ppermute | solution.py:546
  4.3 1.8 %collective-permute-start.1 = (bf16[80,256]{1,0:T(8,128)(2,1)S(1)}, bf16[80,256]{1,0:T(8,128)(2,1)S(1)}, u32[]{:S(2)}, u32[]{:S(2)}) collective-permute-start(bf16[80,256]{1,0:T(8,128)(2,1)S(1)} %get-tuple-element.26), channel_id=1, source_target_pairs={{0,3},{1,2},{2,1},{3,0},{4,7},{5,6},{6,5},{7,4},{8,11},{9,10},{10,... | collective-permute-start | bytes 122888 | tf_op jit(solution)/shard_map/ppermute | solution.py:547
  6.1 0.6 %collective-permute-start.2 = (bf16[64,128]{1,0:T(8,128)(2,1)S(1)}, bf16[64,128]{1,0:T(8,128)(2,1)S(1)}, u32[]{:S(2)}, u32[]{:S(2)}) collective-permute-start(bf16[64,128]{1,0:T(8,128)(2,1)S(1)} %get-tuple-element.27), channel_id=1, source_target_pairs={{0,2},{1,3},{2,0},{3,1},{4,6},{5,7},{6,4},{7,5},{8,10},{9,11},{10,... | collective-permute-start | bytes 49160 | tf_op jit(solution)/shard_map/ppermute | solution.py:548
  6.8 3.5 %collective-permute-done.2.far_in = bf16[64,128]{1,0:T(8,128)(2,1)S(1)} collective-permute-done((bf16[64,128]{1,0:T(8,128)(2,1)S(1)}, bf16[64,128]{1,0:T(8,128)(2,1)S(1)}, u32[]{:S(2)}, u32[]{:S(2)}) %collective-permute-start.2) | collective-permute-done | bytes 16416 | tf_op jit(solution)/shard_map/ppermute | solution.py:548
  10.3 0.0 collective-permute-done.odd_in
  10.3 0.0 collective-permute-done.1.even_in
  10.3 2.8 %shard_map.160 = (bf16[5,192,128]{2,1,0:T(8,128)(2,1)S(1)}, bf16[5,192,128]{2,1,0:T(8,128)(2,1)S(1)}) custom-call(bf16[4,32,256]{2,1,0:T(8,128)(2,1)S(1)} %get-tuple-element.24.own, bf16[80,256]{1,0:T(8,128)(2,1)S(1)} %collective-permute-done.odd_in, bf16[80,256]{1,0:T(8,128)(2,1)S(1)} %collective-permute-done.1.even_in, ...), custom_call_target="tpu_custom_call" | custom-call | flops 500000000 | bytes 1000000 | tf_op jit(solution)/shard_map/pallas_call | solution.py:551
  13.1 0.0 copy-start
  13.1 0.0 copy-start.1
  13.1 0.0 copy-start.2
  13.1 0.0 copy-start.4
  13.2 2.4 %collective-permute-start.5 = (bf16[5,192,128]{2,1,0:T(8,128)(2,1)S(1)}, bf16[5,192,128]{2,1,0:T(8,128)(2,1)S(1)}, u32[]{:S(2)}, u32[]{:S(2)}) collective-permute-start(bf16[5,192,128]{2,1,0:T(8,128)(2,1)S(1)} %get-tuple-element.42.chip_own), channel_id=1, source_target_pairs={{0,4},{4,0},{8,12},{12,8},{16,20},{20,16},{24,28},{28,24},{1,5},{5... | collective-permute-start | bytes 737288 | tf_op jit(solution)/shard_map/ppermute | solution.py:558
  15.5 3.6 %collective-permute-start.6 = (bf16[5,192,128]{2,1,0:T(8,128)(2,1)S(1)}, bf16[5,192,128]{2,1,0:T(8,128)(2,1)S(1)}, u32[]{:S(2)}, u32[]{:S(2)}) collective-permute-start(bf16[5,192,128]{2,1,0:T(8,128)(2,1)S(1)} %get-tuple-element.43.link_own), channel_id=1, source_target_pairs={{0,0},{28,28},{4,8},{8,4},{12,16},{16,12},{20,24},{24,20},{1,1},{2... | collective-permute-start | bytes 737288 | tf_op jit(solution)/shard_map/ppermute | solution.py:557
  19.1 2.8 %shard_map.159 = (bf16[5,192,128]{2,1,0:T(8,128)(2,1)S(1)}, bf16[5,192,128]{2,1,0:T(8,128)(2,1)S(1)}) custom-call(bf16[4,32,256]{2,1,0:T(8,128)(2,1)S(1)} %get-tuple-element.24.own, bf16[80,256]{1,0:T(8,128)(2,1)S(1)} %collective-permute-done.odd_in, bf16[80,256]{1,0:T(8,128)(2,1)S(1)} %collective-permute-done.1.even_in, ...), custom_call_target="tpu_custom_call" | custom-call | flops 500000000 | bytes 1000000 | tf_op jit(solution)/shard_map/pallas_call | solution.py:551
  21.9 0.1 collective-permute-start.3
  22.0 3.9 %collective-permute-start.4 = (bf16[5,192,128]{2,1,0:T(8,128)(2,1)S(1)}, bf16[5,192,128]{2,1,0:T(8,128)(2,1)S(1)}, u32[]{:S(2)}, u32[]{:S(2)}) collective-permute-start(bf16[5,192,128]{2,1,0:T(8,128)(2,1)S(1)} %get-tuple-element.41.link_own), channel_id=1, source_target_pairs={{0,0},{28,28},{4,8},{8,4},{12,16},{16,12},{20,24},{24,20},{1,1},{2... | collective-permute-start | bytes 737288 | tf_op jit(solution)/shard_map/ppermute | solution.py:557
  26.0 0.0 collective-permute-done.5.chip_in
  26.0 0.0 collective-permute-done.6.link_in
  26.0 0.0 copy-done.3
  26.0 1.7 %shard_map.161 = (bf16[2,160,128]{2,1,0:T(8,128)(2,1)S(1)}, f32[2,160]{1,0:T(2,128)S(1)}) custom-call(bf16[2,2,160,128]{3,2,1,0:T(8,128)(2,1)S(1)} %copy-done.1, bf16[2,2,160,384]{3,2,1,0:T(8,128)(2,1)S(1)} %copy-done, bf16[5,192,128]{2,1,0:T(8,128)(2,1)S(1)} %get-tuple-element.42.chip_own, bf16[5,192,128]{2,1,0:T(8,128)(2,1)S(1)} %get-tuple-element.43.link_own, ...), custom_call_target="tpu_custom_call" | custom-call | flops 1000000000 | bytes 4000000 | tf_op jit(solution)/shard_map/pallas_call | solution.py:563
  27.7 0.0 collective-permute-done.3.chip_in
  27.7 2.1 %collective-permute-done.4.link_in = bf16[5,192,128]{2,1,0:T(8,128)(2,1)S(1)} collective-permute-done((bf16[5,192,128]{2,1,0:T(8,128)(2,1)S(1)}, bf16[5,192,128]{2,1,0:T(8,128)(2,1)S(1)}, u32[]{:S(2)}, u32[]{:S(2)}) %collective-permute-start.4) | collective-permute-done | bytes 245792 | tf_op jit(solution)/shard_map/ppermute | solution.py:557
  29.8 2.3 %shard_map.162 = (bf16[2,2,160,128]{3,2,1,0:T(8,128)(2,1)}, f32[2,2,160]{2,1,0:T(2,128)}) custom-call(bf16[2,2,160,128]{3,2,1,0:T(8,128)(2,1)S(1)} %copy-done.1, bf16[2,2,160,384]{3,2,1,0:T(8,128)(2,1)S(1)} %copy-done, bf16[5,192,128]{2,1,0:T(8,128)(2,1)S(1)} %get-tuple-element.40.chip_own, bf16[5,192,128]{2,1,0:T(8,128)(2,1)S(1)} %get-tuple-element.41.link_own, ...), custom_call_target="tpu_custom_call" | custom-call | flops 1000000000 | bytes 4000000 | tf_op jit(solution)/shard_map/pallas_call | solution.py:563
  (5 shorter events, 0.0 us)
Async XLA Ops:
  2.2 8.1 %collective-permute-start = (bf16[80,256]{1,0:T(8,128)(2,1)S(1)}, bf16[80,256]{1,0:T(8,128)(2,1)S(1)}, u32[]{:S(2)}, u32[]{:S(2)}) collective-permute-start(bf16[80,256]{1,0:T(8,128)(2,1)S(1)} %get-tuple-element.25), channel_id=1, source_target_pairs={{0,1},{1,0},{2,3},{3,2},{4,5},{5,4},{6,7},{7,6},{8,9},{9,8},{10,11... | collective-permute-start | bytes 122888 | tf_op jit(solution)/shard_map/ppermute | solution.py:546
  4.3 6.0 %collective-permute-start.1 = (bf16[80,256]{1,0:T(8,128)(2,1)S(1)}, bf16[80,256]{1,0:T(8,128)(2,1)S(1)}, u32[]{:S(2)}, u32[]{:S(2)}) collective-permute-start(bf16[80,256]{1,0:T(8,128)(2,1)S(1)} %get-tuple-element.26), channel_id=1, source_target_pairs={{0,3},{1,2},{2,1},{3,0},{4,7},{5,6},{6,5},{7,4},{8,11},{9,10},{10,... | collective-permute-start | bytes 122888 | tf_op jit(solution)/shard_map/ppermute | solution.py:547
  6.1 4.2 %collective-permute-start.2 = (bf16[64,128]{1,0:T(8,128)(2,1)S(1)}, bf16[64,128]{1,0:T(8,128)(2,1)S(1)}, u32[]{:S(2)}, u32[]{:S(2)}) collective-permute-start(bf16[64,128]{1,0:T(8,128)(2,1)S(1)} %get-tuple-element.27), channel_id=1, source_target_pairs={{0,2},{1,3},{2,0},{3,1},{4,6},{5,7},{6,4},{7,5},{8,10},{9,11},{10,... | collective-permute-start | bytes 49160 | tf_op jit(solution)/shard_map/ppermute | solution.py:548
  10.3 15.7 %copy-start.3 = (bf16[3,3,256,128]{3,2,1,0:T(8,128)(2,1)S(1)}, bf16[3,3,256,128]{3,2,1,0:T(8,128)(2,1)}, u32[]{:S(2)}) copy-start(bf16[3,3,256,128]{3,2,1,0:T(8,128)(2,1)} %cand_k.3) | copy-start | bytes 1769476
  13.1 12.9 %copy-start = (bf16[2,2,160,384]{3,2,1,0:T(8,128)(2,1)S(1)}, bf16[2,2,160,384]{3,2,1,0:T(8,128)(2,1)}, u32[]{:S(2)}) copy-start(bf16[2,2,160,384]{3,2,1,0:T(8,128)(2,1)} %context.3) | copy-start | bytes 1474564
  13.1 12.9 %copy-start.1 = (bf16[2,2,160,128]{3,2,1,0:T(8,128)(2,1)S(1)}, bf16[2,2,160,128]{3,2,1,0:T(8,128)(2,1)}, u32[]{:S(2)}) copy-start(bf16[2,2,160,128]{3,2,1,0:T(8,128)(2,1)} %hidden.3) | copy-start | bytes 491524
  13.1 12.9 %copy-start.2 = (bf16[3,3,256,256]{3,2,1,0:T(8,128)(2,1)S(1)}, bf16[3,3,256,256]{3,2,1,0:T(8,128)(2,1)}, u32[]{:S(2)}) copy-start(bf16[3,3,256,256]{3,2,1,0:T(8,128)(2,1)} %gate_k.3) | copy-start | bytes 3538948
  13.1 12.9 %copy-start.4 = (bf16[128]{0:T(256)(128)(2,1)S(1)}, bf16[128]{0:T(256)(128)(2,1)}, u32[]{:S(2)}) copy-start(bf16[128]{0:T(256)(128)(2,1)} %param.27) | copy-start | bytes 772
  13.2 12.8 %collective-permute-start.5 = (bf16[5,192,128]{2,1,0:T(8,128)(2,1)S(1)}, bf16[5,192,128]{2,1,0:T(8,128)(2,1)S(1)}, u32[]{:S(2)}, u32[]{:S(2)}) collective-permute-start(bf16[5,192,128]{2,1,0:T(8,128)(2,1)S(1)} %get-tuple-element.42.chip_own), channel_id=1, source_target_pairs={{0,4},{4,0},{8,12},{12,8},{16,20},{20,16},{24,28},{28,24},{1,5},{5... | collective-permute-start | bytes 737288 | tf_op jit(solution)/shard_map/ppermute | solution.py:558
  15.5 10.4 %collective-permute-start.6 = (bf16[5,192,128]{2,1,0:T(8,128)(2,1)S(1)}, bf16[5,192,128]{2,1,0:T(8,128)(2,1)S(1)}, u32[]{:S(2)}, u32[]{:S(2)}) collective-permute-start(bf16[5,192,128]{2,1,0:T(8,128)(2,1)S(1)} %get-tuple-element.43.link_own), channel_id=1, source_target_pairs={{0,0},{28,28},{4,8},{8,4},{12,16},{16,12},{20,24},{24,20},{1,1},{2... | collective-permute-start | bytes 737288 | tf_op jit(solution)/shard_map/ppermute | solution.py:557
  21.9 5.8 %collective-permute-start.3 = (bf16[5,192,128]{2,1,0:T(8,128)(2,1)S(1)}, bf16[5,192,128]{2,1,0:T(8,128)(2,1)S(1)}, u32[]{:S(2)}, u32[]{:S(2)}) collective-permute-start(bf16[5,192,128]{2,1,0:T(8,128)(2,1)S(1)} %get-tuple-element.40.chip_own), channel_id=1, source_target_pairs={{0,4},{4,0},{8,12},{12,8},{16,20},{20,16},{24,28},{28,24},{1,5},{5... | collective-permute-start | bytes 737288 | tf_op jit(solution)/shard_map/ppermute | solution.py:558
  22.0 7.8 %collective-permute-start.4 = (bf16[5,192,128]{2,1,0:T(8,128)(2,1)S(1)}, bf16[5,192,128]{2,1,0:T(8,128)(2,1)S(1)}, u32[]{:S(2)}, u32[]{:S(2)}) collective-permute-start(bf16[5,192,128]{2,1,0:T(8,128)(2,1)S(1)} %get-tuple-element.41.link_own), channel_id=1, source_target_pairs={{0,0},{28,28},{4,8},{8,4},{12,16},{16,12},{20,24},{24,20},{1,1},{2... | collective-permute-start | bytes 737288 | tf_op jit(solution)/shard_map/ppermute | solution.py:557

commit v3 on v2

--- a/solution.py
+++ b/solution.py
@@ -487,11 +487,16 @@
     cols = lax.axis_size("col")
     rows = lax.axis_size("row")
     odd = [(i, i ^ 1) for i in range(cols)]
-    even = [(i, (cols - 1) - i) for i in range(cols)]
     across = [(i, (i + 2) % cols) for i in range(cols)]
     chip = [(i, i ^ 1) for i in range(rows)]
-    link = [(0, 0), (rows - 1, rows - 1)]
-    link += [(i, ((i + 1) ^ 1) - 1) for i in range(1, rows - 1)]
+
+    even, link = [], []
+    for r in range(rows):
+        for c in range(cols):
+            outer_col, outer_row = c in (0, cols - 1), r in (0, rows - 1)
+            even.append((r * cols + c, (r ^ 1) * cols + c if outer_col else r * cols + ((c - 1) ^ 1) + 1))
+            link.append((r * cols + c, r * cols + (c ^ 1) if outer_row else (((r - 1) ^ 1) + 1) * cols + c))
+
     pool, lane_rows = tables()
 
     (own, odd_out, even_out, far, hid, con, w1, w1t, w2, w2t, mw, pool, lane_rows, scale, bias, disp) = call(
@@ -544,7 +549,7 @@
         )
     )
     odd_in = lax.ppermute(odd_out, "col", odd)
-    even_in = lax.ppermute(even_out, "col", even)
+    even_in = lax.ppermute(even_out, ("row", "col"), even)
     far_in = lax.ppermute(far, "col", across)
     halos = []
     for v in range(2):
@@ -554,7 +559,7 @@
             flops=5 * 10**8,
             bytes_accessed=10**6,
         )(own, odd_in, even_in, far_in, hid, con, disp, w1, w1t, w2, w2t, mw, scale, bias, pool, lane_rows)
-        link_in = lax.ppermute(link_out, "row", link)
+        link_in = lax.ppermute(link_out, ("row", "col"), link)
         chip_in = lax.ppermute(chip_out, "row", chip)
         halos.append((chip_out, link_out, chip_in, link_in))
     done = ()

time: 32.3 us -> 27.4 us (0.85)
  starting transfers between devices: 14.6 us -> 9.2 us
  waiting for transfers between devices: 5.68 us -> 6.28 us
    ppermute x3, starting transfers between devices: 9.31 us -> 2.99 us  [the longest x2 1.69 us: local(): link_in = lax.ppermute(link_out, ('row', 'col'), link)]
    ppermute x3, waiting for transfers between devices: 2.12 us -> 3.32 us  [the longest x2 3.31 us: local(): link_in = lax.ppermute(link_out, ('row', 'col'), link)]
    ppermute x1, waiting for transfers between devices: 3.55 us -> 2.96 us  [local(): far_in = lax.ppermute(far, 'col', across)]
    ppermute x1, starting transfers between devices: 0.64 us -> 1.15 us  [local(): far_in = lax.ppermute(far, 'col', across)]
    ppermute x2, starting transfers between devices: 2.48 us -> 2.93 us  [local(): chip_in = lax.ppermute(chip_out, 'row', chip)]
  transfers between devices with their start and end apart: 7 -> 7, of which waited for: 2 -> 3; matrix products, arithmetic and copies ran while one was open for 0% -> 0% of each run, Pallas kernels for 14% -> 16%
where the time goes in v3:
time: 27.4 us; the launch traced here: 27.3 us
  Pallas kernels  11.1 us (41%)
  starting transfers between devices  9.2 us (34%)
  waiting for transfers between devices  6.28 us (23%)
  between operations  0.72 us (3%)
    pallas_call x2, Pallas kernels, local(): call(functools.partial(motion_kernel, v), [((5, EXT, UNITS), BF)] * 2, fl...  5.59 us
    pallas_call x2, Pallas kernels, local(): call(functools.partial(update_kernel, v), [(lead + (ROWS, TILE, UNITS), B...  3.94 us
    ppermute x2, waiting for transfers between devices, local(): link_in = lax.ppermute(link_out, ('row', 'col'), link)  3.31 us
    ppermute x1, waiting for transfers between devices, local(): far_in = lax.ppermute(far, 'col', across)  2.96 us
    ppermute x2, starting transfers between devices, local(): chip_in = lax.ppermute(chip_out, 'row', chip)  2.93 us
    ppermute x1, starting transfers between devices, local(): odd_in = lax.ppermute(odd_out, 'col', odd)  2.13 us
    ppermute x2, starting transfers between devices, local(): link_in = lax.ppermute(link_out, ('row', 'col'), link)  1.69 us
    pallas_call x1, Pallas kernels, local(): call(pack_kernel, [((4, 32, 256), BF), ((80, 256), BF), ((80, 256), BF),...  1.53 us
  transfers between devices with their start and end apart: 7, of which 3 were waited for; matrix products, arithmetic and copies ran while one was open for 0% of the time, Pallas kernels for 16%

profile of v3, /device:TPU:1, one launch (start us, length us, event | category | flops | bytes accessed | tf_op | source)
XLA Modules:
  0.0 27.3 jit_solution(3166994350578878834)
XLA Ops:
  0.6 1.5 %shard_map.158 = (bf16[4,32,256]{2,1,0:T(8,128)(2,1)S(1)}, bf16[80,256]{1,0:T(8,128)(2,1)S(1)}, bf16[80,256]{1,0:T(8,128)(2,1)S(1)}, bf16[64,128]{1,0:T(8,128)(2...) custom-call(f32[2,15,2,160]{3,2,1,0:T(2,128)} %vox_h.1, ...), custom_call_target="tpu_custom_call" | custom-call | flops 1000000 | bytes 2000000 | tf_op jit(solution)/shard_map/pallas_call | solution.py:502
  2.2 2.1 %collective-permute-start = (bf16[80,256]{1,0:T(8,128)(2,1)S(1)}, bf16[80,256]{1,0:T(8,128)(2,1)S(1)}, u32[]{:S(2)}, u32[]{:S(2)}) collective-permute-start(bf16[80,256]{1,0:T(8,128)(2,1)S(1)} %get-tuple-element.25), channel_id=1, source_target_pairs={{0,1},{1,0},{2,3},{3,2},{4,5},{5,4},{6,7},{7,6},{8,9},{9,8},{10,11... | collective-permute-start | bytes 122888 | tf_op jit(solution)/shard_map/ppermute | solution.py:551
  4.3 1.3 %collective-permute-start.1 = (bf16[80,256]{1,0:T(8,128)(2,1)S(1)}, bf16[80,256]{1,0:T(8,128)(2,1)S(1)}, u32[]{:S(2)}, u32[]{:S(2)}) collective-permute-start(bf16[80,256]{1,0:T(8,128)(2,1)S(1)} %get-tuple-element.26), channel_id=1, source_target_pairs={{0,4},{1,2},{2,1},{3,7},{4,0},{5,6},{6,5},{7,3},{8,12},{9,10},{10,... | collective-permute-start | bytes 122888 | tf_op jit(solution)/shard_map/ppermute | solution.py:552
  5.6 1.2 %collective-permute-start.2 = (bf16[64,128]{1,0:T(8,128)(2,1)S(1)}, bf16[64,128]{1,0:T(8,128)(2,1)S(1)}, u32[]{:S(2)}, u32[]{:S(2)}) collective-permute-start(bf16[64,128]{1,0:T(8,128)(2,1)S(1)} %get-tuple-element.27), channel_id=1, source_target_pairs={{0,2},{1,3},{2,0},{3,1},{4,6},{5,7},{6,4},{7,5},{8,10},{9,11},{10,... | collective-permute-start | bytes 49160 | tf_op jit(solution)/shard_map/ppermute | solution.py:553
  6.8 3.0 %collective-permute-done.2.far_in = bf16[64,128]{1,0:T(8,128)(2,1)S(1)} collective-permute-done((bf16[64,128]{1,0:T(8,128)(2,1)S(1)}, bf16[64,128]{1,0:T(8,128)(2,1)S(1)}, u32[]{:S(2)}, u32[]{:S(2)}) %collective-permute-start.2) | collective-permute-done | bytes 16416 | tf_op jit(solution)/shard_map/ppermute | solution.py:553
  9.7 0.0 collective-permute-done.odd_in
  9.7 0.0 collective-permute-done.1.even_in
  9.7 2.8 %shard_map.160 = (bf16[5,192,128]{2,1,0:T(8,128)(2,1)S(1)}, bf16[5,192,128]{2,1,0:T(8,128)(2,1)S(1)}) custom-call(bf16[4,32,256]{2,1,0:T(8,128)(2,1)S(1)} %get-tuple-element.24.own, bf16[80,256]{1,0:T(8,128)(2,1)S(1)} %collective-permute-done.odd_in, bf16[80,256]{1,0:T(8,128)(2,1)S(1)} %collective-permute-done.1.even_in, ...), custom_call_target="tpu_custom_call" | custom-call | flops 500000000 | bytes 1000000 | tf_op jit(solution)/shard_map/pallas_call | solution.py:556
  12.5 0.0 copy-start
  12.5 0.0 copy-start.1
  12.5 0.0 copy-start.2
  12.6 0.0 copy-start.4
  12.6 1.7 %collective-permute-start.5 = (bf16[5,192,128]{2,1,0:T(8,128)(2,1)S(1)}, bf16[5,192,128]{2,1,0:T(8,128)(2,1)S(1)}, u32[]{:S(2)}, u32[]{:S(2)}) collective-permute-start(bf16[5,192,128]{2,1,0:T(8,128)(2,1)S(1)} %get-tuple-element.42.chip_own), channel_id=1, source_target_pairs={{0,4},{4,0},{8,12},{12,8},{16,20},{20,16},{24,28},{28,24},{1,5},{5... | collective-permute-start | bytes 737288 | tf_op jit(solution)/shard_map/ppermute | solution.py:563
  14.3 0.8 %collective-permute-start.6 = (bf16[5,192,128]{2,1,0:T(8,128)(2,1)S(1)}, bf16[5,192,128]{2,1,0:T(8,128)(2,1)S(1)}, u32[]{:S(2)}, u32[]{:S(2)}) collective-permute-start(bf16[5,192,128]{2,1,0:T(8,128)(2,1)S(1)} %get-tuple-element.43.link_own), channel_id=1, source_target_pairs={{0,1},{1,0},{2,3},{3,2},{4,8},{5,9},{6,10},{7,11},{8,4},{9,5},{10,... | collective-permute-start | bytes 737288 | tf_op jit(solution)/shard_map/ppermute | solution.py:562
  15.1 2.8 %shard_map.159 = (bf16[5,192,128]{2,1,0:T(8,128)(2,1)S(1)}, bf16[5,192,128]{2,1,0:T(8,128)(2,1)S(1)}) custom-call(bf16[4,32,256]{2,1,0:T(8,128)(2,1)S(1)} %get-tuple-element.24.own, bf16[80,256]{1,0:T(8,128)(2,1)S(1)} %collective-permute-done.odd_in, bf16[80,256]{1,0:T(8,128)(2,1)S(1)} %collective-permute-done.1.even_in, ...), custom_call_target="tpu_custom_call" | custom-call | flops 500000000 | bytes 1000000 | tf_op jit(solution)/shard_map/pallas_call | solution.py:556
  17.9 1.2 %collective-permute-start.3 = (bf16[5,192,128]{2,1,0:T(8,128)(2,1)S(1)}, bf16[5,192,128]{2,1,0:T(8,128)(2,1)S(1)}, u32[]{:S(2)}, u32[]{:S(2)}) collective-permute-start(bf16[5,192,128]{2,1,0:T(8,128)(2,1)S(1)} %get-tuple-element.40.chip_own), channel_id=1, source_target_pairs={{0,4},{4,0},{8,12},{12,8},{16,20},{20,16},{24,28},{28,24},{1,5},{5... | collective-permute-start | bytes 737288 | tf_op jit(solution)/shard_map/ppermute | solution.py:563
  19.1 0.9 %collective-permute-start.4 = (bf16[5,192,128]{2,1,0:T(8,128)(2,1)S(1)}, bf16[5,192,128]{2,1,0:T(8,128)(2,1)S(1)}, u32[]{:S(2)}, u32[]{:S(2)}) collective-permute-start(bf16[5,192,128]{2,1,0:T(8,128)(2,1)S(1)} %get-tuple-element.41.link_own), channel_id=1, source_target_pairs={{0,1},{1,0},{2,3},{3,2},{4,8},{5,9},{6,10},{7,11},{8,4},{9,5},{10,... | collective-permute-start | bytes 737288 | tf_op jit(solution)/shard_map/ppermute | solution.py:562
  20.0 0.0 collective-permute-done.5.chip_in
  20.0 0.2 collective-permute-done.6.link_in
  20.2 0.0 copy-done.2
  20.2 1.7 %shard_map.161 = (bf16[2,160,128]{2,1,0:T(8,128)(2,1)S(1)}, f32[2,160]{1,0:T(2,128)S(1)}) custom-call(bf16[2,2,160,128]{3,2,1,0:T(8,128)(2,1)S(1)} %copy-done.1, bf16[2,2,160,384]{3,2,1,0:T(8,128)(2,1)S(1)} %copy-done, bf16[5,192,128]{2,1,0:T(8,128)(2,1)S(1)} %get-tuple-element.42.chip_own, bf16[5,192,128]{2,1,0:T(8,128)(2,1)S(1)} %get-tuple-element.43.link_own, ...), custom_call_target="tpu_custom_call" | custom-call | flops 1000000000 | bytes 4000000 | tf_op jit(solution)/shard_map/pallas_call | solution.py:568
  21.9 0.0 collective-permute-done.3.chip_in
  21.9 3.2 %collective-permute-done.4.link_in = bf16[5,192,128]{2,1,0:T(8,128)(2,1)S(1)} collective-permute-done((bf16[5,192,128]{2,1,0:T(8,128)(2,1)S(1)}, bf16[5,192,128]{2,1,0:T(8,128)(2,1)S(1)}, u32[]{:S(2)}, u32[]{:S(2)}) %collective-permute-start.4) | collective-permute-done | bytes 245792 | tf_op jit(solution)/shard_map/ppermute | solution.py:562
  25.0 2.3 %shard_map.162 = (bf16[2,2,160,128]{3,2,1,0:T(8,128)(2,1)}, f32[2,2,160]{2,1,0:T(2,128)}) custom-call(bf16[2,2,160,128]{3,2,1,0:T(8,128)(2,1)S(1)} %copy-done.1, bf16[2,2,160,384]{3,2,1,0:T(8,128)(2,1)S(1)} %copy-done, bf16[5,192,128]{2,1,0:T(8,128)(2,1)S(1)} %get-tuple-element.40.chip_own, bf16[5,192,128]{2,1,0:T(8,128)(2,1)S(1)} %get-tuple-element.41.link_own, ...), custom_call_target="tpu_custom_call" | custom-call | flops 1000000000 | bytes 4000000 | tf_op jit(solution)/shard_map/pallas_call | solution.py:568
  (5 shorter events, 0.0 us)
Async XLA Ops:
  2.2 7.5 %collective-permute-start = (bf16[80,256]{1,0:T(8,128)(2,1)S(1)}, bf16[80,256]{1,0:T(8,128)(2,1)S(1)}, u32[]{:S(2)}, u32[]{:S(2)}) collective-permute-start(bf16[80,256]{1,0:T(8,128)(2,1)S(1)} %get-tuple-element.25), channel_id=1, source_target_pairs={{0,1},{1,0},{2,3},{3,2},{4,5},{5,4},{6,7},{7,6},{8,9},{9,8},{10,11... | collective-permute-start | bytes 122888 | tf_op jit(solution)/shard_map/ppermute | solution.py:551
  4.3 5.4 %collective-permute-start.1 = (bf16[80,256]{1,0:T(8,128)(2,1)S(1)}, bf16[80,256]{1,0:T(8,128)(2,1)S(1)}, u32[]{:S(2)}, u32[]{:S(2)}) collective-permute-start(bf16[80,256]{1,0:T(8,128)(2,1)S(1)} %get-tuple-element.26), channel_id=1, source_target_pairs={{0,4},{1,2},{2,1},{3,7},{4,0},{5,6},{6,5},{7,3},{8,12},{9,10},{10,... | collective-permute-start | bytes 122888 | tf_op jit(solution)/shard_map/ppermute | solution.py:552
  5.6 4.1 %collective-permute-start.2 = (bf16[64,128]{1,0:T(8,128)(2,1)S(1)}, bf16[64,128]{1,0:T(8,128)(2,1)S(1)}, u32[]{:S(2)}, u32[]{:S(2)}) collective-permute-start(bf16[64,128]{1,0:T(8,128)(2,1)S(1)} %get-tuple-element.27), channel_id=1, source_target_pairs={{0,2},{1,3},{2,0},{3,1},{4,6},{5,7},{6,4},{7,5},{8,10},{9,11},{10,... | collective-permute-start | bytes 49160 | tf_op jit(solution)/shard_map/ppermute | solution.py:553
  9.7 10.4 %copy-start.3 = (bf16[3,3,256,128]{3,2,1,0:T(8,128)(2,1)S(1)}, bf16[3,3,256,128]{3,2,1,0:T(8,128)(2,1)}, u32[]{:S(2)}) copy-start(bf16[3,3,256,128]{3,2,1,0:T(8,128)(2,1)} %cand_k.3) | copy-start | bytes 1769476
  12.5 7.6 %copy-start = (bf16[2,2,160,384]{3,2,1,0:T(8,128)(2,1)S(1)}, bf16[2,2,160,384]{3,2,1,0:T(8,128)(2,1)}, u32[]{:S(2)}) copy-start(bf16[2,2,160,384]{3,2,1,0:T(8,128)(2,1)} %context.3) | copy-start | bytes 1474564
  12.5 7.6 %copy-start.1 = (bf16[2,2,160,128]{3,2,1,0:T(8,128)(2,1)S(1)}, bf16[2,2,160,128]{3,2,1,0:T(8,128)(2,1)}, u32[]{:S(2)}) copy-start(bf16[2,2,160,128]{3,2,1,0:T(8,128)(2,1)} %hidden.3) | copy-start | bytes 491524
  12.5 7.6 %copy-start.2 = (bf16[3,3,256,256]{3,2,1,0:T(8,128)(2,1)S(1)}, bf16[3,3,256,256]{3,2,1,0:T(8,128)(2,1)}, u32[]{:S(2)}) copy-start(bf16[3,3,256,256]{3,2,1,0:T(8,128)(2,1)} %gate_k.3) | copy-start | bytes 3538948
  12.6 7.6 %copy-start.4 = (bf16[128]{0:T(256)(128)(2,1)S(1)}, bf16[128]{0:T(256)(128)(2,1)}, u32[]{:S(2)}) copy-start(bf16[128]{0:T(256)(128)(2,1)} %param.27) | copy-start | bytes 772
  12.6 7.4 %collective-permute-start.5 = (bf16[5,192,128]{2,1,0:T(8,128)(2,1)S(1)}, bf16[5,192,128]{2,1,0:T(8,128)(2,1)S(1)}, u32[]{:S(2)}, u32[]{:S(2)}) collective-permute-start(bf16[5,192,128]{2,1,0:T(8,128)(2,1)S(1)} %get-tuple-element.42.chip_own), channel_id=1, source_target_pairs={{0,4},{4,0},{8,12},{12,8},{16,20},{20,16},{24,28},{28,24},{1,5},{5... | collective-permute-start | bytes 737288 | tf_op jit(solution)/shard_map/ppermute | solution.py:563
  14.3 5.9 %collective-permute-start.6 = (bf16[5,192,128]{2,1,0:T(8,128)(2,1)S(1)}, bf16[5,192,128]{2,1,0:T(8,128)(2,1)S(1)}, u32[]{:S(2)}, u32[]{:S(2)}) collective-permute-start(bf16[5,192,128]{2,1,0:T(8,128)(2,1)S(1)} %get-tuple-element.43.link_own), channel_id=1, source_target_pairs={{0,1},{1,0},{2,3},{3,2},{4,8},{5,9},{6,10},{7,11},{8,4},{9,5},{10,... | collective-permute-start | bytes 737288 | tf_op jit(solution)/shard_map/ppermute | solution.py:562
  17.9 4.0 %collective-permute-start.3 = (bf16[5,192,128]{2,1,0:T(8,128)(2,1)S(1)}, bf16[5,192,128]{2,1,0:T(8,128)(2,1)S(1)}, u32[]{:S(2)}, u32[]{:S(2)}) collective-permute-start(bf16[5,192,128]{2,1,0:T(8,128)(2,1)S(1)} %get-tuple-element.40.chip_own), channel_id=1, source_target_pairs={{0,4},{4,0},{8,12},{12,8},{16,20},{20,16},{24,28},{28,24},{1,5},{5... | collective-permute-start | bytes 737288 | tf_op jit(solution)/shard_map/ppermute | solution.py:563
  19.1 5.9 %collective-permute-start.4 = (bf16[5,192,128]{2,1,0:T(8,128)(2,1)S(1)}, bf16[5,192,128]{2,1,0:T(8,128)(2,1)S(1)}, u32[]{:S(2)}, u32[]{:S(2)}) collective-permute-start(bf16[5,192,128]{2,1,0:T(8,128)(2,1)S(1)} %get-tuple-element.41.link_own), channel_id=1, source_target_pairs={{0,1},{1,0},{2,3},{3,2},{4,8},{5,9},{6,10},{7,11},{8,4},{9,5},{10,... | collective-permute-start | bytes 737288 | tf_op jit(solution)/shard_map/ppermute | solution.py:562

commit v4 on v3

v4 whole, which is shorter than its diff:
```python
import jax
import jax.numpy as jnp
import numpy as np
from jax import lax
from jax.experimental import pallas as pl
from jax.experimental.pallas import tpu as pltpu
from jax.sharding import PartitionSpec as P

BF = jnp.bfloat16
F32 = jnp.float32

ROWS = 2
TILE = 160
IMAGE = 640
PAD = 16
EXT = TILE + 2 * PAD
BINS = 15
UNITS = 128
NEAR = 48
FAR = 72
WINDOW = 512
LAST = FAR + 2 * TILE + NEAR - 1
TAPS = 9
LEVELS = 4
GROUP = 40
STARTS = (0, 17, 30, 41)
VMEM_LIMIT = 48 * 1024 * 1024


def tables():
    pool = np.zeros((128, 128), np.float32)
    firsts = (28, 12, 4, 0)
    counts = (17, 13, 11, 10)
    for level in range(LEVELS):
        width = 2**level
        for k in range(counts[level]):
            entry = firsts[level] + k
            pool[entry * width : (entry + 1) * width, STARTS[level] + k] = 1.0 / (16 * width)
    lane = np.arange(128)
    member = lane % GROUP
    used = (member < LEVELS * TAPS) & (lane < 3 * GROUP)
    level = np.where(used, member // TAPS, 0)
    first = np.where(used, np.take(np.array(STARTS), level) + member % TAPS, 0)
    scale = np.where(used, 0.5**level, 0.0)
    low = ((lane >= GROUP) & (lane < 2 * GROUP)).astype(np.float32)
    rows = np.zeros((8, 128), np.float32)
    rows[0], rows[1], rows[2] = first, scale, low
    return np.concatenate([pool, pool]).astype(jnp.bfloat16), rows


def split(value):
    high = value.astype(BF).astype(F32)
    return high, value - high


def silu_of_half(half):
    return half + half * jnp.tanh(half)


def sigmoid(value):
    return 0.5 * jnp.tanh(0.5 * value) + 0.5


def pack_kernel(
    vox_h,
    disp_h,
    hidden_h,
    context_h,
    first_h,
    bias_h,
    second_h,
    motion_h,
    scale_h,
    mbias_h,
    pool_h,
    rows_h,
    own,
    odd_out,
    even_out,
    far,
    chip,
    link,
    w1,
    w1t,
    w2,
    w2t,
    mw,
    pool,
    rows,
    scale,
    mbias,
    disp,
    vox,
    first,
    bias,
    motion,
    sems,
):
    row_odd = lax.axis_index("row") % 2
    pairs = [(vox_h, vox), (disp_h, disp)]
    for v in range(2):
        for target, y in ((chip, 1 - row_odd), (link, row_odd)):
            pairs += [
                (hidden_h.at[v], target.at[v, 0:ROWS]),
                (context_h.at[v, y, :, UNITS : 2 * UNITS], target.at[v, ROWS]),
            ]
    data = len(pairs)
    pairs += [
        (first_h, first),
        (bias_h, bias),
        (second_h, w2),
        (motion_h, motion),
        (scale_h, scale),
        (mbias_h, mbias),
        (pool_h, pool),
        (rows_h, rows),
    ]
    copies = [pltpu.make_async_copy(a, b, sems.at[k]) for k, (a, b) in enumerate(pairs)]
    for copy in copies:
        copy.start()
    for copy in copies[:data]:
        copy.wait()
    col = lax.axis_index("col")
    is_even = col % 2 == 0
    row_at = lax.broadcasted_iota(jnp.int32, (8, 128), 0)
    parts = []
    edges_right, edges_left = [], []
    for v in range(2):
        for y in range(ROWS):
            high, low = split(vox[v, :, y, :])
            ones = jnp.ones((1, TILE), F32)
            block = jnp.concatenate([high, ones, low, ones], axis=0)
            parts.append(block)
            own[2 * v + y] = jnp.concatenate(
                [block, jnp.zeros((32, 256 - TILE), F32)], axis=1
            ).astype(BF)

            def context_at(at):
                on_chip, on_link = chip[v, ROWS, at].astype(F32), link[v, ROWS, at].astype(F32)
                return jnp.where(row_odd == y, on_link, on_chip)

            hid_last = pltpu.roll(chip[v, y, 144:160, :].astype(F32)[8:16], 2, 0)
            con_last = pltpu.roll(context_at(slice(144, 160))[8:16], 3, 0)
            hid_first = chip[v, y, 0:16, :].astype(F32)[0:8]
            con_first = pltpu.roll(context_at(slice(0, 16))[0:8], 2, 0)
            depth = disp[v, y : y + 1, :]
            d_last = pltpu.roll(jnp.broadcast_to(depth[:, 32:160], (8, 128)), 8, 1)
            d_first = jnp.broadcast_to(depth[:, 0:128], (8, 128))

            def edge(hid, con, dis):
                d_high, rest = split(dis)
                d_mid, d_low = split(rest)
                out = jnp.where(row_at < 2, hid, con)
                out = jnp.where(row_at == 3, d_high, out)
                out = jnp.where(row_at == 4, d_mid, out)
                return jnp.where(row_at >= 5, d_low, out)

            edges_right.append(edge(hid_last, con_last, d_last))
            edges_left.append(edge(hid_first, con_first, d_first))

    def emit(at, to_right, to_left):
        odd_out[at, :] = jnp.where(is_even, to_right, to_left).astype(BF)
        even_out[at, :] = jnp.where(is_even, to_left, to_right).astype(BF)

    blank = jnp.zeros((32, 256 - TILE - NEAR), F32)
    for y in range(ROWS):
        f0, f1 = parts[y], parts[ROWS + y]
        rows_at = pl.ds(32 * y, 32)
        emit(
            rows_at,
            jnp.concatenate([f1, f0[:, TILE - NEAR :], blank], axis=1),
            jnp.concatenate([f0, f1[:, :NEAR], blank], axis=1),
        )
        tail = jnp.concatenate([f1[:, TILE - FAR :], jnp.zeros((32, 128 - FAR), F32)], axis=1)
        far[rows_at, :] = jnp.where(col < 2, tail, f0[:, :128]).astype(BF)

    def gathered(edges):
        return jnp.concatenate(
            [
                jnp.concatenate([edges[0], edges[1]], axis=0),
                jnp.concatenate([edges[2], edges[3]], axis=0),
            ],
            axis=1,
        )

    emit(pl.ds(64, 16), gathered(edges_right), gathered(edges_left))
    for copy in copies[data:]:
        copy.wait()
    w_high, w_low = split(first[...] * 0.5)
    b_high, rest = split(bias[...] * 0.5)
    b_mid, b_low = split(rest)
    stacked = jnp.concatenate([w_high, b_high, w_high, b_mid, w_low, b_low], axis=0)
    block = jnp.concatenate([stacked, jnp.zeros((16, 256), F32)], axis=0).astype(BF)
    empty = jnp.zeros((64, 256), BF)
    for k in range(4):
        for m in range(4):
            w1[64 * k : 64 * k + 64, 256 * m : 256 * m + 256] = block if k == m else empty
    w1t[...] = jnp.concatenate([stacked, jnp.zeros((80, 256), F32)], axis=0).T.astype(BF)
    w2t[...] = w2[...].astype(F32).T.astype(BF)
    m_high, m_low = split(motion[...])
    gap = jnp.zeros((GROUP - LEVELS * TAPS, 128), F32)
    mw[...] = jnp.concatenate(
        [m_high, gap, m_high, gap, m_low, gap, jnp.zeros((8, 128), F32)], axis=0
    ).astype(BF)


def motion_kernel(
    own,
    odd_in,
    even_in,
    far_in,
    disp,
    w1,
    w1t,
    w2,
    w2t,
    mw,
    scale,
    bias,
    pool,
    rows,
    out,
):
    col = lax.axis_index("col")
    is_even = col % 2 == 0

    def received(at):
        first, second = odd_in[at, :].astype(F32), even_in[at, :].astype(F32)
        left = jnp.where(col > 0, jnp.where(is_even, second, first), 0.0)
        right = jnp.where(col < 3, jnp.where(is_even, first, second), 0.0)
        return left, right

    cases = [(v, y) for v in range(2) for y in range(ROWS)]
    edge_left, edge_right = received(pl.ds(64, 16))
    edges = [
        tuple(e[8 * y : 8 * y + 8, 128 * v : 128 * v + 128] for e in (edge_left, edge_right))
        for v, y in cases
    ]
    depth_rows = []
    for (v, y), (e_l, e_r) in zip(cases, edges):
        d_l = e_l[3:4] + e_l[4:5] + e_l[5:6]
        d_r = e_r[3:4] + e_r[4:5] + e_r[5:6]
        depth_rows.append(
            jnp.concatenate(
                [
                    jnp.zeros((1, 8), F32),
                    d_l[:, :8],
                    disp[v, y : y + 1, :],
                    d_r[:, :8],
                    jnp.zeros((1, 72), F32),
                ],
                axis=1,
            )
        )
    depth_rows.append(jnp.zeros((4, 256), F32))
    depths = jnp.concatenate(depth_rows, axis=0).T

    blank = jnp.zeros((32, WINDOW - 1 - LAST), F32)
    sides = [received(pl.ds(32 * y, 32)) for y in range(ROWS)]
    queries, windows = [], []
    for v, y in cases:
        left, right = sides[y]
        far = far_in[32 * y : 32 * y + 32, :].astype(F32)[:, :FAR]
        mine = own[ROWS * v + y].astype(F32)[:, :TILE]
        other = own[ROWS * (1 - v) + y].astype(F32)[:, :TILE]
        if v == 0:
            far = jnp.where(col >= 2, far, 0.0)
            pieces = [far, left[:, :TILE], other, right[:, TILE : TILE + NEAR], blank]
            ends = (left[:, TILE + NEAR - PAD : TILE + NEAR], right[:, :PAD])
        else:
            far = jnp.where(col < 2, far, 0.0)
            pieces = [left[:, TILE : TILE + NEAR], other, right[:, :TILE], far, blank]
            ends = (left[:, TILE - PAD : TILE], right[:, TILE : TILE + PAD])
        window = jnp.concatenate(pieces, axis=1)
        windows.append(jnp.concatenate([window, window[:16]], axis=0).astype(BF))
        query = jnp.concatenate([ends[0], mine, ends[1], jnp.zeros((32, 256 - EXT), F32)], axis=1)
        queries += [query, query[:16], jnp.zeros((16, 256), F32)]

    stacked = jnp.concatenate(queries, axis=0).T.astype(BF)
    layer = silu_of_half(jnp.dot(stacked[:EXT], w1[...], preferred_element_type=F32)).astype(BF)
    layer = jnp.concatenate([layer[:, 256 * k : 256 * k + 256] for k in range(4)], axis=0)
    features = jnp.dot(layer, w2[...], preferred_element_type=F32).astype(BF)
    layer = silu_of_half(
        jnp.dot(w1t[:, :48], jnp.concatenate(windows, axis=1), preferred_element_type=F32)
    ).astype(BF)
    match = jnp.dot(w2t[...], layer, preferred_element_type=F32).astype(BF)

    first = rows[0:1, :].astype(jnp.int32)
    level_scale = rows[1:2, :]
    is_low = rows[2:3, :] > 0.5
    lane = lax.broadcasted_iota(jnp.int32, (EXT, 128), 1)
    pixel = lax.broadcasted_iota(jnp.int32, (EXT, 1), 0)
    column = pixel + (col * TILE - PAD)
    inside = (column >= 0) & (column < IMAGE)
    pixel = pixel.astype(F32)
    depth_scale = scale[...] * (1.0 / 192.0)

    nears, rests = [], []
    for k, (v, y) in enumerate(cases):
        scores = jnp.dot(
            features[EXT * k : EXT * k + EXT],
            match[:, WINDOW * k : WINDOW * k + WINDOW],
            preferred_element_type=F32,
        )
        spot = (pixel - PAD if v == 0 else (EXT - 1 - PAD) - pixel) - depths[:EXT, k : k + 1]
        eighth = jnp.floor(spot * 0.125)
        rests.append(spot - 8.0 * eighth)
        start = (8.0 * eighth).astype(jnp.int32) + (FAR + TILE - 32)
        index = start + lane if v == 0 else (LAST - start) - lane
        block, place = index >> 7, index & 127
        near = jnp.zeros((EXT, 128), F32)
        for m in range(WINDOW // 128):
            taken = jnp.take_along_axis(
                scores[:, 128 * m : 128 * m + 128], place, axis=1, mode="promise_in_bounds"
            )
            near = jnp.where(block == m, taken, near)
        high, low = split(near)
        nears.append(jnp.concatenate([high.astype(BF), low.astype(BF)], axis=1))
    pooled = jnp.dot(jnp.concatenate(nears, axis=0), pool[...], preferred_element_type=F32)
    looks = []
    for k in range(4):
        table = pooled[EXT * k : EXT * k + EXT]
        at = rests[k] * level_scale
        floor = jnp.floor(at)
        index = floor.astype(jnp.int32) + first
        lower = jnp.take_along_axis(table, index, axis=1, mode="promise_in_bounds")
        upper = jnp.take_along_axis(table, index + 1, axis=1, mode="promise_in_bounds")
        high, low = split(lower + (at - floor) * (upper - lower))
        looks.append(jnp.where(is_low, low, high).astype(BF))
    sums = jnp.dot(jnp.concatenate(looks, axis=0), mw[...], preferred_element_type=F32)
    for k, (v, y) in enumerate(cases):
        half = 0.5 * (
            sums[EXT * k : EXT * k + EXT] + depths[:EXT, k : k + 1] * depth_scale + bias[...]
        )
        value = jnp.where(inside, silu_of_half(half), 0.0)
        e_l, e_r = edges[k]
        out[v, y] = jnp.concatenate([e_l, value[8 : EXT - 8], e_r], axis=0).astype(BF)


def widened(middle, ends, shift_left, shift_right):
    before = pltpu.roll(ends[0:16].astype(F32), shift_left, 0).astype(BF)
    after = pltpu.roll(ends[EXT - 16 :].astype(F32), shift_right, 0).astype(BF)
    return jnp.concatenate([before, middle, after], axis=0)


def wide_hidden(middle, ends):
    return widened(middle, ends, 14, 8)


def wide_context(middle, ends):
    return widened(middle, ends, 13, 6)


def kernel_rows(kernel, rows, inputs=slice(None), outputs=slice(None)):
    return jnp.concatenate(
        [
            jnp.concatenate([kernel[a, b, inputs, outputs] for a in rows], axis=0)
            for b in range(3)
        ],
        axis=1,
    )


def convolved(pieces, weights):
    stacked = jnp.concatenate(
        [jnp.concatenate([piece[v] for piece in pieces], axis=1) for v in range(2)], axis=0
    )
    products = jnp.dot(stacked, weights, preferred_element_type=F32)
    width = weights.shape[1] // 3
    out = []
    for v in range(2):
        mine = products[EXT * v : EXT * v + EXT]
        before, at, after = (mine[:, width * b : width * b + width] for b in range(3))
        if v == 1:
            before, after = after, before
        out.append(pltpu.roll(before, 1, 0) + at + pltpu.roll(after, EXT - 1, 0))
    return out


RESET = slice(UNITS, 2 * UNITS)
FROM_STATE, FROM_MOTION = slice(0, UNITS), slice(UNITS, 2 * UNITS)


def inner_kernel(hidden, context, mot, gate_k, cand_k, gates, outer, cands, state):
    for v in range(2):
        for y in range(ROWS):
            state[v, y] = wide_hidden(hidden[v, y], mot[v, y])
    h2, h3 = ([state[v, y] for v in range(2)] for y in range(ROWS))
    m2, m3 = ([mot[v, y] for v in range(2)] for y in range(ROWS))
    for y, rows in ((0, (1, 2)), (1, (0, 1))):
        terms = convolved([h2, m2, h3, m3], kernel_rows(gate_k, rows))
        for v in range(2):
            wide = wide_context(context[v, y, :, RESET], mot[v, y])
            gates[v, y, :, :UNITS] = terms[v][:, :UNITS]
            gates[v, y, :, UNITS:] = terms[v][:, UNITS:] + wide.astype(F32)
        terms = convolved([m2, m3], kernel_rows(cand_k, rows, FROM_MOTION))
        for v in range(2):
            cands[v, y] = terms[v][PAD : PAD + TILE] + context[v, y, :, 2 * UNITS :].astype(F32)
    for side, pieces, rows in ((0, [h2, m2], (2,)), (1, [h3, m3], (0,))):
        terms = convolved(pieces, kernel_rows(gate_k, rows, outputs=RESET))
        for v in range(2):
            outer[v, side] = terms[v]


def outer_kernel(
    hidden,
    context,
    chip_in,
    link_in,
    mot_chip,
    mot_link,
    gates,
    outer,
    cands,
    state,
    gate_k,
    cand_k,
    head,
    new,
    inc,
    halo,
    halo_mot,
):
    row = lax.axis_index("row")
    row_even = row % 2 == 0
    last = lax.axis_size("row") - 1

    @pl.when(row_even)
    def _():
        halo[0] = jnp.where(row > 0, link_in[...], jnp.zeros_like(link_in))
        halo[1] = chip_in[...]
        halo_mot[0] = jnp.where(row > 0, mot_link[...], jnp.zeros_like(mot_link))
        halo_mot[1] = mot_chip[...]

    @pl.when(jnp.logical_not(row_even))
    def _():
        halo[0] = chip_in[...]
        halo[1] = jnp.where(row < last, link_in[...], jnp.zeros_like(link_in))
        halo_mot[0] = mot_chip[...]
        halo_mot[1] = jnp.where(row < last, mot_link[...], jnp.zeros_like(mot_link))

    def beyond(side, y):
        mots = [halo_mot[side, v, y] for v in range(2)]
        return [wide_hidden(halo[side, v, y], mots[v]) for v in range(2)], mots

    h0, m0 = beyond(0, 0)
    h1, m1 = beyond(0, 1)
    h4, m4 = beyond(1, 0)
    h5, m5 = beyond(1, 1)
    updates, resets = [], []
    for side, pieces, rows in ((0, [h0, m0, h1, m1], (0, 1)), (1, [h4, m4, h5, m5], (1, 2))):
        terms = convolved(pieces, kernel_rows(gate_k, rows, outputs=RESET))
        near_h, near_m = (h1, m1) if side == 0 else (h4, m4)
        resets.append([])
        for v in range(2):
            wide = wide_context(halo[side, v, ROWS], near_m[v]).astype(F32)
            gate = sigmoid(terms[v] + outer[v, side] + wide)
            resets[-1].append((gate * near_h[v].astype(F32)).astype(BF))
    for y, pieces, rows in ((0, [h1, m1], (0,)), (1, [h4, m4], (2,))):
        terms = convolved(pieces, kernel_rows(gate_k, rows))
        updates.append([])
        resets.append([])
        for v in range(2):
            both = terms[v] + gates[v, y]
            gate = sigmoid(both[:, UNITS:])
            resets[-1].append((gate * state[v, y].astype(F32)).astype(BF))
            updates[-1].append(
                sigmoid(
                    both[PAD : PAD + TILE, :UNITS] + context[v, y, :, :UNITS].astype(F32)
                )
            )
    r1, r4, r2, r3 = resets
    head_rows = jnp.broadcast_to(head[...].astype(F32), (8, UNITS)).astype(BF)
    for y, pieces, row_at in ((0, [r1, r2, r3, m1], 0), (1, [r2, r3, r4, m4], 2)):
        weights = jnp.concatenate(
            [
                kernel_rows(cand_k, (0, 1, 2), FROM_STATE),
                kernel_rows(cand_k, (row_at,), FROM_MOTION),
            ],
            axis=0,
        )
        terms = convolved(pieces, weights)
        for v in range(2):
            candidate = jnp.tanh(terms[v][PAD : PAD + TILE] + cands[v, y])
            old = hidden[v, y].astype(F32)
            update = updates[y][v]
            fresh = ((1.0 - update) * old + update * candidate).astype(BF)
            new[v, y] = fresh
            inc[v, y : y + 1, :] = lax.dot_general(
                head_rows, fresh, (((1,), (1,)), ((), ())), preferred_element_type=F32
            )[0:1]


def call(kernel, outs, in_specs=None, scratch=(), **cost):
    return pl.pallas_call(
        kernel,
        **({} if in_specs is None else {"in_specs": in_specs}),
        out_shape=[jax.ShapeDtypeStruct(shape, dtype) for shape, dtype in outs],
        scratch_shapes=list(scratch),
        compiler_params=pltpu.CompilerParams(vmem_limit_bytes=VMEM_LIMIT),
        cost_estimate=pl.CostEstimate(transcendentals=0, **cost),
    )


def local(
    voxels,
    disparity,
    hidden,
    context,
    embed_first,
    embed_bias,
    embed_second,
    motion_weight,
    motion_scale,
    motion_bias,
    gate_kernel,
    candidate_kernel,
    head_weight,
):
    cols = lax.axis_size("col")
    rows = lax.axis_size("row")
    odd = [(i, i ^ 1) for i in range(cols)]
    across = [(i, (i + 2) % cols) for i in range(cols)]
    chip = [(i, i ^ 1) for i in range(rows)]

    even, link = [], []
    for r in range(rows):
        for c in range(cols):
            outer_col, outer_row = c in (0, cols - 1), r in (0, rows - 1)
            even.append((r * cols + c, (r ^ 1) * cols + c if outer_col else r * cols + ((c - 1) ^ 1) + 1))
            link.append((r * cols + c, r * cols + (c ^ 1) if outer_row else (((r - 1) ^ 1) + 1) * cols + c))

    pool, lane_rows = tables()

    (own, odd_out, even_out, far, chip_out, link_out, w1, w1t, w2, w2t, mw, pool, lane_rows, scale, bias, disp) = call(
        pack_kernel,
        [
            ((4, 32, 256), BF),
            ((80, 256), BF),
            ((80, 256), BF),
            ((64, 128), BF),
            ((2, ROWS + 1, TILE, UNITS), BF),
            ((2, ROWS + 1, TILE, UNITS), BF),
            ((256, 1024), BF),
            ((256, 128), BF),
            ((256, 256), BF),
            ((256, 256), BF),
            ((128, 128), BF),
            ((256, 128), BF),
            ((8, 128), F32),
            ((1, 128), F32),
            ((1, 128), F32),
            ((2, ROWS, TILE), F32),
        ],
        in_specs=[pl.BlockSpec(memory_space=pltpu.MemorySpace.HBM)] * 12,
        scratch=[
            pltpu.VMEM((2, BINS, ROWS, TILE), F32),
            pltpu.VMEM((BINS, 256), F32),
            pltpu.VMEM((1, 256), F32),
            pltpu.VMEM((LEVELS * TAPS, 128), F32),
            pltpu.SemaphoreType.DMA((18,)),
        ],
        flops=10**6,
        bytes_accessed=2 * 10**6,
    )(
        *(
            pltpu.with_memory_space_constraint(x, pltpu.MemorySpace.HBM)
            for x in (
                voxels,
                disparity,
                hidden,
                context,
                embed_first,
                embed_bias.reshape(1, -1),
                embed_second,
                motion_weight,
                motion_scale.reshape(1, -1),
                motion_bias.reshape(1, -1),
                jnp.asarray(pool),
                jnp.asarray(lane_rows),
            )
        )
    )
    odd_in = lax.ppermute(odd_out, "col", odd)
    even_in = lax.ppermute(even_out, ("row", "col"), even)
    far_in = lax.ppermute(far, "col", across)
    link_in = lax.ppermute(link_out, ("row", "col"), link)
    chip_in = lax.ppermute(chip_out, "row", chip)
    (mot,) = call(
        motion_kernel,
        [((2, ROWS, EXT, UNITS), BF)],
        flops=10**9,
        bytes_accessed=10**6,
    )(own, odd_in, even_in, far_in, disp, w1, w1t, w2, w2t, mw, scale, bias, pool, lane_rows)
    mot_link = lax.ppermute(mot, ("row", "col"), link)
    mot_chip = lax.ppermute(mot, "row", chip)
    gates, outer, cands, state = call(
        inner_kernel,
        [
            ((2, ROWS, EXT, 2 * UNITS), F32),
            ((2, 2, EXT, UNITS), F32),
            ((2, ROWS, TILE, UNITS), F32),
            ((2, ROWS, EXT, UNITS), BF),
        ],
        flops=10**9,
        bytes_accessed=4 * 10**6,
    )(hidden, context, mot, gate_kernel, candidate_kernel)
    return tuple(
        call(
            outer_kernel,
            [((2, ROWS, TILE, UNITS), BF), ((2, ROWS, TILE), F32)],
            scratch=[
                pltpu.VMEM((2, 2, ROWS + 1, TILE, UNITS), BF),
                pltpu.VMEM((2, 2, ROWS, EXT, UNITS), BF),
            ],
            flops=10**9,
            bytes_accessed=4 * 10**6,
        )(
            hidden,
            context,
            chip_in,
            link_in,
            mot_chip,
            mot_link,
            gates,
            outer,
            cands,
            state,
            gate_kernel,
            candidate_kernel,
            head_weight.reshape(1, -1),
        )
    )


def solution(mesh):
    band = ("pair", "row")
    in_specs = (
        P(None, None, band, "col"),
        P(None, band, "col"),
        P(None, band, "col", None),
        P(None, band, "col", None),
    ) + (P(),) * 9
    out_specs = (P(None, band, "col", None), P(None, band, "col"))
    return jax.shard_map(local, mesh=mesh, in_specs=in_specs, out_specs=out_specs, check_vma=False)
```

time: 27.4 us -> 21.8 us (0.80)
  the two profiles are of different devices: /device:TPU:1 before, /device:TPU:3 now
where the time goes in v4:
time: 21.8 us; the launch traced here: 21.7 us
  starting transfers between devices  9.35 us (43%)
  Pallas kernels  8.23 us (38%)
  waiting for transfers between devices  3.34 us (15%)
  between operations  0.73 us (3%)
    ppermute x1, starting transfers between devices, local(): mot_link = lax.ppermute(mot, ('row', 'col'), link)  3.89 us
    pallas_call x1, Pallas kernels, local(): call(motion_kernel, [((2, ROWS, EXT, UNITS), BF)], flops=10 ** 9, bytes_a...  2.89 us
    pallas_call x1, Pallas kernels, local(): call(outer_kernel, [((2, ROWS, TILE, UNITS), BF), ((2, ROWS, TILE), F32)]...  2.42 us
    ppermute x1, waiting for transfers between devices, local(): mot_link = lax.ppermute(mot, ('row', 'col'), link)  2.38 us
    ppermute x1, starting transfers between devices, local(): even_in = lax.ppermute(even_out, ('row', 'col'), even)  2.12 us
    ppermute x1, starting transfers between devices, local(): link_in = lax.ppermute(link_out, ('row', 'col'), link)  1.75 us
    pallas_call x1, Pallas kernels, local(): call(pack_kernel, [((4, 32, 256), BF), ((80, 256), BF), ((80, 256), BF),...  1.68 us
    pallas_call x1, Pallas kernels, local(): call(inner_kernel, [((2, ROWS, EXT, 2 * UNITS), F32), ((2, 2, EXT, UNITS)...  1.23 us
  transfers between devices with their start and end apart: 7, of which 2 were waited for; matrix products, arithmetic and copies ran while one was open for 0% of the time, Pallas kernels for 19%

profile of v4, /device:TPU:3, one launch (start us, length us, event | category | flops | bytes accessed | tf_op | source)
XLA Modules:
  0.0 21.7 jit_solution(12292311215566288031)
XLA Ops:
  0.6 1.7 %shard_map.158 = (bf16[4,32,256]{2,1,0:T(8,128)(2,1)S(1)}, bf16[80,256]{1,0:T(8,128)(2,1)S(1)}, bf16[80,256]{1,0:T(8,128)(2,1)S(1)}, bf16[64,128]{1,0:T(8,128)(2...) custom-call(f32[2,15,2,160]{3,2,1,0:T(2,128)} %vox_h.1, ...), custom_call_target="tpu_custom_call" | custom-call | flops 1000000 | bytes 2000000 | tf_op jit(solution)/shard_map/pallas_call | solution.py:535
  2.3 0.1 collective-permute-start.2
  2.4 2.1 %collective-permute-start.3 = (bf16[80,256]{1,0:T(8,128)(2,1)S(1)}, bf16[80,256]{1,0:T(8,128)(2,1)S(1)}, u32[]{:S(2)}, u32[]{:S(2)}) collective-permute-start(bf16[80,256]{1,0:T(8,128)(2,1)S(1)} %get-tuple-element.26), channel_id=1, source_target_pairs={{0,4},{1,2},{2,1},{3,7},{4,0},{5,6},{6,5},{7,3},{8,12},{9,10},{10,... | collective-permute-start | bytes 122888 | tf_op jit(solution)/shard_map/ppermute | solution.py:585
  4.5 1.2 %collective-permute-start.4 = (bf16[64,128]{1,0:T(8,128)(2,1)S(1)}, bf16[64,128]{1,0:T(8,128)(2,1)S(1)}, u32[]{:S(2)}, u32[]{:S(2)}) collective-permute-start(bf16[64,128]{1,0:T(8,128)(2,1)S(1)} %get-tuple-element.27), channel_id=1, source_target_pairs={{0,2},{1,3},{2,0},{3,1},{4,6},{5,7},{6,4},{7,5},{8,10},{9,11},{10,... | collective-permute-start | bytes 49160 | tf_op jit(solution)/shard_map/ppermute | solution.py:586
  5.8 0.3 %collective-permute-start = (bf16[2,3,160,128]{3,2,1,0:T(8,128)(2,1)S(1)}, bf16[2,3,160,128]{3,2,1,0:T(8,128)(2,1)S(1)}, u32[]{:S(2)}, u32[]{:S(2)}) collective-permute-start(bf16[2,3,160,128]{3,2,1,0:T(8,128)(2,1)S(1)} %get-tuple-element.22), channel_id=1, source_target_pairs={{0,4},{4,0},{8,12},{12,8},{16,20},{20,16},{24,28},{28,24},{1,5},{5... | collective-permute-start | bytes 737288 | tf_op jit(solution)/shard_map/ppermute | solution.py:588
  6.0 1.8 %collective-permute-start.1 = (bf16[2,3,160,128]{3,2,1,0:T(8,128)(2,1)S(1)}, bf16[2,3,160,128]{3,2,1,0:T(8,128)(2,1)S(1)}, u32[]{:S(2)}, u32[]{:S(2)}) collective-permute-start(bf16[2,3,160,128]{3,2,1,0:T(8,128)(2,1)S(1)} %get-tuple-element.23), channel_id=1, source_target_pairs={{0,1},{1,0},{2,3},{3,2},{4,8},{5,9},{6,10},{7,11},{8,4},{9,5},{10,... | collective-permute-start | bytes 737288 | tf_op jit(solution)/shard_map/ppermute | solution.py:587
  7.8 0.9 %collective-permute-done.4.far_in = bf16[64,128]{1,0:T(8,128)(2,1)S(1)} collective-permute-done((bf16[64,128]{1,0:T(8,128)(2,1)S(1)}, bf16[64,128]{1,0:T(8,128)(2,1)S(1)}, u32[]{:S(2)}, u32[]{:S(2)}) %collective-permute-start.4) | collective-permute-done | bytes 16416 | tf_op jit(solution)/shard_map/ppermute | solution.py:586
  8.7 0.0 collective-permute-done.2.odd_in
  8.7 0.0 collective-permute-done.3.even_in
  8.8 0.0 copy-start.1
  8.8 0.0 copy-start.2
  8.8 0.0 copy-start.3
  8.8 2.9 %shard_map.159.mot = bf16[2,2,192,128]{3,2,1,0:T(8,128)(2,1)S(1)} custom-call(bf16[4,32,256]{2,1,0:T(8,128)(2,1)S(1)} %get-tuple-element.24.own, bf16[80,256]{1,0:T(8,128)(2,1)S(1)} %collective-permute-done.2.odd_in, bf16[80,256]{1,0:T(8,128)(2,1)S(1)} %collective-permute-done.3.even_in, bf16[64,128]{1,0:T(8,128)(2,1)S(1)} %collective-permute-done.4.far_in, ...), custom_call_target="tpu_custom_call" | custom-call | flops 1000000000 | bytes 1000000 | tf_op jit(solution)/shard_map/pallas_call | solution.py:589
  11.7 0.0 copy-start.4
  11.7 3.9 %collective-permute-start.6 = (bf16[2,2,192,128]{3,2,1,0:T(8,128)(2,1)S(1)}, bf16[2,2,192,128]{3,2,1,0:T(8,128)(2,1)S(1)}, u32[]{:S(2)}, u32[]{:S(2)}) collective-permute-start(bf16[2,2,192,128]{3,2,1,0:T(8,128)(2,1)S(1)} %shard_map.159.mot), channel_id=1, source_target_pairs={{0,1},{1,0},{2,3},{3,2},{4,8},{5,9},{6,10},{7,11},{8,4},{9,5},{10,... | collective-permute-start | bytes 589832 | tf_op jit(solution)/shard_map/ppermute | solution.py:595
  15.6 0.0 collective-permute-start.5
  15.6 0.0 copy-done
  15.6 0.0 copy-done.1
  15.6 1.2 %shard_map.160 = (f32[2,2,192,256]{3,2,1,0:T(8,128)S(1)}, f32[2,2,192,128]{3,2,1,0:T(8,128)S(1)}, f32[2,2,160,128]{3,2,1,0:T(8,128)S(1)}, bf16[2,2,192,128]{3,2,1,0:T(8,128)(2,1)S(1)}) custom-call(bf16[2,2,160,128]{3,2,1,0:T(8,128)(2,1)S(1)} %copy-done.2, bf16[2,2,160,384]{3,2,1,0:T(8,128)(2,1)S(1)} %copy-done, bf16[2,2,192,128]{3,2,1,0:T(8,128)(2,1)S(1)} %shard_map.159.mot, ...), custom_call_target="tpu_custom_call" | custom-call | flops 1000000000 | bytes 4000000 | tf_op jit(solution)/shard_map/pallas_call | solution.py:597
  16.9 2.4 %collective-permute-done.6.mot_link = bf16[2,2,192,128]{3,2,1,0:T(8,128)(2,1)S(1)} collective-permute-done((bf16[2,2,192,128]{3,2,1,0:T(8,128)(2,1)S(1)}, bf16[2,2,192,128]{3,2,1,0:T(8,128)(2,1)S(1)}, u32[]{:S(2)}, u32[]{:S(2)}) %collective-permute-start.6) | collective-permute-done | bytes 196640 | tf_op jit(solution)/shard_map/ppermute | solution.py:595
  19.2 0.0 collective-permute-done.5.mot_chip
  19.2 0.0 collective-permute-done.chip_in
  19.2 0.0 collective-permute-done.1.link_in
  19.3 2.4 %shard_map.161 = (bf16[2,2,160,128]{3,2,1,0:T(8,128)(2,1)}, f32[2,2,160]{2,1,0:T(2,128)}) custom-call(bf16[2,2,160,128]{3,2,1,0:T(8,128)(2,1)S(1)} %copy-done.2, bf16[2,2,160,384]{3,2,1,0:T(8,128)(2,1)S(1)} %copy-done, bf16[2,3,160,128]{3,2,1,0:T(8,128)(2,1)S(1)} %collective-permute-done.chip_in, ...), custom_call_target="tpu_custom_call" | custom-call | flops 1000000000 | bytes 4000000 | tf_op jit(solution)/shard_map/pallas_call | solution.py:609
  (4 shorter events, 0.0 us)
Async XLA Ops:
  2.3 6.4 %collective-permute-start.2 = (bf16[80,256]{1,0:T(8,128)(2,1)S(1)}, bf16[80,256]{1,0:T(8,128)(2,1)S(1)}, u32[]{:S(2)}, u32[]{:S(2)}) collective-permute-start(bf16[80,256]{1,0:T(8,128)(2,1)S(1)} %get-tuple-element.25), channel_id=1, source_target_pairs={{0,1},{1,0},{2,3},{3,2},{4,5},{5,4},{6,7},{7,6},{8,9},{9,8},{10,11... | collective-permute-start | bytes 122888 | tf_op jit(solution)/shard_map/ppermute | solution.py:584
  2.4 6.3 %collective-permute-start.3 = (bf16[80,256]{1,0:T(8,128)(2,1)S(1)}, bf16[80,256]{1,0:T(8,128)(2,1)S(1)}, u32[]{:S(2)}, u32[]{:S(2)}) collective-permute-start(bf16[80,256]{1,0:T(8,128)(2,1)S(1)} %get-tuple-element.26), channel_id=1, source_target_pairs={{0,4},{1,2},{2,1},{3,7},{4,0},{5,6},{6,5},{7,3},{8,12},{9,10},{10,... | collective-permute-start | bytes 122888 | tf_op jit(solution)/shard_map/ppermute | solution.py:585
  4.5 4.2 %collective-permute-start.4 = (bf16[64,128]{1,0:T(8,128)(2,1)S(1)}, bf16[64,128]{1,0:T(8,128)(2,1)S(1)}, u32[]{:S(2)}, u32[]{:S(2)}) collective-permute-start(bf16[64,128]{1,0:T(8,128)(2,1)S(1)} %get-tuple-element.27), channel_id=1, source_target_pairs={{0,2},{1,3},{2,0},{3,1},{4,6},{5,7},{6,4},{7,5},{8,10},{9,11},{10,... | collective-permute-start | bytes 49160 | tf_op jit(solution)/shard_map/ppermute | solution.py:586
  5.8 13.5 %collective-permute-start = (bf16[2,3,160,128]{3,2,1,0:T(8,128)(2,1)S(1)}, bf16[2,3,160,128]{3,2,1,0:T(8,128)(2,1)S(1)}, u32[]{:S(2)}, u32[]{:S(2)}) collective-permute-start(bf16[2,3,160,128]{3,2,1,0:T(8,128)(2,1)S(1)} %get-tuple-element.22), channel_id=1, source_target_pairs={{0,4},{4,0},{8,12},{12,8},{16,20},{20,16},{24,28},{28,24},{1,5},{5... | collective-permute-start | bytes 737288 | tf_op jit(solution)/shard_map/ppermute | solution.py:588
  6.0 13.2 %collective-permute-start.1 = (bf16[2,3,160,128]{3,2,1,0:T(8,128)(2,1)S(1)}, bf16[2,3,160,128]{3,2,1,0:T(8,128)(2,1)S(1)}, u32[]{:S(2)}, u32[]{:S(2)}) collective-permute-start(bf16[2,3,160,128]{3,2,1,0:T(8,128)(2,1)S(1)} %get-tuple-element.23), channel_id=1, source_target_pairs={{0,1},{1,0},{2,3},{3,2},{4,8},{5,9},{6,10},{7,11},{8,4},{9,5},{10,... | collective-permute-start | bytes 737288 | tf_op jit(solution)/shard_map/ppermute | solution.py:587
  8.7 6.8 %copy-start = (bf16[2,2,160,384]{3,2,1,0:T(8,128)(2,1)S(1)}, bf16[2,2,160,384]{3,2,1,0:T(8,128)(2,1)}, u32[]{:S(2)}) copy-start(bf16[2,2,160,384]{3,2,1,0:T(8,128)(2,1)} %context.3) | copy-start | bytes 1474564
  8.8 6.8 %copy-start.1 = (bf16[3,3,256,256]{3,2,1,0:T(8,128)(2,1)S(1)}, bf16[3,3,256,256]{3,2,1,0:T(8,128)(2,1)}, u32[]{:S(2)}) copy-start(bf16[3,3,256,256]{3,2,1,0:T(8,128)(2,1)} %gate_k.3) | copy-start | bytes 3538948
  8.8 6.8 %copy-start.2 = (bf16[2,2,160,128]{3,2,1,0:T(8,128)(2,1)S(1)}, bf16[2,2,160,128]{3,2,1,0:T(8,128)(2,1)}, u32[]{:S(2)}) copy-start(bf16[2,2,160,128]{3,2,1,0:T(8,128)(2,1)} %hidden.3) | copy-start | bytes 491524
  8.8 6.8 %copy-start.3 = (bf16[3,3,256,128]{3,2,1,0:T(8,128)(2,1)S(1)}, bf16[3,3,256,128]{3,2,1,0:T(8,128)(2,1)}, u32[]{:S(2)}) copy-start(bf16[3,3,256,128]{3,2,1,0:T(8,128)(2,1)} %cand_k.3) | copy-start | bytes 1769476
  11.7 7.6 %copy-start.4 = (bf16[128]{0:T(256)(128)(2,1)S(1)}, bf16[128]{0:T(256)(128)(2,1)}, u32[]{:S(2)}) copy-start(bf16[128]{0:T(256)(128)(2,1)} %param.27) | copy-start | bytes 772
  11.7 7.5 %collective-permute-start.6 = (bf16[2,2,192,128]{3,2,1,0:T(8,128)(2,1)S(1)}, bf16[2,2,192,128]{3,2,1,0:T(8,128)(2,1)S(1)}, u32[]{:S(2)}, u32[]{:S(2)}) collective-permute-start(bf16[2,2,192,128]{3,2,1,0:T(8,128)(2,1)S(1)} %shard_map.159.mot), channel_id=1, source_target_pairs={{0,1},{1,0},{2,3},{3,2},{4,8},{5,9},{6,10},{7,11},{8,4},{9,5},{10,... | collective-permute-start | bytes 589832 | tf_op jit(solution)/shard_map/ppermute | solution.py:595
  15.6 3.7 %collective-permute-start.5 = (bf16[2,2,192,128]{3,2,1,0:T(8,128)(2,1)S(1)}, bf16[2,2,192,128]{3,2,1,0:T(8,128)(2,1)S(1)}, u32[]{:S(2)}, u32[]{:S(2)}) collective-permute-start(bf16[2,2,192,128]{3,2,1,0:T(8,128)(2,1)S(1)} %shard_map.159.mot), channel_id=1, source_target_pairs={{0,4},{4,0},{8,12},{12,8},{16,20},{20,16},{24,28},{28,24},{1,5},{5... | collective-permute-start | bytes 589832 | tf_op jit(solution)/shard_map/ppermute | solution.py:596

commit v5 on v4

--- a/solution.py
+++ b/solution.py
@@ -28,14 +28,18 @@
 
 
 def tables():
-    pool = np.zeros((128, 128), np.float32)
+    pool = np.zeros((128, 256), np.float32)
     firsts = (28, 12, 4, 0)
     counts = (17, 13, 11, 10)
     for level in range(LEVELS):
         width = 2**level
         for k in range(counts[level]):
             entry = firsts[level] + k
-            pool[entry * width : (entry + 1) * width, STARTS[level] + k] = 1.0 / (16 * width)
+            weight = 1.0 / (16 * width)
+            pool[entry * width : (entry + 1) * width, STARTS[level] + k] = weight
+            pool[entry * width : (entry + 1) * width, 128 + STARTS[level] + k] = -weight
+            if k:
+                pool[entry * width : (entry + 1) * width, 127 + STARTS[level] + k] = weight
     lane = np.arange(128)
     member = lane % GROUP
     used = (member < LEVELS * TAPS) & (lane < 3 * GROUP)
@@ -45,6 +49,8 @@
     low = ((lane >= GROUP) & (lane < 2 * GROUP)).astype(np.float32)
     rows = np.zeros((8, 128), np.float32)
     rows[0], rows[1], rows[2] = first, scale, low
+    for level in range(LEVELS):
+        rows[3, STARTS[level] : STARTS[level] + counts[level]] = 0.5**level
     return np.concatenate([pool, pool]).astype(jnp.bfloat16), rows
 
 
@@ -80,20 +86,16 @@
     far,
     chip,
     link,
-    w1,
-    w1t,
+    first,
+    bias,
     w2,
-    w2t,
-    mw,
+    motion,
     pool,
     rows,
     scale,
     mbias,
     disp,
     vox,
-    first,
-    bias,
-    motion,
     sems,
 ):
     row_odd = lax.axis_index("row") % 2
@@ -118,13 +120,16 @@
     copies = [pltpu.make_async_copy(a, b, sems.at[k]) for k, (a, b) in enumerate(pairs)]
     for copy in copies:
         copy.start()
-    for copy in copies[:data]:
+    for copy in copies[:2]:
         copy.wait()
     col = lax.axis_index("col")
     is_even = col % 2 == 0
-    row_at = lax.broadcasted_iota(jnp.int32, (8, 128), 0)
+
+    def emit(at, to_right, to_left):
+        odd_out[at, :] = jnp.where(is_even, to_right, to_left).astype(BF)
+        even_out[at, :] = jnp.where(is_even, to_left, to_right).astype(BF)
+
     parts = []
-    edges_right, edges_left = [], []
     for v in range(2):
         for y in range(ROWS):
             high, low = split(vox[v, :, y, :])
@@ -134,34 +139,6 @@
             own[2 * v + y] = jnp.concatenate(
                 [block, jnp.zeros((32, 256 - TILE), F32)], axis=1
             ).astype(BF)
-
-            def context_at(at):
-                on_chip, on_link = chip[v, ROWS, at].astype(F32), link[v, ROWS, at].astype(F32)
-                return jnp.where(row_odd == y, on_link, on_chip)
-
-            hid_last = pltpu.roll(chip[v, y, 144:160, :].astype(F32)[8:16], 2, 0)
-            con_last = pltpu.roll(context_at(slice(144, 160))[8:16], 3, 0)
-            hid_first = chip[v, y, 0:16, :].astype(F32)[0:8]
-            con_first = pltpu.roll(context_at(slice(0, 16))[0:8], 2, 0)
-            depth = disp[v, y : y + 1, :]
-            d_last = pltpu.roll(jnp.broadcast_to(depth[:, 32:160], (8, 128)), 8, 1)
-            d_first = jnp.broadcast_to(depth[:, 0:128], (8, 128))
-
-            def edge(hid, con, dis):
-                d_high, rest = split(dis)
-                d_mid, d_low = split(rest)
-                out = jnp.where(row_at < 2, hid, con)
-                out = jnp.where(row_at == 3, d_high, out)
-                out = jnp.where(row_at == 4, d_mid, out)
-                return jnp.where(row_at >= 5, d_low, out)
-
-            edges_right.append(edge(hid_last, con_last, d_last))
-            edges_left.append(edge(hid_first, con_first, d_first))
-
-    def emit(at, to_right, to_left):
-        odd_out[at, :] = jnp.where(is_even, to_right, to_left).astype(BF)
-        even_out[at, :] = jnp.where(is_even, to_left, to_right).astype(BF)
-
     blank = jnp.zeros((32, 256 - TILE - NEAR), F32)
     for y in range(ROWS):
         f0, f1 = parts[y], parts[ROWS + y]
@@ -174,6 +151,36 @@
         tail = jnp.concatenate([f1[:, TILE - FAR :], jnp.zeros((32, 128 - FAR), F32)], axis=1)
         far[rows_at, :] = jnp.where(col < 2, tail, f0[:, :128]).astype(BF)
 
+    for copy in copies[2:data]:
+        copy.wait()
+    row_at = lax.broadcasted_iota(jnp.int32, (8, 128), 0)
+    edges_right, edges_left = [], []
+    for v in range(2):
+        for y in range(ROWS):
+
+            def context_at(at):
+                on_chip, on_link = chip[v, ROWS, at].astype(F32), link[v, ROWS, at].astype(F32)
+                return jnp.where(row_odd == y, on_link, on_chip)
+
+            hid_last = pltpu.roll(chip[v, y, 144:160, :].astype(F32)[8:16], 2, 0)
+            con_last = pltpu.roll(context_at(slice(144, 160))[8:16], 3, 0)
+            hid_first = chip[v, y, 0:16, :].astype(F32)[0:8]
+            con_first = pltpu.roll(context_at(slice(0, 16))[0:8], 2, 0)
+            depth = disp[v, y : y + 1, :]
+            d_last = pltpu.roll(jnp.broadcast_to(depth[:, 32:160], (8, 128)), 8, 1)
+            d_first = jnp.broadcast_to(depth[:, 0:128], (8, 128))
+
+            def edge(hid, con, dis):
+                d_high, rest = split(dis)
+                d_mid, d_low = split(rest)
+                out = jnp.where(row_at < 2, hid, con)
+                out = jnp.where(row_at == 3, d_high, out)
+                out = jnp.where(row_at == 4, d_mid, out)
+                return jnp.where(row_at >= 5, d_low, out)
+
+            edges_right.append(edge(hid_last, con_last, d_last))
+            edges_left.append(edge(hid_first, con_first, d_first))
+
     def gathered(edges):
         return jnp.concatenate(
             [
@@ -186,6 +193,9 @@
     emit(pl.ds(64, 16), gathered(edges_right), gathered(edges_left))
     for copy in copies[data:]:
         copy.wait()
+
+
+def weight_kernel(first, bias, w2, motion, w1, w1t, w2t, mw):
     w_high, w_low = split(first[...] * 0.5)
     b_high, rest = split(bias[...] * 0.5)
     b_mid, b_low = split(rest)
@@ -288,6 +298,7 @@
     first = rows[0:1, :].astype(jnp.int32)
     level_scale = rows[1:2, :]
     is_low = rows[2:3, :] > 0.5
+    entry_scale = rows[3:4, :]
     lane = lax.broadcasted_iota(jnp.int32, (EXT, 128), 1)
     pixel = lax.broadcasted_iota(jnp.int32, (EXT, 1), 0)
     column = pixel + (col * TILE - PAD)
@@ -306,26 +317,25 @@
         eighth = jnp.floor(spot * 0.125)
         rests.append(spot - 8.0 * eighth)
         start = (8.0 * eighth).astype(jnp.int32) + (FAR + TILE - 32)
-        index = start + lane if v == 0 else (LAST - start) - lane
-        block, place = index >> 7, index & 127
-        near = jnp.zeros((EXT, 128), F32)
-        for m in range(WINDOW // 128):
-            taken = jnp.take_along_axis(
-                scores[:, 128 * m : 128 * m + 128], place, axis=1, mode="promise_in_bounds"
-            )
-            near = jnp.where(block == m, taken, near)
+        if v == 0:
+            block, place = (start + 127 - lane) >> 7, (start + lane) & 127
+        else:
+            index = (LAST - start) - lane
+            block, place = index >> 7, index & 127
+        source = scores[:, :128]
+        for m in range(1, WINDOW // 128):
+            source = jnp.where(block == m, scores[:, 128 * m : 128 * m + 128], source)
+        near = jnp.take_along_axis(source, place, axis=1, mode="promise_in_bounds")
         high, low = split(near)
         nears.append(jnp.concatenate([high.astype(BF), low.astype(BF)], axis=1))
     pooled = jnp.dot(jnp.concatenate(nears, axis=0), pool[...], preferred_element_type=F32)
     looks = []
     for k in range(4):
         table = pooled[EXT * k : EXT * k + EXT]
-        at = rests[k] * level_scale
-        floor = jnp.floor(at)
-        index = floor.astype(jnp.int32) + first
-        lower = jnp.take_along_axis(table, index, axis=1, mode="promise_in_bounds")
-        upper = jnp.take_along_axis(table, index + 1, axis=1, mode="promise_in_bounds")
-        high, low = split(lower + (at - floor) * (upper - lower))
+        at = rests[k] * entry_scale
+        table = table[:, :128] + (at - jnp.floor(at)) * table[:, 128:]
+        index = jnp.floor(rests[k] * level_scale).astype(jnp.int32) + first
+        high, low = split(jnp.take_along_axis(table, index, axis=1, mode="promise_in_bounds"))
         looks.append(jnp.where(is_low, low, high).astype(BF))
     sums = jnp.dot(jnp.concatenate(looks, axis=0), mw[...], preferred_element_type=F32)
     for k, (v, y) in enumerate(cases):
@@ -484,10 +494,10 @@
             candidate = jnp.tanh(terms[v][PAD : PAD + TILE] + cands[v, y])
             old = hidden[v, y].astype(F32)
             update = updates[y][v]
-            fresh = ((1.0 - update) * old + update * candidate).astype(BF)
-            new[v, y] = fresh
+            new[v, y] = ((1.0 - update) * old + update * candidate).astype(BF)
+        for v in range(2):
             inc[v, y : y + 1, :] = lax.dot_general(
-                head_rows, fresh, (((1,), (1,)), ((), ())), preferred_element_type=F32
+                head_rows, new[v, y], (((1,), (1,)), ((), ())), preferred_element_type=F32
             )[0:1]
 
 
@@ -532,7 +542,7 @@
 
     pool, lane_rows = tables()
 
-    (own, odd_out, even_out, far, chip_out, link_out, w1, w1t, w2, w2t, mw, pool, lane_rows, scale, bias, disp) = call(
+    (own, odd_out, even_out, far, chip_out, link_out, *raw, pool, lane_rows, scale, bias, disp) = call(
         pack_kernel,
         [
             ((4, 32, 256), BF),
@@ -541,12 +551,11 @@
             ((64, 128), BF),
             ((2, ROWS + 1, TILE, UNITS), BF),
             ((2, ROWS + 1, TILE, UNITS), BF),
-            ((256, 1024), BF),
-            ((256, 128), BF),
+            ((BINS, 256), F32),
+            ((1, 256), F32),
             ((256, 256), BF),
+            ((LEVELS * TAPS, 128), F32),
             ((256, 256), BF),
-            ((128, 128), BF),
-            ((256, 128), BF),
             ((8, 128), F32),
             ((1, 128), F32),
             ((1, 128), F32),
@@ -555,9 +564,6 @@
         in_specs=[pl.BlockSpec(memory_space=pltpu.MemorySpace.HBM)] * 12,
         scratch=[
             pltpu.VMEM((2, BINS, ROWS, TILE), F32),
-            pltpu.VMEM((BINS, 256), F32),
-            pltpu.VMEM((1, 256), F32),
-            pltpu.VMEM((LEVELS * TAPS, 128), F32),
             pltpu.SemaphoreType.DMA((18,)),
         ],
         flops=10**6,
@@ -581,11 +587,18 @@
             )
         )
     )
+    far_in = lax.ppermute(far, "col", across)
     odd_in = lax.ppermute(odd_out, "col", odd)
     even_in = lax.ppermute(even_out, ("row", "col"), even)
-    far_in = lax.ppermute(far, "col", across)
     link_in = lax.ppermute(link_out, ("row", "col"), link)
     chip_in = lax.ppermute(chip_out, "row", chip)
+    w1, w1t, w2t, mw = call(
+        weight_kernel,
+        [((256, 1024), BF), ((256, 128), BF), ((256, 256), BF), ((128, 128), BF)],
+        flops=10**6,
+        bytes_accessed=2 * 10**6,
+    )(*raw)
+    w2 = raw[2]
     (mot,) = call(
         motion_kernel,
         [((2, ROWS, EXT, UNITS), BF)],

time: 21.8 us -> 20.9 us (0.959)
  the two profiles are of different devices: /device:TPU:3 before, /device:TPU:11 now
where the time goes in v5:
time: 20.9 us; the launch traced here: 20.8 us
  starting transfers between devices  9.47 us (45%)
  Pallas kernels  7.51 us (36%)
  waiting for transfers between devices  3.06 us (15%)
  between operations  0.73 us (3%)
    ppermute x1, starting transfers between devices, local(): mot_link = lax.ppermute(mot, ('row', 'col'), link)  4 us
    pallas_call x1, Pallas kernels, local(): call(outer_kernel, [((2, ROWS, TILE, UNITS), BF), ((2, ROWS, TILE), F32)]...  2.51 us
    ppermute x1, waiting for transfers between devices, local(): mot_link = lax.ppermute(mot, ('row', 'col'), link)  2.37 us
    pallas_call x1, Pallas kernels, local(): call(motion_kernel, [((2, ROWS, EXT, UNITS), BF)], flops=10 ** 9, bytes_a...  2.13 us
    ppermute x1, starting transfers between devices, local(): even_in = lax.ppermute(even_out, ('row', 'col'), even)  1.87 us
    ppermute x1, starting transfers between devices, local(): link_in = lax.ppermute(link_out, ('row', 'col'), link)  1.75 us
    pallas_call x1, Pallas kernels, local(): call(pack_kernel, [((4, 32, 256), BF), ((80, 256), BF), ((80, 256), BF),...  1.46 us
    pallas_call x1, Pallas kernels, local(): call(inner_kernel, [((2, ROWS, EXT, 2 * UNITS), F32), ((2, 2, EXT, UNITS)...  1.24 us
  transfers between devices with their start and end apart: 7, of which 2 were waited for; matrix products, arithmetic and copies ran while one was open for 0% of the time, Pallas kernels for 17%

profile of v5, /device:TPU:11, one launch (start us, length us, event | category | flops | bytes accessed | tf_op | source)
XLA Modules:
  0.0 20.8 jit_solution(14487034155454938393)
XLA Ops:
  0.6 1.5 %shard_map.158 = (bf16[4,32,256]{2,1,0:T(8,128)(2,1)S(1)}, bf16[80,256]{1,0:T(8,128)(2,1)S(1)}, bf16[80,256]{1,0:T(8,128)(2,1)S(1)}, bf16[64,128]{1,0:T(8,128)(2...) custom-call(f32[2,15,2,160]{3,2,1,0:T(2,128)} %vox_h.1, ...), custom_call_target="tpu_custom_call" | custom-call | flops 1000000 | bytes 2000000 | tf_op jit(solution)/shard_map/pallas_call | solution.py:545
  2.1 0.3 %collective-permute-start.2 = (bf16[80,256]{1,0:T(8,128)(2,1)S(1)}, bf16[80,256]{1,0:T(8,128)(2,1)S(1)}, u32[]{:S(2)}, u32[]{:S(2)}) collective-permute-start(bf16[80,256]{1,0:T(8,128)(2,1)S(1)} %get-tuple-element.28), channel_id=1, source_target_pairs={{0,1},{1,0},{2,3},{3,2},{4,5},{5,4},{6,7},{7,6},{8,9},{9,8},{10,11... | collective-permute-start | bytes 122888 | tf_op jit(solution)/shard_map/ppermute | solution.py:591
  2.4 1.9 %collective-permute-start.3 = (bf16[80,256]{1,0:T(8,128)(2,1)S(1)}, bf16[80,256]{1,0:T(8,128)(2,1)S(1)}, u32[]{:S(2)}, u32[]{:S(2)}) collective-permute-start(bf16[80,256]{1,0:T(8,128)(2,1)S(1)} %get-tuple-element.29), channel_id=1, source_target_pairs={{0,4},{1,2},{2,1},{3,7},{4,0},{5,6},{6,5},{7,3},{8,12},{9,10},{10,... | collective-permute-start | bytes 122888 | tf_op jit(solution)/shard_map/ppermute | solution.py:592
  4.3 1.2 %collective-permute-start.4 = (bf16[64,128]{1,0:T(8,128)(2,1)S(1)}, bf16[64,128]{1,0:T(8,128)(2,1)S(1)}, u32[]{:S(2)}, u32[]{:S(2)}) collective-permute-start(bf16[64,128]{1,0:T(8,128)(2,1)S(1)} %get-tuple-element.30), channel_id=1, source_target_pairs={{0,2},{1,3},{2,0},{3,1},{4,6},{5,7},{6,4},{7,5},{8,10},{9,11},{10,... | collective-permute-start | bytes 49160 | tf_op jit(solution)/shard_map/ppermute | solution.py:590
  5.5 0.3 %collective-permute-start = (bf16[2,3,160,128]{3,2,1,0:T(8,128)(2,1)S(1)}, bf16[2,3,160,128]{3,2,1,0:T(8,128)(2,1)S(1)}, u32[]{:S(2)}, u32[]{:S(2)}) collective-permute-start(bf16[2,3,160,128]{3,2,1,0:T(8,128)(2,1)S(1)} %get-tuple-element.25), channel_id=1, source_target_pairs={{0,4},{4,0},{8,12},{12,8},{16,20},{20,16},{24,28},{28,24},{1,5},{5... | collective-permute-start | bytes 737288 | tf_op jit(solution)/shard_map/ppermute | solution.py:594
  5.8 1.8 %collective-permute-start.1 = (bf16[2,3,160,128]{3,2,1,0:T(8,128)(2,1)S(1)}, bf16[2,3,160,128]{3,2,1,0:T(8,128)(2,1)S(1)}, u32[]{:S(2)}, u32[]{:S(2)}) collective-permute-start(bf16[2,3,160,128]{3,2,1,0:T(8,128)(2,1)S(1)} %get-tuple-element.26), channel_id=1, source_target_pairs={{0,1},{1,0},{2,3},{3,2},{4,8},{5,9},{6,10},{7,11},{8,4},{9,5},{10,... | collective-permute-start | bytes 737288 | tf_op jit(solution)/shard_map/ppermute | solution.py:593
  7.6 0.2 shard_map.159
  7.7 0.7 %collective-permute-done.4.far_in = bf16[64,128]{1,0:T(8,128)(2,1)S(1)} collective-permute-done((bf16[64,128]{1,0:T(8,128)(2,1)S(1)}, bf16[64,128]{1,0:T(8,128)(2,1)S(1)}, u32[]{:S(2)}, u32[]{:S(2)}) %collective-permute-start.4) | collective-permute-done | bytes 16416 | tf_op jit(solution)/shard_map/ppermute | solution.py:590
  8.4 0.0 collective-permute-done.2.odd_in
  8.4 0.0 collective-permute-done.3.even_in
  8.4 0.0 copy-start.1
  8.4 0.0 copy-start.2
  8.4 0.0 copy-start.3
  8.5 2.1 %shard_map.160.mot = bf16[2,2,192,128]{3,2,1,0:T(8,128)(2,1)S(1)} custom-call(bf16[4,32,256]{2,1,0:T(8,128)(2,1)S(1)} %get-tuple-element.27.own, bf16[80,256]{1,0:T(8,128)(2,1)S(1)} %collective-permute-done.2.odd_in, bf16[80,256]{1,0:T(8,128)(2,1)S(1)} %collective-permute-done.3.even_in, bf16[64,128]{1,0:T(8,128)(2,1)S(1)} %collective-permute-done.4.far_in, ...), custom_call_target="tpu_custom_call" | custom-call | flops 1000000000 | bytes 1000000 | tf_op jit(solution)/shard_map/pallas_call | solution.py:602
  10.6 0.0 copy-start.4
  10.6 4.0 %collective-permute-start.6 = (bf16[2,2,192,128]{3,2,1,0:T(8,128)(2,1)S(1)}, bf16[2,2,192,128]{3,2,1,0:T(8,128)(2,1)S(1)}, u32[]{:S(2)}, u32[]{:S(2)}) collective-permute-start(bf16[2,2,192,128]{3,2,1,0:T(8,128)(2,1)S(1)} %shard_map.160.mot), channel_id=1, source_target_pairs={{0,1},{1,0},{2,3},{3,2},{4,8},{5,9},{6,10},{7,11},{8,4},{9,5},{10,... | collective-permute-start | bytes 589832 | tf_op jit(solution)/shard_map/ppermute | solution.py:608
  14.6 0.0 collective-permute-start.5
  14.6 0.0 copy-done
  14.6 1.2 %shard_map.161 = (f32[2,2,192,256]{3,2,1,0:T(8,128)S(1)}, f32[2,2,192,128]{3,2,1,0:T(8,128)S(1)}, f32[2,2,160,128]{3,2,1,0:T(8,128)S(1)}, bf16[2,2,192,128]{3,2,1,0:T(8,128)(2,1)S(1)}) custom-call(bf16[2,2,160,128]{3,2,1,0:T(8,128)(2,1)S(1)} %copy-done.2, bf16[2,2,160,384]{3,2,1,0:T(8,128)(2,1)S(1)} %copy-done, bf16[2,2,192,128]{3,2,1,0:T(8,128)(2,1)S(1)} %shard_map.160.mot, ...), custom_call_target="tpu_custom_call" | custom-call | flops 1000000000 | bytes 4000000 | tf_op jit(solution)/shard_map/pallas_call | solution.py:610
  15.9 2.4 %collective-permute-done.6.mot_link = bf16[2,2,192,128]{3,2,1,0:T(8,128)(2,1)S(1)} collective-permute-done((bf16[2,2,192,128]{3,2,1,0:T(8,128)(2,1)S(1)}, bf16[2,2,192,128]{3,2,1,0:T(8,128)(2,1)S(1)}, u32[]{:S(2)}, u32[]{:S(2)}) %collective-permute-start.6) | collective-permute-done | bytes 196640 | tf_op jit(solution)/shard_map/ppermute | solution.py:608
  18.3 0.0 collective-permute-done.5.mot_chip
  18.3 0.0 collective-permute-done.chip_in
  18.3 0.0 collective-permute-done.1.link_in
  18.3 2.5 %shard_map.162 = (bf16[2,2,160,128]{3,2,1,0:T(8,128)(2,1)}, f32[2,2,160]{2,1,0:T(2,128)}) custom-call(bf16[2,2,160,128]{3,2,1,0:T(8,128)(2,1)S(1)} %copy-done.2, bf16[2,2,160,384]{3,2,1,0:T(8,128)(2,1)S(1)} %copy-done, bf16[2,3,160,128]{3,2,1,0:T(8,128)(2,1)S(1)} %collective-permute-done.chip_in, ...), custom_call_target="tpu_custom_call" | custom-call | flops 1000000000 | bytes 4000000 | tf_op jit(solution)/shard_map/pallas_call | solution.py:622
  (5 shorter events, 0.0 us)
Async XLA Ops:
  2.1 6.3 %collective-permute-start.2 = (bf16[80,256]{1,0:T(8,128)(2,1)S(1)}, bf16[80,256]{1,0:T(8,128)(2,1)S(1)}, u32[]{:S(2)}, u32[]{:S(2)}) collective-permute-start(bf16[80,256]{1,0:T(8,128)(2,1)S(1)} %get-tuple-element.28), channel_id=1, source_target_pairs={{0,1},{1,0},{2,3},{3,2},{4,5},{5,4},{6,7},{7,6},{8,9},{9,8},{10,11... | collective-permute-start | bytes 122888 | tf_op jit(solution)/shard_map/ppermute | solution.py:591
  2.4 6.0 %collective-permute-start.3 = (bf16[80,256]{1,0:T(8,128)(2,1)S(1)}, bf16[80,256]{1,0:T(8,128)(2,1)S(1)}, u32[]{:S(2)}, u32[]{:S(2)}) collective-permute-start(bf16[80,256]{1,0:T(8,128)(2,1)S(1)} %get-tuple-element.29), channel_id=1, source_target_pairs={{0,4},{1,2},{2,1},{3,7},{4,0},{5,6},{6,5},{7,3},{8,12},{9,10},{10,... | collective-permute-start | bytes 122888 | tf_op jit(solution)/shard_map/ppermute | solution.py:592
  4.3 4.1 %collective-permute-start.4 = (bf16[64,128]{1,0:T(8,128)(2,1)S(1)}, bf16[64,128]{1,0:T(8,128)(2,1)S(1)}, u32[]{:S(2)}, u32[]{:S(2)}) collective-permute-start(bf16[64,128]{1,0:T(8,128)(2,1)S(1)} %get-tuple-element.30), channel_id=1, source_target_pairs={{0,2},{1,3},{2,0},{3,1},{4,6},{5,7},{6,4},{7,5},{8,10},{9,11},{10,... | collective-permute-start | bytes 49160 | tf_op jit(solution)/shard_map/ppermute | solution.py:590
  5.5 12.7 %collective-permute-start = (bf16[2,3,160,128]{3,2,1,0:T(8,128)(2,1)S(1)}, bf16[2,3,160,128]{3,2,1,0:T(8,128)(2,1)S(1)}, u32[]{:S(2)}, u32[]{:S(2)}) collective-permute-start(bf16[2,3,160,128]{3,2,1,0:T(8,128)(2,1)S(1)} %get-tuple-element.25), channel_id=1, source_target_pairs={{0,4},{4,0},{8,12},{12,8},{16,20},{20,16},{24,28},{28,24},{1,5},{5... | collective-permute-start | bytes 737288 | tf_op jit(solution)/shard_map/ppermute | solution.py:594
  5.8 12.4 %collective-permute-start.1 = (bf16[2,3,160,128]{3,2,1,0:T(8,128)(2,1)S(1)}, bf16[2,3,160,128]{3,2,1,0:T(8,128)(2,1)S(1)}, u32[]{:S(2)}, u32[]{:S(2)}) collective-permute-start(bf16[2,3,160,128]{3,2,1,0:T(8,128)(2,1)S(1)} %get-tuple-element.26), channel_id=1, source_target_pairs={{0,1},{1,0},{2,3},{3,2},{4,8},{5,9},{6,10},{7,11},{8,4},{9,5},{10,... | collective-permute-start | bytes 737288 | tf_op jit(solution)/shard_map/ppermute | solution.py:593
  8.4 6.2 %copy-start = (bf16[2,2,160,384]{3,2,1,0:T(8,128)(2,1)S(1)}, bf16[2,2,160,384]{3,2,1,0:T(8,128)(2,1)}, u32[]{:S(2)}) copy-start(bf16[2,2,160,384]{3,2,1,0:T(8,128)(2,1)} %context.3) | copy-start | bytes 1474564
  8.4 6.2 %copy-start.1 = (bf16[3,3,256,256]{3,2,1,0:T(8,128)(2,1)S(1)}, bf16[3,3,256,256]{3,2,1,0:T(8,128)(2,1)}, u32[]{:S(2)}) copy-start(bf16[3,3,256,256]{3,2,1,0:T(8,128)(2,1)} %gate_k.3) | copy-start | bytes 3538948
  8.4 6.2 %copy-start.2 = (bf16[2,2,160,128]{3,2,1,0:T(8,128)(2,1)S(1)}, bf16[2,2,160,128]{3,2,1,0:T(8,128)(2,1)}, u32[]{:S(2)}) copy-start(bf16[2,2,160,128]{3,2,1,0:T(8,128)(2,1)} %hidden.3) | copy-start | bytes 491524
  8.4 6.2 %copy-start.3 = (bf16[3,3,256,128]{3,2,1,0:T(8,128)(2,1)S(1)}, bf16[3,3,256,128]{3,2,1,0:T(8,128)(2,1)}, u32[]{:S(2)}) copy-start(bf16[3,3,256,128]{3,2,1,0:T(8,128)(2,1)} %cand_k.3) | copy-start | bytes 1769476
  10.6 7.7 %copy-start.4 = (bf16[128]{0:T(256)(128)(2,1)S(1)}, bf16[128]{0:T(256)(128)(2,1)}, u32[]{:S(2)}) copy-start(bf16[128]{0:T(256)(128)(2,1)} %param.27) | copy-start | bytes 772
  10.6 7.6 %collective-permute-start.6 = (bf16[2,2,192,128]{3,2,1,0:T(8,128)(2,1)S(1)}, bf16[2,2,192,128]{3,2,1,0:T(8,128)(2,1)S(1)}, u32[]{:S(2)}, u32[]{:S(2)}) collective-permute-start(bf16[2,2,192,128]{3,2,1,0:T(8,128)(2,1)S(1)} %shard_map.160.mot), channel_id=1, source_target_pairs={{0,1},{1,0},{2,3},{3,2},{4,8},{5,9},{6,10},{7,11},{8,4},{9,5},{10,... | collective-permute-start | bytes 589832 | tf_op jit(solution)/shard_map/ppermute | solution.py:608
  14.6 3.7 %collective-permute-start.5 = (bf16[2,2,192,128]{3,2,1,0:T(8,128)(2,1)S(1)}, bf16[2,2,192,128]{3,2,1,0:T(8,128)(2,1)S(1)}, u32[]{:S(2)}, u32[]{:S(2)}) collective-permute-start(bf16[2,2,192,128]{3,2,1,0:T(8,128)(2,1)S(1)} %shard_map.160.mot), channel_id=1, source_target_pairs={{0,4},{4,0},{8,12},{12,8},{16,20},{20,16},{24,28},{28,24},{1,5},{5... | collective-permute-start | bytes 589832 | tf_op jit(solution)/shard_map/ppermute | solution.py:609

commit v6 on v5

--- a/solution.py
+++ b/solution.py
@@ -12,7 +12,7 @@
 ROWS = 2
 TILE = 160
 IMAGE = 640
-PAD = 16
+PAD = 8
 EXT = TILE + 2 * PAD
 BINS = 15
 UNITS = 128
@@ -253,11 +253,10 @@
         depth_rows.append(
             jnp.concatenate(
                 [
-                    jnp.zeros((1, 8), F32),
                     d_l[:, :8],
                     disp[v, y : y + 1, :],
                     d_r[:, :8],
-                    jnp.zeros((1, 72), F32),
+                    jnp.zeros((1, 80), F32),
                 ],
                 axis=1,
             )
@@ -305,6 +304,7 @@
     inside = (column >= 0) & (column < IMAGE)
     pixel = pixel.astype(F32)
     depth_scale = scale[...] * (1.0 / 192.0)
+    row_at = lax.broadcasted_iota(jnp.int32, (8, 128), 0)
 
     nears, rests = [], []
     for k, (v, y) in enumerate(cases):
@@ -344,21 +344,28 @@
         )
         value = jnp.where(inside, silu_of_half(half), 0.0)
         e_l, e_r = edges[k]
-        out[v, y] = jnp.concatenate([e_l, value[8 : EXT - 8], e_r], axis=0).astype(BF)
+        out[v, y] = jnp.concatenate(
+            [
+                jnp.where(row_at < 6, e_l, value[:8]),
+                value[8 : EXT - 8],
+                jnp.where(row_at < 2, value[EXT - 8 :], pltpu.roll(e_r, 2, 0)),
+            ],
+            axis=0,
+        ).astype(BF)
 
 
 def widened(middle, ends, shift_left, shift_right):
-    before = pltpu.roll(ends[0:16].astype(F32), shift_left, 0).astype(BF)
-    after = pltpu.roll(ends[EXT - 16 :].astype(F32), shift_right, 0).astype(BF)
-    return jnp.concatenate([before, middle, after], axis=0)
+    before = pltpu.roll(ends[:16].astype(F32)[:8], shift_left, 0)
+    after = pltpu.roll(ends[EXT - 16 :].astype(F32)[8:], shift_right, 0)
+    return jnp.concatenate([before, middle.astype(F32), after], axis=0)
 
 
 def wide_hidden(middle, ends):
-    return widened(middle, ends, 14, 8)
+    return widened(middle, ends, 6, 6).astype(BF)
 
 
 def wide_context(middle, ends):
-    return widened(middle, ends, 13, 6)
+    return widened(middle, ends, 5, 4)
 
 
 def kernel_rows(kernel, rows, inputs=slice(None), outputs=slice(None)):
@@ -402,7 +409,7 @@
         for v in range(2):
             wide = wide_context(context[v, y, :, RESET], mot[v, y])
             gates[v, y, :, :UNITS] = terms[v][:, :UNITS]
-            gates[v, y, :, UNITS:] = terms[v][:, UNITS:] + wide.astype(F32)
+            gates[v, y, :, UNITS:] = terms[v][:, UNITS:] + wide
         terms = convolved([m2, m3], kernel_rows(cand_k, rows, FROM_MOTION))
         for v in range(2):
             cands[v, y] = terms[v][PAD : PAD + TILE] + context[v, y, :, 2 * UNITS :].astype(F32)
@@ -428,30 +435,21 @@
     head,
     new,
     inc,
-    halo,
-    halo_mot,
 ):
     row = lax.axis_index("row")
     row_even = row % 2 == 0
-    last = lax.axis_size("row") - 1
-
-    @pl.when(row_even)
-    def _():
-        halo[0] = jnp.where(row > 0, link_in[...], jnp.zeros_like(link_in))
-        halo[1] = chip_in[...]
-        halo_mot[0] = jnp.where(row > 0, mot_link[...], jnp.zeros_like(mot_link))
-        halo_mot[1] = mot_chip[...]
-
-    @pl.when(jnp.logical_not(row_even))
-    def _():
-        halo[0] = chip_in[...]
-        halo[1] = jnp.where(row < last, link_in[...], jnp.zeros_like(link_in))
-        halo_mot[0] = mot_chip[...]
-        halo_mot[1] = jnp.where(row < last, mot_link[...], jnp.zeros_like(mot_link))
+    linked = (row > 0) & (row < lax.axis_size("row") - 1)
+
+    def chosen(side, on_link, on_chip):
+        on_link = jnp.where(linked, on_link, jnp.zeros_like(on_link))
+        return jnp.where(row_even == (side == 0), on_link, on_chip)
+
+    def state_at(side, v, k):
+        return chosen(side, link_in[v, k], chip_in[v, k])
 
     def beyond(side, y):
-        mots = [halo_mot[side, v, y] for v in range(2)]
-        return [wide_hidden(halo[side, v, y], mots[v]) for v in range(2)], mots
+        mots = [chosen(side, mot_link[v, y], mot_chip[v, y]) for v in range(2)]
+        return [wide_hidden(state_at(side, v, y), mots[v]) for v in range(2)], mots
 
     h0, m0 = beyond(0, 0)
     h1, m1 = beyond(0, 1)
@@ -463,7 +461,7 @@
         near_h, near_m = (h1, m1) if side == 0 else (h4, m4)
         resets.append([])
         for v in range(2):
-            wide = wide_context(halo[side, v, ROWS], near_m[v]).astype(F32)
+            wide = wide_context(state_at(side, v, ROWS), near_m[v])
             gate = sigmoid(terms[v] + outer[v, side] + wide)
             resets[-1].append((gate * near_h[v].astype(F32)).astype(BF))
     for y, pieces, rows in ((0, [h1, m1], (0,)), (1, [h4, m4], (2,))):
@@ -494,10 +492,10 @@
             candidate = jnp.tanh(terms[v][PAD : PAD + TILE] + cands[v, y])
             old = hidden[v, y].astype(F32)
             update = updates[y][v]
-            new[v, y] = ((1.0 - update) * old + update * candidate).astype(BF)
-        for v in range(2):
+            fresh = ((1.0 - update) * old + update * candidate).astype(BF)
+            new[v, y] = fresh
             inc[v, y : y + 1, :] = lax.dot_general(
-                head_rows, new[v, y], (((1,), (1,)), ((), ())), preferred_element_type=F32
+                head_rows, fresh, (((1,), (1,)), ((), ())), preferred_element_type=F32
             )[0:1]
 
 
@@ -622,10 +620,6 @@
         call(
             outer_kernel,
             [((2, ROWS, TILE, UNITS), BF), ((2, ROWS, TILE), F32)],
-            scratch=[
-                pltpu.VMEM((2, 2, ROWS + 1, TILE, UNITS), BF),
-                pltpu.VMEM((2, 2, ROWS, EXT, UNITS), BF),
-            ],
             flops=10**9,
             bytes_accessed=4 * 10**6,
         )(

time: 20.9 us -> 20.4 us (0.976)
  Pallas kernels: 7.51 us -> 7.07 us
    pallas_call x1, Pallas kernels: 2.51 us -> 2.2 us  [local(): call(outer_kernel, [((2, ROWS, TILE, UNITS), BF), ((2, ROWS, TILE), F32)]...]
where the time goes in v6:
time: 20.4 us; the launch traced here: 20.3 us
  starting transfers between devices  9.46 us (46%)
  Pallas kernels  7.07 us (35%)
  waiting for transfers between devices  2.97 us (15%)
  between operations  0.73 us (4%)
    ppermute x1, starting transfers between devices, local(): mot_link = lax.ppermute(mot, ('row', 'col'), link)  3.99 us
    ppermute x1, waiting for transfers between devices, local(): mot_link = lax.ppermute(mot, ('row', 'col'), link)  2.29 us
    pallas_call x1, Pallas kernels, local(): call(outer_kernel, [((2, ROWS, TILE, UNITS), BF), ((2, ROWS, TILE), F32)]...  2.2 us
    pallas_call x1, Pallas kernels, local(): call(motion_kernel, [((2, ROWS, EXT, UNITS), BF)], flops=10 ** 9, bytes_a...  2.09 us
    ppermute x1, starting transfers between devices, local(): even_in = lax.ppermute(even_out, ('row', 'col'), even)  1.87 us
    ppermute x1, starting transfers between devices, local(): link_in = lax.ppermute(link_out, ('row', 'col'), link)  1.75 us
    pallas_call x1, Pallas kernels, local(): call(pack_kernel, [((4, 32, 256), BF), ((80, 256), BF), ((80, 256), BF),...  1.46 us
    ppermute x1, starting transfers between devices, local(): far_in = lax.ppermute(far, 'col', across)  1.22 us
  transfers between devices with their start and end apart: 7, of which 2 were waited for; matrix products, arithmetic and copies ran while one was open for 0% of the time, Pallas kernels for 17%

profile of v6, /device:TPU:11, one launch (start us, length us, event | category | flops | bytes accessed | tf_op | source)
XLA Modules:
  0.0 20.3 jit_solution(14460202337419288342)
XLA Ops:
  0.6 1.5 %shard_map.158 = (bf16[4,32,256]{2,1,0:T(8,128)(2,1)S(1)}, bf16[80,256]{1,0:T(8,128)(2,1)S(1)}, bf16[80,256]{1,0:T(8,128)(2,1)S(1)}, bf16[64,128]{1,0:T(8,128)(2...) custom-call(f32[2,15,2,160]{3,2,1,0:T(2,128)} %vox_h.1, ...), custom_call_target="tpu_custom_call" | custom-call | flops 1000000 | bytes 2000000 | tf_op jit(solution)/shard_map/pallas_call | solution.py:543
  2.1 0.3 %collective-permute-start.2 = (bf16[80,256]{1,0:T(8,128)(2,1)S(1)}, bf16[80,256]{1,0:T(8,128)(2,1)S(1)}, u32[]{:S(2)}, u32[]{:S(2)}) collective-permute-start(bf16[80,256]{1,0:T(8,128)(2,1)S(1)} %get-tuple-element.28), channel_id=1, source_target_pairs={{0,1},{1,0},{2,3},{3,2},{4,5},{5,4},{6,7},{7,6},{8,9},{9,8},{10,11... | collective-permute-start | bytes 122888 | tf_op jit(solution)/shard_map/ppermute | solution.py:589
  2.4 1.9 %collective-permute-start.3 = (bf16[80,256]{1,0:T(8,128)(2,1)S(1)}, bf16[80,256]{1,0:T(8,128)(2,1)S(1)}, u32[]{:S(2)}, u32[]{:S(2)}) collective-permute-start(bf16[80,256]{1,0:T(8,128)(2,1)S(1)} %get-tuple-element.29), channel_id=1, source_target_pairs={{0,4},{1,2},{2,1},{3,7},{4,0},{5,6},{6,5},{7,3},{8,12},{9,10},{10,... | collective-permute-start | bytes 122888 | tf_op jit(solution)/shard_map/ppermute | solution.py:590
  4.3 1.2 %collective-permute-start.4 = (bf16[64,128]{1,0:T(8,128)(2,1)S(1)}, bf16[64,128]{1,0:T(8,128)(2,1)S(1)}, u32[]{:S(2)}, u32[]{:S(2)}) collective-permute-start(bf16[64,128]{1,0:T(8,128)(2,1)S(1)} %get-tuple-element.30), channel_id=1, source_target_pairs={{0,2},{1,3},{2,0},{3,1},{4,6},{5,7},{6,4},{7,5},{8,10},{9,11},{10,... | collective-permute-start | bytes 49160 | tf_op jit(solution)/shard_map/ppermute | solution.py:588
  5.5 0.3 %collective-permute-start = (bf16[2,3,160,128]{3,2,1,0:T(8,128)(2,1)S(1)}, bf16[2,3,160,128]{3,2,1,0:T(8,128)(2,1)S(1)}, u32[]{:S(2)}, u32[]{:S(2)}) collective-permute-start(bf16[2,3,160,128]{3,2,1,0:T(8,128)(2,1)S(1)} %get-tuple-element.25), channel_id=1, source_target_pairs={{0,4},{4,0},{8,12},{12,8},{16,20},{20,16},{24,28},{28,24},{1,5},{5... | collective-permute-start | bytes 737288 | tf_op jit(solution)/shard_map/ppermute | solution.py:592
  5.8 1.8 %collective-permute-start.1 = (bf16[2,3,160,128]{3,2,1,0:T(8,128)(2,1)S(1)}, bf16[2,3,160,128]{3,2,1,0:T(8,128)(2,1)S(1)}, u32[]{:S(2)}, u32[]{:S(2)}) collective-permute-start(bf16[2,3,160,128]{3,2,1,0:T(8,128)(2,1)S(1)} %get-tuple-element.26), channel_id=1, source_target_pairs={{0,1},{1,0},{2,3},{3,2},{4,8},{5,9},{6,10},{7,11},{8,4},{9,5},{10,... | collective-permute-start | bytes 737288 | tf_op jit(solution)/shard_map/ppermute | solution.py:591
  7.6 0.2 shard_map.159
  7.7 0.7 %collective-permute-done.4.far_in = bf16[64,128]{1,0:T(8,128)(2,1)S(1)} collective-permute-done((bf16[64,128]{1,0:T(8,128)(2,1)S(1)}, bf16[64,128]{1,0:T(8,128)(2,1)S(1)}, u32[]{:S(2)}, u32[]{:S(2)}) %collective-permute-start.4) | collective-permute-done | bytes 16416 | tf_op jit(solution)/shard_map/ppermute | solution.py:588
  8.4 0.0 collective-permute-done.2.odd_in
  8.4 0.0 collective-permute-done.3.even_in
  8.4 0.0 copy-start.1
  8.4 0.0 copy-start.2
  8.4 0.0 copy-start.3
  8.5 2.1 %shard_map.160.mot = bf16[2,2,176,128]{3,2,1,0:T(8,128)(2,1)S(1)} custom-call(bf16[4,32,256]{2,1,0:T(8,128)(2,1)S(1)} %get-tuple-element.27.own, bf16[80,256]{1,0:T(8,128)(2,1)S(1)} %collective-permute-done.2.odd_in, bf16[80,256]{1,0:T(8,128)(2,1)S(1)} %collective-permute-done.3.even_in, bf16[64,128]{1,0:T(8,128)(2,1)S(1)} %collective-permute-done.4.far_in, ...), custom_call_target="tpu_custom_call" | custom-call | flops 1000000000 | bytes 1000000 | tf_op jit(solution)/shard_map/pallas_call | solution.py:600
  10.6 0.0 copy-start.4
  10.6 4.0 %collective-permute-start.6 = (bf16[2,2,176,128]{3,2,1,0:T(8,128)(2,1)S(1)}, bf16[2,2,176,128]{3,2,1,0:T(8,128)(2,1)S(1)}, u32[]{:S(2)}, u32[]{:S(2)}) collective-permute-start(bf16[2,2,176,128]{3,2,1,0:T(8,128)(2,1)S(1)} %shard_map.160.mot), channel_id=1, source_target_pairs={{0,1},{1,0},{2,3},{3,2},{4,8},{5,9},{6,10},{7,11},{8,4},{9,5},{10,... | collective-permute-start | bytes 540680 | tf_op jit(solution)/shard_map/ppermute | solution.py:606
  14.6 0.0 collective-permute-start.5
  14.6 0.0 copy-done.2
  14.6 1.1 %shard_map.161 = (f32[2,2,176,256]{3,2,1,0:T(8,128)S(1)}, f32[2,2,176,128]{3,2,1,0:T(8,128)S(1)}, f32[2,2,160,128]{3,2,1,0:T(8,128)S(1)}, bf16[2,2,176,128]{3,2,1,0:T(8,128)(2,1)S(1)}) custom-call(bf16[2,2,160,128]{3,2,1,0:T(8,128)(2,1)S(1)} %copy-done.2, bf16[2,2,160,384]{3,2,1,0:T(8,128)(2,1)S(1)} %copy-done, bf16[2,2,176,128]{3,2,1,0:T(8,128)(2,1)S(1)} %shard_map.160.mot, ...), custom_call_target="tpu_custom_call" | custom-call | flops 1000000000 | bytes 4000000 | tf_op jit(solution)/shard_map/pallas_call | solution.py:608
  15.7 2.3 %collective-permute-done.6.mot_link = bf16[2,2,176,128]{3,2,1,0:T(8,128)(2,1)S(1)} collective-permute-done((bf16[2,2,176,128]{3,2,1,0:T(8,128)(2,1)S(1)}, bf16[2,2,176,128]{3,2,1,0:T(8,128)(2,1)S(1)}, u32[]{:S(2)}, u32[]{:S(2)}) %collective-permute-start.6) | collective-permute-done | bytes 180256 | tf_op jit(solution)/shard_map/ppermute | solution.py:606
  18.0 0.0 collective-permute-done.5.mot_chip
  18.0 0.0 collective-permute-done.chip_in
  18.0 0.0 collective-permute-done.1.link_in
  18.1 2.2 %shard_map.162 = (bf16[2,2,160,128]{3,2,1,0:T(8,128)(2,1)}, f32[2,2,160]{2,1,0:T(2,128)}) custom-call(bf16[2,2,160,128]{3,2,1,0:T(8,128)(2,1)S(1)} %copy-done.2, bf16[2,2,160,384]{3,2,1,0:T(8,128)(2,1)S(1)} %copy-done, bf16[2,3,160,128]{3,2,1,0:T(8,128)(2,1)S(1)} %collective-permute-done.chip_in, ...), custom_call_target="tpu_custom_call" | custom-call | flops 1000000000 | bytes 4000000 | tf_op jit(solution)/shard_map/pallas_call | solution.py:620
  (5 shorter events, 0.0 us)
Async XLA Ops:
  2.1 6.3 %collective-permute-start.2 = (bf16[80,256]{1,0:T(8,128)(2,1)S(1)}, bf16[80,256]{1,0:T(8,128)(2,1)S(1)}, u32[]{:S(2)}, u32[]{:S(2)}) collective-permute-start(bf16[80,256]{1,0:T(8,128)(2,1)S(1)} %get-tuple-element.28), channel_id=1, source_target_pairs={{0,1},{1,0},{2,3},{3,2},{4,5},{5,4},{6,7},{7,6},{8,9},{9,8},{10,11... | collective-permute-start | bytes 122888 | tf_op jit(solution)/shard_map/ppermute | solution.py:589
  2.4 6.0 %collective-permute-start.3 = (bf16[80,256]{1,0:T(8,128)(2,1)S(1)}, bf16[80,256]{1,0:T(8,128)(2,1)S(1)}, u32[]{:S(2)}, u32[]{:S(2)}) collective-permute-start(bf16[80,256]{1,0:T(8,128)(2,1)S(1)} %get-tuple-element.29), channel_id=1, source_target_pairs={{0,4},{1,2},{2,1},{3,7},{4,0},{5,6},{6,5},{7,3},{8,12},{9,10},{10,... | collective-permute-start | bytes 122888 | tf_op jit(solution)/shard_map/ppermute | solution.py:590
  4.3 4.1 %collective-permute-start.4 = (bf16[64,128]{1,0:T(8,128)(2,1)S(1)}, bf16[64,128]{1,0:T(8,128)(2,1)S(1)}, u32[]{:S(2)}, u32[]{:S(2)}) collective-permute-start(bf16[64,128]{1,0:T(8,128)(2,1)S(1)} %get-tuple-element.30), channel_id=1, source_target_pairs={{0,2},{1,3},{2,0},{3,1},{4,6},{5,7},{6,4},{7,5},{8,10},{9,11},{10,... | collective-permute-start | bytes 49160 | tf_op jit(solution)/shard_map/ppermute | solution.py:588
  5.5 12.5 %collective-permute-start = (bf16[2,3,160,128]{3,2,1,0:T(8,128)(2,1)S(1)}, bf16[2,3,160,128]{3,2,1,0:T(8,128)(2,1)S(1)}, u32[]{:S(2)}, u32[]{:S(2)}) collective-permute-start(bf16[2,3,160,128]{3,2,1,0:T(8,128)(2,1)S(1)} %get-tuple-element.25), channel_id=1, source_target_pairs={{0,4},{4,0},{8,12},{12,8},{16,20},{20,16},{24,28},{28,24},{1,5},{5... | collective-permute-start | bytes 737288 | tf_op jit(solution)/shard_map/ppermute | solution.py:592
  5.8 12.2 %collective-permute-start.1 = (bf16[2,3,160,128]{3,2,1,0:T(8,128)(2,1)S(1)}, bf16[2,3,160,128]{3,2,1,0:T(8,128)(2,1)S(1)}, u32[]{:S(2)}, u32[]{:S(2)}) collective-permute-start(bf16[2,3,160,128]{3,2,1,0:T(8,128)(2,1)S(1)} %get-tuple-element.26), channel_id=1, source_target_pairs={{0,1},{1,0},{2,3},{3,2},{4,8},{5,9},{6,10},{7,11},{8,4},{9,5},{10,... | collective-permute-start | bytes 737288 | tf_op jit(solution)/shard_map/ppermute | solution.py:591
  8.4 6.1 %copy-start = (bf16[2,2,160,384]{3,2,1,0:T(8,128)(2,1)S(1)}, bf16[2,2,160,384]{3,2,1,0:T(8,128)(2,1)}, u32[]{:S(2)}) copy-start(bf16[2,2,160,384]{3,2,1,0:T(8,128)(2,1)} %context.3) | copy-start | bytes 1474564
  8.4 6.1 %copy-start.1 = (bf16[3,3,256,256]{3,2,1,0:T(8,128)(2,1)S(1)}, bf16[3,3,256,256]{3,2,1,0:T(8,128)(2,1)}, u32[]{:S(2)}) copy-start(bf16[3,3,256,256]{3,2,1,0:T(8,128)(2,1)} %gate_k.3) | copy-start | bytes 3538948
  8.4 6.1 %copy-start.2 = (bf16[2,2,160,128]{3,2,1,0:T(8,128)(2,1)S(1)}, bf16[2,2,160,128]{3,2,1,0:T(8,128)(2,1)}, u32[]{:S(2)}) copy-start(bf16[2,2,160,128]{3,2,1,0:T(8,128)(2,1)} %hidden.3) | copy-start | bytes 491524
  8.4 6.1 %copy-start.3 = (bf16[3,3,256,128]{3,2,1,0:T(8,128)(2,1)S(1)}, bf16[3,3,256,128]{3,2,1,0:T(8,128)(2,1)}, u32[]{:S(2)}) copy-start(bf16[3,3,256,128]{3,2,1,0:T(8,128)(2,1)} %cand_k.3) | copy-start | bytes 1769476
  10.6 7.5 %copy-start.4 = (bf16[128]{0:T(256)(128)(2,1)S(1)}, bf16[128]{0:T(256)(128)(2,1)}, u32[]{:S(2)}) copy-start(bf16[128]{0:T(256)(128)(2,1)} %param.27) | copy-start | bytes 772
  10.6 7.5 %collective-permute-start.6 = (bf16[2,2,176,128]{3,2,1,0:T(8,128)(2,1)S(1)}, bf16[2,2,176,128]{3,2,1,0:T(8,128)(2,1)S(1)}, u32[]{:S(2)}, u32[]{:S(2)}) collective-permute-start(bf16[2,2,176,128]{3,2,1,0:T(8,128)(2,1)S(1)} %shard_map.160.mot), channel_id=1, source_target_pairs={{0,1},{1,0},{2,3},{3,2},{4,8},{5,9},{6,10},{7,11},{8,4},{9,5},{10,... | collective-permute-start | bytes 540680 | tf_op jit(solution)/shard_map/ppermute | solution.py:606
  14.6 3.5 %collective-permute-start.5 = (bf16[2,2,176,128]{3,2,1,0:T(8,128)(2,1)S(1)}, bf16[2,2,176,128]{3,2,1,0:T(8,128)(2,1)S(1)}, u32[]{:S(2)}, u32[]{:S(2)}) collective-permute-start(bf16[2,2,176,128]{3,2,1,0:T(8,128)(2,1)S(1)} %shard_map.160.mot), channel_id=1, source_target_pairs={{0,4},{4,0},{8,12},{12,8},{16,20},{20,16},{24,28},{28,24},{1,5},{5... | collective-permute-start | bytes 540680 | tf_op jit(solution)/shard_map/ppermute | solution.py:607

commit v7 on v6

--- a/solution.py
+++ b/solution.py
@@ -17,9 +17,8 @@
 BINS = 15
 UNITS = 128
 NEAR = 48
-FAR = 72
-WINDOW = 512
-LAST = FAR + 2 * TILE + NEAR - 1
+CLOSE = 384
+WINDOW = CLOSE + 128
 TAPS = 9
 LEVELS = 4
 GROUP = 40
@@ -148,8 +147,7 @@
             jnp.concatenate([f1, f0[:, TILE - NEAR :], blank], axis=1),
             jnp.concatenate([f0, f1[:, :NEAR], blank], axis=1),
         )
-        tail = jnp.concatenate([f1[:, TILE - FAR :], jnp.zeros((32, 128 - FAR), F32)], axis=1)
-        far[rows_at, :] = jnp.where(col < 2, tail, f0[:, :128]).astype(BF)
+        far[rows_at, :] = jnp.where(col < 2, f1[:, TILE - 128 :], f0[:, :128]).astype(BF)
 
     for copy in copies[2:data]:
         copy.wait()
@@ -214,23 +212,17 @@
     ).astype(BF)
 
 
-def motion_kernel(
-    own,
-    odd_in,
-    even_in,
-    far_in,
-    disp,
-    w1,
-    w1t,
-    w2,
-    w2t,
-    mw,
-    scale,
-    bias,
-    pool,
-    rows,
-    out,
-):
+def matched(windows, w1t, w2t):
+    layer = silu_of_half(
+        jnp.dot(w1t[:, :48], jnp.concatenate(windows, axis=1), preferred_element_type=F32)
+    ).astype(BF)
+    return jnp.dot(w2t[...], layer, preferred_element_type=F32).astype(BF)
+
+
+CASES = [(v, y) for v in range(2) for y in range(ROWS)]
+
+
+def close_kernel(own, odd_in, even_in, disp, w1, w1t, w2, w2t, query_out, match_out, depth_out, edge_out):
     col = lax.axis_index("col")
     is_even = col % 2 == 0
 
@@ -240,14 +232,13 @@
         right = jnp.where(col < 3, jnp.where(is_even, first, second), 0.0)
         return left, right
 
-    cases = [(v, y) for v in range(2) for y in range(ROWS)]
     edge_left, edge_right = received(pl.ds(64, 16))
     edges = [
         tuple(e[8 * y : 8 * y + 8, 128 * v : 128 * v + 128] for e in (edge_left, edge_right))
-        for v, y in cases
+        for v, y in CASES
     ]
     depth_rows = []
-    for (v, y), (e_l, e_r) in zip(cases, edges):
+    for (v, y), (e_l, e_r) in zip(CASES, edges):
         d_l = e_l[3:4] + e_l[4:5] + e_l[5:6]
         d_r = e_r[3:4] + e_r[4:5] + e_r[5:6]
         depth_rows.append(
@@ -262,23 +253,22 @@
             )
         )
     depth_rows.append(jnp.zeros((4, 256), F32))
-    depths = jnp.concatenate(depth_rows, axis=0).T
-
-    blank = jnp.zeros((32, WINDOW - 1 - LAST), F32)
+    depth_out[...] = jnp.concatenate(depth_rows, axis=0).T[:EXT]
+    edge_out[0] = edge_left
+    edge_out[1] = edge_right
+
+    blank = jnp.zeros((32, CLOSE - 2 * TILE - NEAR), F32)
     sides = [received(pl.ds(32 * y, 32)) for y in range(ROWS)]
     queries, windows = [], []
-    for v, y in cases:
+    for v, y in CASES:
         left, right = sides[y]
-        far = far_in[32 * y : 32 * y + 32, :].astype(F32)[:, :FAR]
         mine = own[ROWS * v + y].astype(F32)[:, :TILE]
         other = own[ROWS * (1 - v) + y].astype(F32)[:, :TILE]
         if v == 0:
-            far = jnp.where(col >= 2, far, 0.0)
-            pieces = [far, left[:, :TILE], other, right[:, TILE : TILE + NEAR], blank]
+            pieces = [left[:, :TILE], other, right[:, TILE : TILE + NEAR], blank]
             ends = (left[:, TILE + NEAR - PAD : TILE + NEAR], right[:, :PAD])
         else:
-            far = jnp.where(col < 2, far, 0.0)
-            pieces = [left[:, TILE : TILE + NEAR], other, right[:, :TILE], far, blank]
+            pieces = [blank, left[:, TILE : TILE + NEAR], other, right[:, :TILE]]
             ends = (left[:, TILE - PAD : TILE], right[:, TILE : TILE + PAD])
         window = jnp.concatenate(pieces, axis=1)
         windows.append(jnp.concatenate([window, window[:16]], axis=0).astype(BF))
@@ -288,12 +278,14 @@
     stacked = jnp.concatenate(queries, axis=0).T.astype(BF)
     layer = silu_of_half(jnp.dot(stacked[:EXT], w1[...], preferred_element_type=F32)).astype(BF)
     layer = jnp.concatenate([layer[:, 256 * k : 256 * k + 256] for k in range(4)], axis=0)
-    features = jnp.dot(layer, w2[...], preferred_element_type=F32).astype(BF)
-    layer = silu_of_half(
-        jnp.dot(w1t[:, :48], jnp.concatenate(windows, axis=1), preferred_element_type=F32)
-    ).astype(BF)
-    match = jnp.dot(w2t[...], layer, preferred_element_type=F32).astype(BF)
-
+    query_out[...] = jnp.dot(layer, w2[...], preferred_element_type=F32).astype(BF)
+    match_out[...] = matched(windows, w1t, w2t)
+
+
+def motion_kernel(
+    far_in, query, match, depths, edges, w1t, w2t, mw, scale, bias, pool, rows, out
+):
+    col = lax.axis_index("col")
     first = rows[0:1, :].astype(jnp.int32)
     level_scale = rows[1:2, :]
     is_low = rows[2:3, :] > 0.5
@@ -306,25 +298,36 @@
     depth_scale = scale[...] * (1.0 / 192.0)
     row_at = lax.broadcasted_iota(jnp.int32, (8, 128), 0)
 
+    windows = []
+    for v, y in CASES:
+        usable = col >= 2 if v == 0 else col < 2
+        window = jnp.where(usable, far_in[32 * y : 32 * y + 32, :].astype(F32), 0.0)
+        windows.append(jnp.concatenate([window, window[:16]], axis=0).astype(BF))
+    far_match = matched(windows, w1t, w2t)
+
     nears, rests = [], []
-    for k, (v, y) in enumerate(cases):
+    for k, (v, y) in enumerate(CASES):
+        features = query[EXT * k : EXT * k + EXT, :]
         scores = jnp.dot(
-            features[EXT * k : EXT * k + EXT],
-            match[:, WINDOW * k : WINDOW * k + WINDOW],
-            preferred_element_type=F32,
-        )
-        spot = (pixel - PAD if v == 0 else (EXT - 1 - PAD) - pixel) - depths[:EXT, k : k + 1]
+            features, match[:, CLOSE * k : CLOSE * k + CLOSE], preferred_element_type=F32
+        )
+        far_scores = jnp.dot(
+            features, far_match[:, 128 * k : 128 * k + 128], preferred_element_type=F32
+        )
+        blocks = [scores[:, 128 * m : 128 * m + 128] for m in range(CLOSE // 128)]
+        blocks = [far_scores] + blocks if v == 0 else blocks + [far_scores]
+        spot = (pixel - PAD if v == 0 else (EXT - 1 - PAD) - pixel) - depths[:, k : k + 1]
         eighth = jnp.floor(spot * 0.125)
         rests.append(spot - 8.0 * eighth)
-        start = (8.0 * eighth).astype(jnp.int32) + (FAR + TILE - 32)
+        start = (8.0 * eighth).astype(jnp.int32) + (128 + TILE - 32)
         if v == 0:
             block, place = (start + 127 - lane) >> 7, (start + lane) & 127
         else:
-            index = (LAST - start) - lane
+            index = (WINDOW - 1 - start) - lane
             block, place = index >> 7, index & 127
-        source = scores[:, :128]
+        source = blocks[0]
         for m in range(1, WINDOW // 128):
-            source = jnp.where(block == m, scores[:, 128 * m : 128 * m + 128], source)
+            source = jnp.where(block == m, blocks[m], source)
         near = jnp.take_along_axis(source, place, axis=1, mode="promise_in_bounds")
         high, low = split(near)
         nears.append(jnp.concatenate([high.astype(BF), low.astype(BF)], axis=1))
@@ -338,12 +341,12 @@
         high, low = split(jnp.take_along_axis(table, index, axis=1, mode="promise_in_bounds"))
         looks.append(jnp.where(is_low, low, high).astype(BF))
     sums = jnp.dot(jnp.concatenate(looks, axis=0), mw[...], preferred_element_type=F32)
-    for k, (v, y) in enumerate(cases):
+    for k, (v, y) in enumerate(CASES):
         half = 0.5 * (
-            sums[EXT * k : EXT * k + EXT] + depths[:EXT, k : k + 1] * depth_scale + bias[...]
+            sums[EXT * k : EXT * k + EXT] + depths[:, k : k + 1] * depth_scale + bias[...]
         )
         value = jnp.where(inside, silu_of_half(half), 0.0)
-        e_l, e_r = edges[k]
+        e_l, e_r = (edges[m, 8 * y : 8 * y + 8, 128 * v : 128 * v + 128] for m in range(2))
         out[v, y] = jnp.concatenate(
             [
                 jnp.where(row_at < 6, e_l, value[:8]),
@@ -597,12 +600,23 @@
         bytes_accessed=2 * 10**6,
     )(*raw)
     w2 = raw[2]
+    query, match, depths, edges = call(
+        close_kernel,
+        [
+            ((4 * EXT, 256), BF),
+            ((256, 4 * CLOSE), BF),
+            ((EXT, 8), F32),
+            ((2, 16, 256), F32),
+        ],
+        flops=10**9,
+        bytes_accessed=10**6,
+    )(own, odd_in, even_in, disp, w1, w1t, w2, w2t)
     (mot,) = call(
         motion_kernel,
         [((2, ROWS, EXT, UNITS), BF)],
         flops=10**9,
         bytes_accessed=10**6,
-    )(own, odd_in, even_in, far_in, disp, w1, w1t, w2, w2t, mw, scale, bias, pool, lane_rows)
+    )(far_in, query, match, depths, edges, w1t, w2t, mw, scale, bias, pool, lane_rows)
     mot_link = lax.ppermute(mot, ("row", "col"), link)
     mot_chip = lax.ppermute(mot, "row", chip)
     gates, outer, cands, state = call(

time: 20.4 us -> 19.9 us (0.975)
  the two profiles are of different devices: /device:TPU:11 before, /device:TPU:1 now
where the time goes in v7:
time: 19.9 us; the launch traced here: 19.8 us
  starting transfers between devices  9.85 us (49%)
  Pallas kernels  7.43 us (37%)
  waiting for transfers between devices  1.74 us (9%)
  between operations  0.75 us (4%)
    ppermute x1, starting transfers between devices, local(): chip_in = lax.ppermute(chip_out, 'row', chip)  2.84 us
    pallas_call x1, Pallas kernels, local(): call(outer_kernel, [((2, ROWS, TILE, UNITS), BF), ((2, ROWS, TILE), F32)]...  2.22 us
    ppermute x1, starting transfers between devices, local(): odd_in = lax.ppermute(odd_out, 'col', odd)  2.13 us
    ppermute x1, starting transfers between devices, local(): mot_link = lax.ppermute(mot, ('row', 'col'), link)  1.84 us
    ppermute x1, waiting for transfers between devices, local(): mot_link = lax.ppermute(mot, ('row', 'col'), link)  1.72 us
    pallas_call x1, Pallas kernels, local(): call(pack_kernel, [((4, 32, 256), BF), ((80, 256), BF), ((80, 256), BF),...  1.46 us
    pallas_call x1, Pallas kernels, local(): call(motion_kernel, [((2, ROWS, EXT, UNITS), BF)], flops=10 ** 9, bytes_a...  1.42 us
    ppermute x1, starting transfers between devices, local(): even_in = lax.ppermute(even_out, ('row', 'col'), even)  1.3 us
  transfers between devices with their start and end apart: 7, of which 1 were waited for; matrix products, arithmetic and copies ran while one was open for 0% of the time, Pallas kernels for 19%

profile of v7, /device:TPU:1, one launch (start us, length us, event | category | flops | bytes accessed | tf_op | source)
XLA Modules:
  0.0 19.8 jit_solution(16829937347700306742)
XLA Ops:
  0.6 1.5 %shard_map.158 = (bf16[4,32,256]{2,1,0:T(8,128)(2,1)S(1)}, bf16[80,256]{1,0:T(8,128)(2,1)S(1)}, bf16[80,256]{1,0:T(8,128)(2,1)S(1)}, bf16[64,128]{1,0:T(8,128)(2...) custom-call(f32[2,15,2,160]{3,2,1,0:T(2,128)} %vox_h.1, ...), custom_call_target="tpu_custom_call" | custom-call | flops 1000000 | bytes 2000000 | tf_op jit(solution)/shard_map/pallas_call | solution.py:546
  2.1 2.1 %collective-permute-start.3 = (bf16[80,256]{1,0:T(8,128)(2,1)S(1)}, bf16[80,256]{1,0:T(8,128)(2,1)S(1)}, u32[]{:S(2)}, u32[]{:S(2)}) collective-permute-start(bf16[80,256]{1,0:T(8,128)(2,1)S(1)} %get-tuple-element.33), channel_id=1, source_target_pairs={{0,1},{1,0},{2,3},{3,2},{4,5},{5,4},{6,7},{7,6},{8,9},{9,8},{10,11... | collective-permute-start | bytes 122888 | tf_op jit(solution)/shard_map/ppermute | solution.py:592
  4.2 1.3 %collective-permute-start.4 = (bf16[80,256]{1,0:T(8,128)(2,1)S(1)}, bf16[80,256]{1,0:T(8,128)(2,1)S(1)}, u32[]{:S(2)}, u32[]{:S(2)}) collective-permute-start(bf16[80,256]{1,0:T(8,128)(2,1)S(1)} %get-tuple-element.34), channel_id=1, source_target_pairs={{0,4},{1,2},{2,1},{3,7},{4,0},{5,6},{6,5},{7,3},{8,12},{9,10},{10,... | collective-permute-start | bytes 122888 | tf_op jit(solution)/shard_map/ppermute | solution.py:593
  5.5 1.2 %collective-permute-start.2 = (bf16[64,128]{1,0:T(8,128)(2,1)S(1)}, bf16[64,128]{1,0:T(8,128)(2,1)S(1)}, u32[]{:S(2)}, u32[]{:S(2)}) collective-permute-start(bf16[64,128]{1,0:T(8,128)(2,1)S(1)} %get-tuple-element.31), channel_id=1, source_target_pairs={{0,2},{1,3},{2,0},{3,1},{4,6},{5,7},{6,4},{7,5},{8,10},{9,11},{10,... | collective-permute-start | bytes 49160 | tf_op jit(solution)/shard_map/ppermute | solution.py:591
  6.7 2.8 %collective-permute-start = (bf16[2,3,160,128]{3,2,1,0:T(8,128)(2,1)S(1)}, bf16[2,3,160,128]{3,2,1,0:T(8,128)(2,1)S(1)}, u32[]{:S(2)}, u32[]{:S(2)}) collective-permute-start(bf16[2,3,160,128]{3,2,1,0:T(8,128)(2,1)S(1)} %get-tuple-element.29), channel_id=1, source_target_pairs={{0,4},{4,0},{8,12},{12,8},{16,20},{20,16},{24,28},{28,24},{1,5},{5... | collective-permute-start | bytes 737288 | tf_op jit(solution)/shard_map/ppermute | solution.py:595
  9.5 0.0 collective-permute-start.1
  9.5 0.2 shard_map.159
  9.7 0.0 collective-permute-done.3.odd_in
  9.7 0.0 collective-permute-done.4.even_in
  9.7 1.0 %shard_map.160 = (bf16[704,256]{1,0:T(8,128)(2,1)S(1)}, bf16[256,1536]{1,0:T(8,128)(2,1)S(1)}, f32[176,8]{1,0:T(8,128)S(1)}, f32[2,16,256]{2,1,0:T(8,128)S(1)}) custom-call(bf16[4,32,256]{2,1,0:T(8,128)(2,1)S(1)} %get-tuple-element.32.own, bf16[80,256]{1,0:T(8,128)(2,1)S(1)} %collective-permute-done.3.odd_in, ...), custom_call_target="tpu_custom_call" | custom-call | flops 1000000000 | bytes 1000000 | tf_op jit(solution)/shard_map/pallas_call | solution.py:603
  10.7 0.0 collective-permute-done.2.far_in
  10.8 0.0 copy-start
  10.8 0.0 copy-start.1
  10.8 0.0 copy-start.2
  10.8 0.0 copy-start.3
  10.8 1.4 %shard_map.161.mot = bf16[2,2,176,128]{3,2,1,0:T(8,128)(2,1)S(1)} custom-call(bf16[64,128]{1,0:T(8,128)(2,1)S(1)} %collective-permute-done.2.far_in, bf16[704,256]{1,0:T(8,128)(2,1)S(1)} %get-tuple-element.43.query, bf16[256,1536]{1,0:T(8,128)(2,1)S(1)} %get-tuple-element.44.match, f32[176,8]{1,0:T(8,128)S(1)} %get-tuple-element.45.depths, ...), custom_call_target="tpu_custom_call" | custom-call | flops 1000000000 | bytes 1000000 | tf_op jit(solution)/shard_map/pallas_call | solution.py:614
  12.2 0.0 copy-start.4
  12.2 1.8 %collective-permute-start.6 = (bf16[2,2,176,128]{3,2,1,0:T(8,128)(2,1)S(1)}, bf16[2,2,176,128]{3,2,1,0:T(8,128)(2,1)S(1)}, u32[]{:S(2)}, u32[]{:S(2)}) collective-permute-start(bf16[2,2,176,128]{3,2,1,0:T(8,128)(2,1)S(1)} %shard_map.161.mot), channel_id=1, source_target_pairs={{0,1},{1,0},{2,3},{3,2},{4,8},{5,9},{6,10},{7,11},{8,4},{9,5},{10,... | collective-permute-start | bytes 540680 | tf_op jit(solution)/shard_map/ppermute | solution.py:620
  14.1 0.6 %collective-permute-start.5 = (bf16[2,2,176,128]{3,2,1,0:T(8,128)(2,1)S(1)}, bf16[2,2,176,128]{3,2,1,0:T(8,128)(2,1)S(1)}, u32[]{:S(2)}, u32[]{:S(2)}) collective-permute-start(bf16[2,2,176,128]{3,2,1,0:T(8,128)(2,1)S(1)} %shard_map.161.mot), channel_id=1, source_target_pairs={{0,4},{4,0},{8,12},{12,8},{16,20},{20,16},{24,28},{28,24},{1,5},{5... | collective-permute-start | bytes 540680 | tf_op jit(solution)/shard_map/ppermute | solution.py:621
  14.7 1.1 %shard_map.162 = (f32[2,2,176,256]{3,2,1,0:T(8,128)S(1)}, f32[2,2,176,128]{3,2,1,0:T(8,128)S(1)}, f32[2,2,160,128]{3,2,1,0:T(8,128)S(1)}, bf16[2,2,176,128]{3,2,1,0:T(8,128)(2,1)S(1)}) custom-call(bf16[2,2,160,128]{3,2,1,0:T(8,128)(2,1)S(1)} %copy-done.2, bf16[2,2,160,384]{3,2,1,0:T(8,128)(2,1)S(1)} %copy-done, bf16[2,2,176,128]{3,2,1,0:T(8,128)(2,1)S(1)} %shard_map.161.mot, ...), custom_call_target="tpu_custom_call" | custom-call | flops 1000000000 | bytes 4000000 | tf_op jit(solution)/shard_map/pallas_call | solution.py:622
  15.8 1.7 %collective-permute-done.6.mot_link = bf16[2,2,176,128]{3,2,1,0:T(8,128)(2,1)S(1)} collective-permute-done((bf16[2,2,176,128]{3,2,1,0:T(8,128)(2,1)S(1)}, bf16[2,2,176,128]{3,2,1,0:T(8,128)(2,1)S(1)}, u32[]{:S(2)}, u32[]{:S(2)}) %collective-permute-start.6) | collective-permute-done | bytes 180256 | tf_op jit(solution)/shard_map/ppermute | solution.py:620
  17.6 0.0 collective-permute-done.5.mot_chip
  17.6 0.0 collective-permute-done.1.link_in
  17.6 2.2 %shard_map.163 = (bf16[2,2,160,128]{3,2,1,0:T(8,128)(2,1)}, f32[2,2,160]{2,1,0:T(2,128)}) custom-call(bf16[2,2,160,128]{3,2,1,0:T(8,128)(2,1)S(1)} %copy-done.2, bf16[2,2,160,384]{3,2,1,0:T(8,128)(2,1)S(1)} %copy-done, bf16[2,3,160,128]{3,2,1,0:T(8,128)(2,1)S(1)} %collective-permute-done.chip_in, ...), custom_call_target="tpu_custom_call" | custom-call | flops 1000000000 | bytes 4000000 | tf_op jit(solution)/shard_map/pallas_call | solution.py:634
  (6 shorter events, 0.0 us)
Async XLA Ops:
  2.1 7.6 %collective-permute-start.3 = (bf16[80,256]{1,0:T(8,128)(2,1)S(1)}, bf16[80,256]{1,0:T(8,128)(2,1)S(1)}, u32[]{:S(2)}, u32[]{:S(2)}) collective-permute-start(bf16[80,256]{1,0:T(8,128)(2,1)S(1)} %get-tuple-element.33), channel_id=1, source_target_pairs={{0,1},{1,0},{2,3},{3,2},{4,5},{5,4},{6,7},{7,6},{8,9},{9,8},{10,11... | collective-permute-start | bytes 122888 | tf_op jit(solution)/shard_map/ppermute | solution.py:592
  4.2 5.5 %collective-permute-start.4 = (bf16[80,256]{1,0:T(8,128)(2,1)S(1)}, bf16[80,256]{1,0:T(8,128)(2,1)S(1)}, u32[]{:S(2)}, u32[]{:S(2)}) collective-permute-start(bf16[80,256]{1,0:T(8,128)(2,1)S(1)} %get-tuple-element.34), channel_id=1, source_target_pairs={{0,4},{1,2},{2,1},{3,7},{4,0},{5,6},{6,5},{7,3},{8,12},{9,10},{10,... | collective-permute-start | bytes 122888 | tf_op jit(solution)/shard_map/ppermute | solution.py:593
  5.5 5.2 %collective-permute-start.2 = (bf16[64,128]{1,0:T(8,128)(2,1)S(1)}, bf16[64,128]{1,0:T(8,128)(2,1)S(1)}, u32[]{:S(2)}, u32[]{:S(2)}) collective-permute-start(bf16[64,128]{1,0:T(8,128)(2,1)S(1)} %get-tuple-element.31), channel_id=1, source_target_pairs={{0,2},{1,3},{2,0},{3,1},{4,6},{5,7},{6,4},{7,5},{8,10},{9,11},{10,... | collective-permute-start | bytes 49160 | tf_op jit(solution)/shard_map/ppermute | solution.py:591
  6.7 10.9 %collective-permute-start = (bf16[2,3,160,128]{3,2,1,0:T(8,128)(2,1)S(1)}, bf16[2,3,160,128]{3,2,1,0:T(8,128)(2,1)S(1)}, u32[]{:S(2)}, u32[]{:S(2)}) collective-permute-start(bf16[2,3,160,128]{3,2,1,0:T(8,128)(2,1)S(1)} %get-tuple-element.29), channel_id=1, source_target_pairs={{0,4},{4,0},{8,12},{12,8},{16,20},{20,16},{24,28},{28,24},{1,5},{5... | collective-permute-start | bytes 737288 | tf_op jit(solution)/shard_map/ppermute | solution.py:595
  9.5 8.0 %collective-permute-start.1 = (bf16[2,3,160,128]{3,2,1,0:T(8,128)(2,1)S(1)}, bf16[2,3,160,128]{3,2,1,0:T(8,128)(2,1)S(1)}, u32[]{:S(2)}, u32[]{:S(2)}) collective-permute-start(bf16[2,3,160,128]{3,2,1,0:T(8,128)(2,1)S(1)} %get-tuple-element.30), channel_id=1, source_target_pairs={{0,1},{1,0},{2,3},{3,2},{4,8},{5,9},{6,10},{7,11},{8,4},{9,5},{10,... | collective-permute-start | bytes 737288 | tf_op jit(solution)/shard_map/ppermute | solution.py:594
  10.8 3.9 %copy-start = (bf16[2,2,160,384]{3,2,1,0:T(8,128)(2,1)S(1)}, bf16[2,2,160,384]{3,2,1,0:T(8,128)(2,1)}, u32[]{:S(2)}) copy-start(bf16[2,2,160,384]{3,2,1,0:T(8,128)(2,1)} %context.3) | copy-start | bytes 1474564
  10.8 3.9 %copy-start.1 = (bf16[3,3,256,256]{3,2,1,0:T(8,128)(2,1)S(1)}, bf16[3,3,256,256]{3,2,1,0:T(8,128)(2,1)}, u32[]{:S(2)}) copy-start(bf16[3,3,256,256]{3,2,1,0:T(8,128)(2,1)} %gate_k.3) | copy-start | bytes 3538948
  10.8 3.9 %copy-start.2 = (bf16[2,2,160,128]{3,2,1,0:T(8,128)(2,1)S(1)}, bf16[2,2,160,128]{3,2,1,0:T(8,128)(2,1)}, u32[]{:S(2)}) copy-start(bf16[2,2,160,128]{3,2,1,0:T(8,128)(2,1)} %hidden.3) | copy-start | bytes 491524
  10.8 3.9 %copy-start.3 = (bf16[3,3,256,128]{3,2,1,0:T(8,128)(2,1)S(1)}, bf16[3,3,256,128]{3,2,1,0:T(8,128)(2,1)}, u32[]{:S(2)}) copy-start(bf16[3,3,256,128]{3,2,1,0:T(8,128)(2,1)} %cand_k.3) | copy-start | bytes 1769476
  12.2 5.3 %copy-start.4 = (bf16[128]{0:T(256)(128)(2,1)S(1)}, bf16[128]{0:T(256)(128)(2,1)}, u32[]{:S(2)}) copy-start(bf16[128]{0:T(256)(128)(2,1)} %param.27) | copy-start | bytes 772
  12.2 5.3 %collective-permute-start.6 = (bf16[2,2,176,128]{3,2,1,0:T(8,128)(2,1)S(1)}, bf16[2,2,176,128]{3,2,1,0:T(8,128)(2,1)S(1)}, u32[]{:S(2)}, u32[]{:S(2)}) collective-permute-start(bf16[2,2,176,128]{3,2,1,0:T(8,128)(2,1)S(1)} %shard_map.161.mot), channel_id=1, source_target_pairs={{0,1},{1,0},{2,3},{3,2},{4,8},{5,9},{6,10},{7,11},{8,4},{9,5},{10,... | collective-permute-start | bytes 540680 | tf_op jit(solution)/shard_map/ppermute | solution.py:620
  14.1 3.5 %collective-permute-start.5 = (bf16[2,2,176,128]{3,2,1,0:T(8,128)(2,1)S(1)}, bf16[2,2,176,128]{3,2,1,0:T(8,128)(2,1)S(1)}, u32[]{:S(2)}, u32[]{:S(2)}) collective-permute-start(bf16[2,2,176,128]{3,2,1,0:T(8,128)(2,1)S(1)} %shard_map.161.mot), channel_id=1, source_target_pairs={{0,4},{4,0},{8,12},{12,8},{16,20},{20,16},{24,28},{28,24},{1,5},{5... | collective-permute-start | bytes 540680 | tf_op jit(solution)/shard_map/ppermute | solution.py:621

commit v8 on v7

--- a/solution.py
+++ b/solution.py
@@ -50,7 +50,7 @@
     rows[0], rows[1], rows[2] = first, scale, low
     for level in range(LEVELS):
         rows[3, STARTS[level] : STARTS[level] + counts[level]] = 0.5**level
-    return np.concatenate([pool, pool]).astype(jnp.bfloat16), rows
+    return pool.astype(jnp.bfloat16), rows
 
 
 def split(value):
@@ -100,11 +100,9 @@
     row_odd = lax.axis_index("row") % 2
     pairs = [(vox_h, vox), (disp_h, disp)]
     for v in range(2):
+        pairs.append((hidden_h.at[v], chip.at[v, 0:ROWS]))
         for target, y in ((chip, 1 - row_odd), (link, row_odd)):
-            pairs += [
-                (hidden_h.at[v], target.at[v, 0:ROWS]),
-                (context_h.at[v, y, :, UNITS : 2 * UNITS], target.at[v, ROWS]),
-            ]
+            pairs.append((context_h.at[v, y, :, UNITS : 2 * UNITS], target.at[v, ROWS]))
     data = len(pairs)
     pairs += [
         (first_h, first),
@@ -151,6 +149,8 @@
 
     for copy in copies[2:data]:
         copy.wait()
+    for v in range(2):
+        link[v, 0:ROWS] = chip[v, 0:ROWS]
     row_at = lax.broadcasted_iota(jnp.int32, (8, 128), 0)
     edges_right, edges_left = [], []
     for v in range(2):
@@ -200,8 +200,8 @@
     stacked = jnp.concatenate([w_high, b_high, w_high, b_mid, w_low, b_low], axis=0)
     block = jnp.concatenate([stacked, jnp.zeros((16, 256), F32)], axis=0).astype(BF)
     empty = jnp.zeros((64, 256), BF)
-    for k in range(4):
-        for m in range(4):
+    for k in range(2):
+        for m in range(2):
             w1[64 * k : 64 * k + 64, 256 * m : 256 * m + 256] = block if k == m else empty
     w1t[...] = jnp.concatenate([stacked, jnp.zeros((80, 256), F32)], axis=0).T.astype(BF)
     w2t[...] = w2[...].astype(F32).T.astype(BF)
@@ -276,8 +276,11 @@
         queries += [query, query[:16], jnp.zeros((16, 256), F32)]
 
     stacked = jnp.concatenate(queries, axis=0).T.astype(BF)
-    layer = silu_of_half(jnp.dot(stacked[:EXT], w1[...], preferred_element_type=F32)).astype(BF)
-    layer = jnp.concatenate([layer[:, 256 * k : 256 * k + 256] for k in range(4)], axis=0)
+    layers = []
+    for half in (stacked[:EXT, :128], stacked[:EXT, 128:]):
+        layer = silu_of_half(jnp.dot(half, w1[...], preferred_element_type=F32)).astype(BF)
+        layers += [layer[:, :256], layer[:, 256:]]
+    layer = jnp.concatenate(layers, axis=0)
     query_out[...] = jnp.dot(layer, w2[...], preferred_element_type=F32).astype(BF)
     match_out[...] = matched(windows, w1t, w2t)
 
@@ -331,7 +334,8 @@
         near = jnp.take_along_axis(source, place, axis=1, mode="promise_in_bounds")
         high, low = split(near)
         nears.append(jnp.concatenate([high.astype(BF), low.astype(BF)], axis=1))
-    pooled = jnp.dot(jnp.concatenate(nears, axis=0), pool[...], preferred_element_type=F32)
+    twice = jnp.concatenate([pool[...], pool[...]], axis=0)
+    pooled = jnp.dot(jnp.concatenate(nears, axis=0), twice, preferred_element_type=F32)
     looks = []
     for k in range(4):
         table = pooled[EXT * k : EXT * k + EXT]
@@ -556,7 +560,7 @@
             ((1, 256), F32),
             ((256, 256), BF),
             ((LEVELS * TAPS, 128), F32),
-            ((256, 256), BF),
+            ((128, 256), BF),
             ((8, 128), F32),
             ((1, 128), F32),
             ((1, 128), F32),
@@ -565,7 +569,7 @@
         in_specs=[pl.BlockSpec(memory_space=pltpu.MemorySpace.HBM)] * 12,
         scratch=[
             pltpu.VMEM((2, BINS, ROWS, TILE), F32),
-            pltpu.SemaphoreType.DMA((18,)),
+            pltpu.SemaphoreType.DMA((16,)),
         ],
         flops=10**6,
         bytes_accessed=2 * 10**6,
@@ -595,7 +599,7 @@
     chip_in = lax.ppermute(chip_out, "row", chip)
     w1, w1t, w2t, mw = call(
         weight_kernel,
-        [((256, 1024), BF), ((256, 128), BF), ((256, 256), BF), ((128, 128), BF)],
+        [((128, 512), BF), ((256, 128), BF), ((256, 256), BF), ((128, 128), BF)],
         flops=10**6,
         bytes_accessed=2 * 10**6,
     )(*raw)

time: 19.9 us -> 19.7 us (0.990)
  no operation moved by 1% of the time
where the time goes in v8:
time: 19.7 us; the launch traced here: 19.6 us
  starting transfers between devices  9.9 us (50%)
  Pallas kernels  7.26 us (37%)
  waiting for transfers between devices  1.67 us (8%)
  between operations  0.75 us (4%)
    ppermute x1, starting transfers between devices, local(): chip_in = lax.ppermute(chip_out, 'row', chip)  2.84 us
    pallas_call x1, Pallas kernels, local(): call(outer_kernel, [((2, ROWS, TILE, UNITS), BF), ((2, ROWS, TILE), F32)]...  2.21 us
    ppermute x1, starting transfers between devices, local(): odd_in = lax.ppermute(odd_out, 'col', odd)  2.13 us
    ppermute x1, starting transfers between devices, local(): mot_link = lax.ppermute(mot, ('row', 'col'), link)  1.83 us
    ppermute x1, waiting for transfers between devices, local(): mot_link = lax.ppermute(mot, ('row', 'col'), link)  1.66 us
    pallas_call x1, Pallas kernels, local(): call(motion_kernel, [((2, ROWS, EXT, UNITS), BF)], flops=10 ** 9, bytes_a...  1.41 us
    pallas_call x1, Pallas kernels, local(): call(pack_kernel, [((4, 32, 256), BF), ((80, 256), BF), ((80, 256), BF),...  1.38 us
    ppermute x1, starting transfers between devices, local(): even_in = lax.ppermute(even_out, ('row', 'col'), even)  1.3 us
  transfers between devices with their start and end apart: 7, of which 1 were waited for; matrix products, arithmetic and copies ran while one was open for 0% of the time, Pallas kernels for 19%

profile of v8, /device:TPU:1, one launch (start us, length us, event | category | flops | bytes accessed | tf_op | source)
XLA Modules:
  0.0 19.6 jit_solution(6800514946352035308)
XLA Ops:
  0.6 1.4 %shard_map.158 = (bf16[4,32,256]{2,1,0:T(8,128)(2,1)S(1)}, bf16[80,256]{1,0:T(8,128)(2,1)S(1)}, bf16[80,256]{1,0:T(8,128)(2,1)S(1)}, bf16[64,128]{1,0:T(8,128)(2...) custom-call(f32[2,15,2,160]{3,2,1,0:T(2,128)} %vox_h.1, ...), custom_call_target="tpu_custom_call" | custom-call | flops 1000000 | bytes 2000000 | tf_op jit(solution)/shard_map/pallas_call | solution.py:550
  2.0 2.1 %collective-permute-start.3 = (bf16[80,256]{1,0:T(8,128)(2,1)S(1)}, bf16[80,256]{1,0:T(8,128)(2,1)S(1)}, u32[]{:S(2)}, u32[]{:S(2)}) collective-permute-start(bf16[80,256]{1,0:T(8,128)(2,1)S(1)} %get-tuple-element.33), channel_id=1, source_target_pairs={{0,1},{1,0},{2,3},{3,2},{4,5},{5,4},{6,7},{7,6},{8,9},{9,8},{10,11... | collective-permute-start | bytes 122888 | tf_op jit(solution)/shard_map/ppermute | solution.py:596
  4.1 1.3 %collective-permute-start.4 = (bf16[80,256]{1,0:T(8,128)(2,1)S(1)}, bf16[80,256]{1,0:T(8,128)(2,1)S(1)}, u32[]{:S(2)}, u32[]{:S(2)}) collective-permute-start(bf16[80,256]{1,0:T(8,128)(2,1)S(1)} %get-tuple-element.34), channel_id=1, source_target_pairs={{0,4},{1,2},{2,1},{3,7},{4,0},{5,6},{6,5},{7,3},{8,12},{9,10},{10,... | collective-permute-start | bytes 122888 | tf_op jit(solution)/shard_map/ppermute | solution.py:597
  5.4 1.2 %collective-permute-start.2 = (bf16[64,128]{1,0:T(8,128)(2,1)S(1)}, bf16[64,128]{1,0:T(8,128)(2,1)S(1)}, u32[]{:S(2)}, u32[]{:S(2)}) collective-permute-start(bf16[64,128]{1,0:T(8,128)(2,1)S(1)} %get-tuple-element.31), channel_id=1, source_target_pairs={{0,2},{1,3},{2,0},{3,1},{4,6},{5,7},{6,4},{7,5},{8,10},{9,11},{10,... | collective-permute-start | bytes 49160 | tf_op jit(solution)/shard_map/ppermute | solution.py:595
  6.6 2.8 %collective-permute-start = (bf16[2,3,160,128]{3,2,1,0:T(8,128)(2,1)S(1)}, bf16[2,3,160,128]{3,2,1,0:T(8,128)(2,1)S(1)}, u32[]{:S(2)}, u32[]{:S(2)}) collective-permute-start(bf16[2,3,160,128]{3,2,1,0:T(8,128)(2,1)S(1)} %get-tuple-element.29), channel_id=1, source_target_pairs={{0,4},{4,0},{8,12},{12,8},{16,20},{20,16},{24,28},{28,24},{1,5},{5... | collective-permute-start | bytes 737288 | tf_op jit(solution)/shard_map/ppermute | solution.py:599
  9.4 0.0 collective-permute-start.1
  9.4 0.1 shard_map.159
  9.6 0.0 collective-permute-done.3.odd_in
  9.6 0.0 collective-permute-done.4.even_in
  9.6 1.0 %shard_map.160 = (bf16[704,256]{1,0:T(8,128)(2,1)S(1)}, bf16[256,1536]{1,0:T(8,128)(2,1)S(1)}, f32[176,8]{1,0:T(8,128)S(1)}, f32[2,16,256]{2,1,0:T(8,128)S(1)}) custom-call(bf16[4,32,256]{2,1,0:T(8,128)(2,1)S(1)} %get-tuple-element.32.own, bf16[80,256]{1,0:T(8,128)(2,1)S(1)} %collective-permute-done.3.odd_in, ...), custom_call_target="tpu_custom_call" | custom-call | flops 1000000000 | bytes 1000000 | tf_op jit(solution)/shard_map/pallas_call | solution.py:607
  10.6 0.0 collective-permute-done.2.far_in
  10.6 0.0 copy-start
  10.6 0.0 copy-start.1
  10.6 0.0 copy-start.2
  10.6 0.0 copy-start.3
  10.7 1.4 %shard_map.161.mot = bf16[2,2,176,128]{3,2,1,0:T(8,128)(2,1)S(1)} custom-call(bf16[64,128]{1,0:T(8,128)(2,1)S(1)} %collective-permute-done.2.far_in, bf16[704,256]{1,0:T(8,128)(2,1)S(1)} %get-tuple-element.43.query, bf16[256,1536]{1,0:T(8,128)(2,1)S(1)} %get-tuple-element.44.match, f32[176,8]{1,0:T(8,128)S(1)} %get-tuple-element.45.depths, ...), custom_call_target="tpu_custom_call" | custom-call | flops 1000000000 | bytes 1000000 | tf_op jit(solution)/shard_map/pallas_call | solution.py:618
  12.1 0.0 copy-start.4
  12.1 1.8 %collective-permute-start.6 = (bf16[2,2,176,128]{3,2,1,0:T(8,128)(2,1)S(1)}, bf16[2,2,176,128]{3,2,1,0:T(8,128)(2,1)S(1)}, u32[]{:S(2)}, u32[]{:S(2)}) collective-permute-start(bf16[2,2,176,128]{3,2,1,0:T(8,128)(2,1)S(1)} %shard_map.161.mot), channel_id=1, source_target_pairs={{0,1},{1,0},{2,3},{3,2},{4,8},{5,9},{6,10},{7,11},{8,4},{9,5},{10,... | collective-permute-start | bytes 540680 | tf_op jit(solution)/shard_map/ppermute | solution.py:624
  13.9 0.7 %collective-permute-start.5 = (bf16[2,2,176,128]{3,2,1,0:T(8,128)(2,1)S(1)}, bf16[2,2,176,128]{3,2,1,0:T(8,128)(2,1)S(1)}, u32[]{:S(2)}, u32[]{:S(2)}) collective-permute-start(bf16[2,2,176,128]{3,2,1,0:T(8,128)(2,1)S(1)} %shard_map.161.mot), channel_id=1, source_target_pairs={{0,4},{4,0},{8,12},{12,8},{16,20},{20,16},{24,28},{28,24},{1,5},{5... | collective-permute-start | bytes 540680 | tf_op jit(solution)/shard_map/ppermute | solution.py:625
  14.6 1.1 %shard_map.162 = (f32[2,2,176,256]{3,2,1,0:T(8,128)S(1)}, f32[2,2,176,128]{3,2,1,0:T(8,128)S(1)}, f32[2,2,160,128]{3,2,1,0:T(8,128)S(1)}, bf16[2,2,176,128]{3,2,1,0:T(8,128)(2,1)S(1)}) custom-call(bf16[2,2,160,128]{3,2,1,0:T(8,128)(2,1)S(1)} %copy-done.2, bf16[2,2,160,384]{3,2,1,0:T(8,128)(2,1)S(1)} %copy-done, bf16[2,2,176,128]{3,2,1,0:T(8,128)(2,1)S(1)} %shard_map.161.mot, ...), custom_call_target="tpu_custom_call" | custom-call | flops 1000000000 | bytes 4000000 | tf_op jit(solution)/shard_map/pallas_call | solution.py:626
  15.7 1.7 %collective-permute-done.6.mot_link = bf16[2,2,176,128]{3,2,1,0:T(8,128)(2,1)S(1)} collective-permute-done((bf16[2,2,176,128]{3,2,1,0:T(8,128)(2,1)S(1)}, bf16[2,2,176,128]{3,2,1,0:T(8,128)(2,1)S(1)}, u32[]{:S(2)}, u32[]{:S(2)}) %collective-permute-start.6) | collective-permute-done | bytes 180256 | tf_op jit(solution)/shard_map/ppermute | solution.py:624
  17.4 0.0 collective-permute-done.5.mot_chip
  17.4 0.0 collective-permute-done.chip_in
  17.4 2.2 %shard_map.163 = (bf16[2,2,160,128]{3,2,1,0:T(8,128)(2,1)}, f32[2,2,160]{2,1,0:T(2,128)}) custom-call(bf16[2,2,160,128]{3,2,1,0:T(8,128)(2,1)S(1)} %copy-done.2, bf16[2,2,160,384]{3,2,1,0:T(8,128)(2,1)S(1)} %copy-done, bf16[2,3,160,128]{3,2,1,0:T(8,128)(2,1)S(1)} %collective-permute-done.chip_in, ...), custom_call_target="tpu_custom_call" | custom-call | flops 1000000000 | bytes 4000000 | tf_op jit(solution)/shard_map/pallas_call | solution.py:638
  (6 shorter events, 0.0 us)
Async XLA Ops:
  2.0 7.6 %collective-permute-start.3 = (bf16[80,256]{1,0:T(8,128)(2,1)S(1)}, bf16[80,256]{1,0:T(8,128)(2,1)S(1)}, u32[]{:S(2)}, u32[]{:S(2)}) collective-permute-start(bf16[80,256]{1,0:T(8,128)(2,1)S(1)} %get-tuple-element.33), channel_id=1, source_target_pairs={{0,1},{1,0},{2,3},{3,2},{4,5},{5,4},{6,7},{7,6},{8,9},{9,8},{10,11... | collective-permute-start | bytes 122888 | tf_op jit(solution)/shard_map/ppermute | solution.py:596
  4.1 5.5 %collective-permute-start.4 = (bf16[80,256]{1,0:T(8,128)(2,1)S(1)}, bf16[80,256]{1,0:T(8,128)(2,1)S(1)}, u32[]{:S(2)}, u32[]{:S(2)}) collective-permute-start(bf16[80,256]{1,0:T(8,128)(2,1)S(1)} %get-tuple-element.34), channel_id=1, source_target_pairs={{0,4},{1,2},{2,1},{3,7},{4,0},{5,6},{6,5},{7,3},{8,12},{9,10},{10,... | collective-permute-start | bytes 122888 | tf_op jit(solution)/shard_map/ppermute | solution.py:597
  5.4 5.2 %collective-permute-start.2 = (bf16[64,128]{1,0:T(8,128)(2,1)S(1)}, bf16[64,128]{1,0:T(8,128)(2,1)S(1)}, u32[]{:S(2)}, u32[]{:S(2)}) collective-permute-start(bf16[64,128]{1,0:T(8,128)(2,1)S(1)} %get-tuple-element.31), channel_id=1, source_target_pairs={{0,2},{1,3},{2,0},{3,1},{4,6},{5,7},{6,4},{7,5},{8,10},{9,11},{10,... | collective-permute-start | bytes 49160 | tf_op jit(solution)/shard_map/ppermute | solution.py:595
  6.6 10.8 %collective-permute-start = (bf16[2,3,160,128]{3,2,1,0:T(8,128)(2,1)S(1)}, bf16[2,3,160,128]{3,2,1,0:T(8,128)(2,1)S(1)}, u32[]{:S(2)}, u32[]{:S(2)}) collective-permute-start(bf16[2,3,160,128]{3,2,1,0:T(8,128)(2,1)S(1)} %get-tuple-element.29), channel_id=1, source_target_pairs={{0,4},{4,0},{8,12},{12,8},{16,20},{20,16},{24,28},{28,24},{1,5},{5... | collective-permute-start | bytes 737288 | tf_op jit(solution)/shard_map/ppermute | solution.py:599
  9.4 8.0 %collective-permute-start.1 = (bf16[2,3,160,128]{3,2,1,0:T(8,128)(2,1)S(1)}, bf16[2,3,160,128]{3,2,1,0:T(8,128)(2,1)S(1)}, u32[]{:S(2)}, u32[]{:S(2)}) collective-permute-start(bf16[2,3,160,128]{3,2,1,0:T(8,128)(2,1)S(1)} %get-tuple-element.30), channel_id=1, source_target_pairs={{0,1},{1,0},{2,3},{3,2},{4,8},{5,9},{6,10},{7,11},{8,4},{9,5},{10,... | collective-permute-start | bytes 737288 | tf_op jit(solution)/shard_map/ppermute | solution.py:598
  10.6 4.0 %copy-start = (bf16[2,2,160,384]{3,2,1,0:T(8,128)(2,1)S(1)}, bf16[2,2,160,384]{3,2,1,0:T(8,128)(2,1)}, u32[]{:S(2)}) copy-start(bf16[2,2,160,384]{3,2,1,0:T(8,128)(2,1)} %context.3) | copy-start | bytes 1474564
  10.6 3.9 %copy-start.1 = (bf16[3,3,256,256]{3,2,1,0:T(8,128)(2,1)S(1)}, bf16[3,3,256,256]{3,2,1,0:T(8,128)(2,1)}, u32[]{:S(2)}) copy-start(bf16[3,3,256,256]{3,2,1,0:T(8,128)(2,1)} %gate_k.3) | copy-start | bytes 3538948
  10.6 3.9 %copy-start.2 = (bf16[2,2,160,128]{3,2,1,0:T(8,128)(2,1)S(1)}, bf16[2,2,160,128]{3,2,1,0:T(8,128)(2,1)}, u32[]{:S(2)}) copy-start(bf16[2,2,160,128]{3,2,1,0:T(8,128)(2,1)} %hidden.3) | copy-start | bytes 491524
  10.6 3.9 %copy-start.3 = (bf16[3,3,256,128]{3,2,1,0:T(8,128)(2,1)S(1)}, bf16[3,3,256,128]{3,2,1,0:T(8,128)(2,1)}, u32[]{:S(2)}) copy-start(bf16[3,3,256,128]{3,2,1,0:T(8,128)(2,1)} %cand_k.3) | copy-start | bytes 1769476
  12.1 5.3 %copy-start.4 = (bf16[128]{0:T(256)(128)(2,1)S(1)}, bf16[128]{0:T(256)(128)(2,1)}, u32[]{:S(2)}) copy-start(bf16[128]{0:T(256)(128)(2,1)} %param.27) | copy-start | bytes 772
  12.1 5.3 %collective-permute-start.6 = (bf16[2,2,176,128]{3,2,1,0:T(8,128)(2,1)S(1)}, bf16[2,2,176,128]{3,2,1,0:T(8,128)(2,1)S(1)}, u32[]{:S(2)}, u32[]{:S(2)}) collective-permute-start(bf16[2,2,176,128]{3,2,1,0:T(8,128)(2,1)S(1)} %shard_map.161.mot), channel_id=1, source_target_pairs={{0,1},{1,0},{2,3},{3,2},{4,8},{5,9},{6,10},{7,11},{8,4},{9,5},{10,... | collective-permute-start | bytes 540680 | tf_op jit(solution)/shard_map/ppermute | solution.py:624
  13.9 3.5 %collective-permute-start.5 = (bf16[2,2,176,128]{3,2,1,0:T(8,128)(2,1)S(1)}, bf16[2,2,176,128]{3,2,1,0:T(8,128)(2,1)S(1)}, u32[]{:S(2)}, u32[]{:S(2)}) collective-permute-start(bf16[2,2,176,128]{3,2,1,0:T(8,128)(2,1)S(1)} %shard_map.161.mot), channel_id=1, source_target_pairs={{0,4},{4,0},{8,12},{12,8},{16,20},{20,16},{24,28},{28,24},{1,5},{5... | collective-permute-start | bytes 540680 | tf_op jit(solution)/shard_map/ppermute | solution.py:625

commit v9 on v8

--- a/solution.py
+++ b/solution.py
@@ -222,7 +222,21 @@
 CASES = [(v, y) for v in range(2) for y in range(ROWS)]
 
 
-def close_kernel(own, odd_in, even_in, disp, w1, w1t, w2, w2t, query_out, match_out, depth_out, edge_out):
+def located(depth, v):
+    lane = lax.broadcasted_iota(jnp.int32, (EXT, 128), 1)
+    pixel = lax.broadcasted_iota(jnp.int32, (EXT, 1), 0).astype(F32)
+    spot = (pixel - PAD if v == 0 else (EXT - 1 - PAD) - pixel) - depth
+    eighth = jnp.floor(spot * 0.125)
+    start = (8.0 * eighth).astype(jnp.int32) + (128 + TILE - 32)
+    if v == 0:
+        block, place = (start + 127 - lane) >> 7, (start + lane) & 127
+    else:
+        index = (WINDOW - 1 - start) - lane
+        block, place = index >> 7, index & 127
+    return spot - 8.0 * eighth, block, place
+
+
+def close_kernel(own, odd_in, even_in, disp, w1, w1t, w2, w2t, query_out, near_out, depth_out, edge_out):
     col = lax.axis_index("col")
     is_even = col % 2 == 0
 
@@ -253,7 +267,8 @@
             )
         )
     depth_rows.append(jnp.zeros((4, 256), F32))
-    depth_out[...] = jnp.concatenate(depth_rows, axis=0).T[:EXT]
+    depths = jnp.concatenate(depth_rows, axis=0).T[:EXT]
+    depth_out[...] = depths
     edge_out[0] = edge_left
     edge_out[1] = edge_right
 
@@ -281,23 +296,34 @@
         layer = silu_of_half(jnp.dot(half, w1[...], preferred_element_type=F32)).astype(BF)
         layers += [layer[:, :256], layer[:, 256:]]
     layer = jnp.concatenate(layers, axis=0)
-    query_out[...] = jnp.dot(layer, w2[...], preferred_element_type=F32).astype(BF)
-    match_out[...] = matched(windows, w1t, w2t)
+    query = jnp.dot(layer, w2[...], preferred_element_type=F32).astype(BF)
+    query_out[...] = query
+    match = matched(windows, w1t, w2t)
+    for k, (v, y) in enumerate(CASES):
+        scores = jnp.dot(
+            query[EXT * k : EXT * k + EXT],
+            match[:, CLOSE * k : CLOSE * k + CLOSE],
+            preferred_element_type=F32,
+        )
+        _, block, _ = located(depths[:, k : k + 1], v)
+        source = scores[:, :128]
+        for m in range(1, CLOSE // 128):
+            at = m + 1 if v == 0 else m
+            source = jnp.where(block == at, scores[:, 128 * m : 128 * m + 128], source)
+        near_out[EXT * k : EXT * k + EXT, :] = source
 
 
 def motion_kernel(
-    far_in, query, match, depths, edges, w1t, w2t, mw, scale, bias, pool, rows, out
+    far_in, query, near_scores, depths, edges, w1t, w2t, mw, scale, bias, pool, rows, out
 ):
     col = lax.axis_index("col")
     first = rows[0:1, :].astype(jnp.int32)
     level_scale = rows[1:2, :]
     is_low = rows[2:3, :] > 0.5
     entry_scale = rows[3:4, :]
-    lane = lax.broadcasted_iota(jnp.int32, (EXT, 128), 1)
     pixel = lax.broadcasted_iota(jnp.int32, (EXT, 1), 0)
     column = pixel + (col * TILE - PAD)
     inside = (column >= 0) & (column < IMAGE)
-    pixel = pixel.astype(F32)
     depth_scale = scale[...] * (1.0 / 192.0)
     row_at = lax.broadcasted_iota(jnp.int32, (8, 128), 0)
 
@@ -311,26 +337,13 @@
     nears, rests = [], []
     for k, (v, y) in enumerate(CASES):
         features = query[EXT * k : EXT * k + EXT, :]
-        scores = jnp.dot(
-            features, match[:, CLOSE * k : CLOSE * k + CLOSE], preferred_element_type=F32
-        )
         far_scores = jnp.dot(
             features, far_match[:, 128 * k : 128 * k + 128], preferred_element_type=F32
         )
-        blocks = [scores[:, 128 * m : 128 * m + 128] for m in range(CLOSE // 128)]
-        blocks = [far_scores] + blocks if v == 0 else blocks + [far_scores]
-        spot = (pixel - PAD if v == 0 else (EXT - 1 - PAD) - pixel) - depths[:, k : k + 1]
-        eighth = jnp.floor(spot * 0.125)
-        rests.append(spot - 8.0 * eighth)
-        start = (8.0 * eighth).astype(jnp.int32) + (128 + TILE - 32)
-        if v == 0:
-            block, place = (start + 127 - lane) >> 7, (start + lane) & 127
-        else:
-            index = (WINDOW - 1 - start) - lane
-            block, place = index >> 7, index & 127
-        source = blocks[0]
-        for m in range(1, WINDOW // 128):
-            source = jnp.where(block == m, blocks[m], source)
+        rest, block, place = located(depths[:, k : k + 1], v)
+        rests.append(rest)
+        far_block = 0 if v == 0 else WINDOW // 128 - 1
+        source = jnp.where(block == far_block, far_scores, near_scores[EXT * k : EXT * k + EXT, :])
         near = jnp.take_along_axis(source, place, axis=1, mode="promise_in_bounds")
         high, low = split(near)
         nears.append(jnp.concatenate([high.astype(BF), low.astype(BF)], axis=1))
@@ -604,11 +617,11 @@
         bytes_accessed=2 * 10**6,
     )(*raw)
     w2 = raw[2]
-    query, match, depths, edges = call(
+    query, near, depths, edges = call(
         close_kernel,
         [
             ((4 * EXT, 256), BF),
-            ((256, 4 * CLOSE), BF),
+            ((4 * EXT, 128), F32),
             ((EXT, 8), F32),
             ((2, 16, 256), F32),
         ],
@@ -620,7 +633,7 @@
         [((2, ROWS, EXT, UNITS), BF)],
         flops=10**9,
         bytes_accessed=10**6,
-    )(far_in, query, match, depths, edges, w1t, w2t, mw, scale, bias, pool, lane_rows)
+    )(far_in, query, near, depths, edges, w1t, w2t, mw, scale, bias, pool, lane_rows)
     mot_link = lax.ppermute(mot, ("row", "col"), link)
     mot_chip = lax.ppermute(mot, "row", chip)
     gates, outer, cands, state = call(

time: 19.7 us -> 19.9 us (1.010)
  waiting for transfers between devices: 1.67 us -> 1.92 us
  starting transfers between devices: 9.9 us -> 9.66 us
    ppermute x1, waiting for transfers between devices: 1.66 us -> 1.9 us  [local(): mot_link = lax.ppermute(mot, ('row', 'col'), link)]
    ppermute x1, starting transfers between devices: 0.65 us -> 0.41 us  [local(): mot_chip = lax.ppermute(mot, 'row', chip)]
    pallas_call x1, Pallas kernels: 0.98 us -> 1.22 us  [local(): call(close_kernel, [((4 * EXT, 256), BF), ((4 * EXT, 128), F32), ((EXT, 8...]
  transfers between devices with their start and end apart: 7 -> 7, of which waited for: 1 -> 1; matrix products, arithmetic and copies ran while one was open for 0% -> 0% of each run, Pallas kernels for 19% -> 20%
where the time goes in v9:
time: 19.9 us; the launch traced here: 19.8 us
  starting transfers between devices  9.66 us (49%)
  Pallas kernels  7.45 us (37%)
  waiting for transfers between devices  1.92 us (10%)
  between operations  0.75 us (4%)
    ppermute x1, starting transfers between devices, local(): chip_in = lax.ppermute(chip_out, 'row', chip)  2.84 us
    pallas_call x1, Pallas kernels, local(): call(outer_kernel, [((2, ROWS, TILE, UNITS), BF), ((2, ROWS, TILE), F32)]...  2.2 us
    ppermute x1, starting transfers between devices, local(): odd_in = lax.ppermute(odd_out, 'col', odd)  2.13 us
    ppermute x1, waiting for transfers between devices, local(): mot_link = lax.ppermute(mot, ('row', 'col'), link)  1.9 us
    ppermute x1, starting transfers between devices, local(): mot_link = lax.ppermute(mot, ('row', 'col'), link)  1.83 us
    pallas_call x1, Pallas kernels, local(): call(pack_kernel, [((4, 32, 256), BF), ((80, 256), BF), ((80, 256), BF),...  1.38 us
    pallas_call x1, Pallas kernels, local(): call(motion_kernel, [((2, ROWS, EXT, UNITS), BF)], flops=10 ** 9, bytes_a...  1.36 us
    ppermute x1, starting transfers between devices, local(): even_in = lax.ppermute(even_out, ('row', 'col'), even)  1.3 us
  transfers between devices with their start and end apart: 7, of which 1 were waited for; matrix products, arithmetic and copies ran while one was open for 0% of the time, Pallas kernels for 20%

profile of v9, /device:TPU:1, one launch (start us, length us, event | category | flops | bytes accessed | tf_op | source)
XLA Modules:
  0.0 19.8 jit_solution(9243369087011301542)
XLA Ops:
  0.6 1.4 %shard_map.158 = (bf16[4,32,256]{2,1,0:T(8,128)(2,1)S(1)}, bf16[80,256]{1,0:T(8,128)(2,1)S(1)}, bf16[80,256]{1,0:T(8,128)(2,1)S(1)}, bf16[64,128]{1,0:T(8,128)(2...) custom-call(f32[2,15,2,160]{3,2,1,0:T(2,128)} %vox_h.1, ...), custom_call_target="tpu_custom_call" | custom-call | flops 1000000 | bytes 2000000 | tf_op jit(solution)/shard_map/pallas_call | solution.py:563
  2.0 2.1 %collective-permute-start.3 = (bf16[80,256]{1,0:T(8,128)(2,1)S(1)}, bf16[80,256]{1,0:T(8,128)(2,1)S(1)}, u32[]{:S(2)}, u32[]{:S(2)}) collective-permute-start(bf16[80,256]{1,0:T(8,128)(2,1)S(1)} %get-tuple-element.33), channel_id=1, source_target_pairs={{0,1},{1,0},{2,3},{3,2},{4,5},{5,4},{6,7},{7,6},{8,9},{9,8},{10,11... | collective-permute-start | bytes 122888 | tf_op jit(solution)/shard_map/ppermute | solution.py:609
  4.1 1.3 %collective-permute-start.4 = (bf16[80,256]{1,0:T(8,128)(2,1)S(1)}, bf16[80,256]{1,0:T(8,128)(2,1)S(1)}, u32[]{:S(2)}, u32[]{:S(2)}) collective-permute-start(bf16[80,256]{1,0:T(8,128)(2,1)S(1)} %get-tuple-element.34), channel_id=1, source_target_pairs={{0,4},{1,2},{2,1},{3,7},{4,0},{5,6},{6,5},{7,3},{8,12},{9,10},{10,... | collective-permute-start | bytes 122888 | tf_op jit(solution)/shard_map/ppermute | solution.py:610
  5.4 1.2 %collective-permute-start.2 = (bf16[64,128]{1,0:T(8,128)(2,1)S(1)}, bf16[64,128]{1,0:T(8,128)(2,1)S(1)}, u32[]{:S(2)}, u32[]{:S(2)}) collective-permute-start(bf16[64,128]{1,0:T(8,128)(2,1)S(1)} %get-tuple-element.31), channel_id=1, source_target_pairs={{0,2},{1,3},{2,0},{3,1},{4,6},{5,7},{6,4},{7,5},{8,10},{9,11},{10,... | collective-permute-start | bytes 49160 | tf_op jit(solution)/shard_map/ppermute | solution.py:608
  6.6 2.8 %collective-permute-start = (bf16[2,3,160,128]{3,2,1,0:T(8,128)(2,1)S(1)}, bf16[2,3,160,128]{3,2,1,0:T(8,128)(2,1)S(1)}, u32[]{:S(2)}, u32[]{:S(2)}) collective-permute-start(bf16[2,3,160,128]{3,2,1,0:T(8,128)(2,1)S(1)} %get-tuple-element.29), channel_id=1, source_target_pairs={{0,4},{4,0},{8,12},{12,8},{16,20},{20,16},{24,28},{28,24},{1,5},{5... | collective-permute-start | bytes 737288 | tf_op jit(solution)/shard_map/ppermute | solution.py:612
  9.4 0.0 collective-permute-start.1
  9.4 0.1 shard_map.159
  9.6 0.0 collective-permute-done.3.odd_in
  9.6 0.0 collective-permute-done.4.even_in
  9.6 1.2 %shard_map.160 = (bf16[704,256]{1,0:T(8,128)(2,1)S(1)}, f32[704,128]{1,0:T(8,128)S(1)}, f32[176,8]{1,0:T(8,128)S(1)}, f32[2,16,256]{2,1,0:T(8,128)S(1)}) custom-call(bf16[4,32,256]{2,1,0:T(8,128)(2,1)S(1)} %get-tuple-element.32.own, bf16[80,256]{1,0:T(8,128)(2,1)S(1)} %collective-permute-done.3.odd_in, bf16[80,256]{1,0:T(8,128)(2,1)S(1)} %collective-permute-done.4.even_in, ...), custom_call_target="tpu_custom_call" | custom-call | flops 1000000000 | bytes 1000000 | tf_op jit(solution)/shard_map/pallas_call | solution.py:620
  10.8 0.0 collective-permute-done.2.far_in
  10.9 0.0 copy-start
  10.9 0.0 copy-start.1
  10.9 0.0 copy-start.2
  10.9 0.0 copy-start.3
  10.9 1.4 %shard_map.161.mot = bf16[2,2,176,128]{3,2,1,0:T(8,128)(2,1)S(1)} custom-call(bf16[64,128]{1,0:T(8,128)(2,1)S(1)} %collective-permute-done.2.far_in, bf16[704,256]{1,0:T(8,128)(2,1)S(1)} %get-tuple-element.43.query, f32[704,128]{1,0:T(8,128)S(1)} %get-tuple-element.44.near_scores, f32[176,8]{1,0:T(8,128)S(1)} %get-tuple-element.45.depths, ...), custom_call_target="tpu_custom_call" | custom-call | flops 1000000000 | bytes 1000000 | tf_op jit(solution)/shard_map/pallas_call | solution.py:631
  12.3 0.0 copy-start.4
  12.3 1.8 %collective-permute-start.6 = (bf16[2,2,176,128]{3,2,1,0:T(8,128)(2,1)S(1)}, bf16[2,2,176,128]{3,2,1,0:T(8,128)(2,1)S(1)}, u32[]{:S(2)}, u32[]{:S(2)}) collective-permute-start(bf16[2,2,176,128]{3,2,1,0:T(8,128)(2,1)S(1)} %shard_map.161.mot), channel_id=1, source_target_pairs={{0,1},{1,0},{2,3},{3,2},{4,8},{5,9},{6,10},{7,11},{8,4},{9,5},{10,... | collective-permute-start | bytes 540680 | tf_op jit(solution)/shard_map/ppermute | solution.py:637
  14.1 0.4 %collective-permute-start.5 = (bf16[2,2,176,128]{3,2,1,0:T(8,128)(2,1)S(1)}, bf16[2,2,176,128]{3,2,1,0:T(8,128)(2,1)S(1)}, u32[]{:S(2)}, u32[]{:S(2)}) collective-permute-start(bf16[2,2,176,128]{3,2,1,0:T(8,128)(2,1)S(1)} %shard_map.161.mot), channel_id=1, source_target_pairs={{0,4},{4,0},{8,12},{12,8},{16,20},{20,16},{24,28},{28,24},{1,5},{5... | collective-permute-start | bytes 540680 | tf_op jit(solution)/shard_map/ppermute | solution.py:638
  14.5 1.1 %shard_map.162 = (f32[2,2,176,256]{3,2,1,0:T(8,128)S(1)}, f32[2,2,176,128]{3,2,1,0:T(8,128)S(1)}, f32[2,2,160,128]{3,2,1,0:T(8,128)S(1)}, bf16[2,2,176,128]{3,2,1,0:T(8,128)(2,1)S(1)}) custom-call(bf16[2,2,160,128]{3,2,1,0:T(8,128)(2,1)S(1)} %copy-done.2, bf16[2,2,160,384]{3,2,1,0:T(8,128)(2,1)S(1)} %copy-done, bf16[2,2,176,128]{3,2,1,0:T(8,128)(2,1)S(1)} %shard_map.161.mot, ...), custom_call_target="tpu_custom_call" | custom-call | flops 1000000000 | bytes 4000000 | tf_op jit(solution)/shard_map/pallas_call | solution.py:639
  15.7 1.9 %collective-permute-done.6.mot_link = bf16[2,2,176,128]{3,2,1,0:T(8,128)(2,1)S(1)} collective-permute-done((bf16[2,2,176,128]{3,2,1,0:T(8,128)(2,1)S(1)}, bf16[2,2,176,128]{3,2,1,0:T(8,128)(2,1)S(1)}, u32[]{:S(2)}, u32[]{:S(2)}) %collective-permute-start.6) | collective-permute-done | bytes 180256 | tf_op jit(solution)/shard_map/ppermute | solution.py:637
  17.6 0.0 collective-permute-done.5.mot_chip
  17.6 0.0 collective-permute-done.chip_in
  17.6 2.2 %shard_map.163 = (bf16[2,2,160,128]{3,2,1,0:T(8,128)(2,1)}, f32[2,2,160]{2,1,0:T(2,128)}) custom-call(bf16[2,2,160,128]{3,2,1,0:T(8,128)(2,1)S(1)} %copy-done.2, bf16[2,2,160,384]{3,2,1,0:T(8,128)(2,1)S(1)} %copy-done, bf16[2,3,160,128]{3,2,1,0:T(8,128)(2,1)S(1)} %collective-permute-done.chip_in, ...), custom_call_target="tpu_custom_call" | custom-call | flops 1000000000 | bytes 4000000 | tf_op jit(solution)/shard_map/pallas_call | solution.py:651
  (6 shorter events, 0.0 us)
Async XLA Ops:
  2.0 7.6 %collective-permute-start.3 = (bf16[80,256]{1,0:T(8,128)(2,1)S(1)}, bf16[80,256]{1,0:T(8,128)(2,1)S(1)}, u32[]{:S(2)}, u32[]{:S(2)}) collective-permute-start(bf16[80,256]{1,0:T(8,128)(2,1)S(1)} %get-tuple-element.33), channel_id=1, source_target_pairs={{0,1},{1,0},{2,3},{3,2},{4,5},{5,4},{6,7},{7,6},{8,9},{9,8},{10,11... | collective-permute-start | bytes 122888 | tf_op jit(solution)/shard_map/ppermute | solution.py:609
  4.1 5.5 %collective-permute-start.4 = (bf16[80,256]{1,0:T(8,128)(2,1)S(1)}, bf16[80,256]{1,0:T(8,128)(2,1)S(1)}, u32[]{:S(2)}, u32[]{:S(2)}) collective-permute-start(bf16[80,256]{1,0:T(8,128)(2,1)S(1)} %get-tuple-element.34), channel_id=1, source_target_pairs={{0,4},{1,2},{2,1},{3,7},{4,0},{5,6},{6,5},{7,3},{8,12},{9,10},{10,... | collective-permute-start | bytes 122888 | tf_op jit(solution)/shard_map/ppermute | solution.py:610
  5.4 5.4 %collective-permute-start.2 = (bf16[64,128]{1,0:T(8,128)(2,1)S(1)}, bf16[64,128]{1,0:T(8,128)(2,1)S(1)}, u32[]{:S(2)}, u32[]{:S(2)}) collective-permute-start(bf16[64,128]{1,0:T(8,128)(2,1)S(1)} %get-tuple-element.31), channel_id=1, source_target_pairs={{0,2},{1,3},{2,0},{3,1},{4,6},{5,7},{6,4},{7,5},{8,10},{9,11},{10,... | collective-permute-start | bytes 49160 | tf_op jit(solution)/shard_map/ppermute | solution.py:608
  6.6 11.0 %collective-permute-start = (bf16[2,3,160,128]{3,2,1,0:T(8,128)(2,1)S(1)}, bf16[2,3,160,128]{3,2,1,0:T(8,128)(2,1)S(1)}, u32[]{:S(2)}, u32[]{:S(2)}) collective-permute-start(bf16[2,3,160,128]{3,2,1,0:T(8,128)(2,1)S(1)} %get-tuple-element.29), channel_id=1, source_target_pairs={{0,4},{4,0},{8,12},{12,8},{16,20},{20,16},{24,28},{28,24},{1,5},{5... | collective-permute-start | bytes 737288 | tf_op jit(solution)/shard_map/ppermute | solution.py:612
  9.4 8.1 %collective-permute-start.1 = (bf16[2,3,160,128]{3,2,1,0:T(8,128)(2,1)S(1)}, bf16[2,3,160,128]{3,2,1,0:T(8,128)(2,1)S(1)}, u32[]{:S(2)}, u32[]{:S(2)}) collective-permute-start(bf16[2,3,160,128]{3,2,1,0:T(8,128)(2,1)S(1)} %get-tuple-element.30), channel_id=1, source_target_pairs={{0,1},{1,0},{2,3},{3,2},{4,8},{5,9},{6,10},{7,11},{8,4},{9,5},{10,... | collective-permute-start | bytes 737288 | tf_op jit(solution)/shard_map/ppermute | solution.py:611
  10.9 3.7 %copy-start = (bf16[2,2,160,384]{3,2,1,0:T(8,128)(2,1)S(1)}, bf16[2,2,160,384]{3,2,1,0:T(8,128)(2,1)}, u32[]{:S(2)}) copy-start(bf16[2,2,160,384]{3,2,1,0:T(8,128)(2,1)} %context.3) | copy-start | bytes 1474564
  10.9 3.7 %copy-start.1 = (bf16[3,3,256,256]{3,2,1,0:T(8,128)(2,1)S(1)}, bf16[3,3,256,256]{3,2,1,0:T(8,128)(2,1)}, u32[]{:S(2)}) copy-start(bf16[3,3,256,256]{3,2,1,0:T(8,128)(2,1)} %gate_k.3) | copy-start | bytes 3538948
  10.9 3.6 %copy-start.2 = (bf16[2,2,160,128]{3,2,1,0:T(8,128)(2,1)S(1)}, bf16[2,2,160,128]{3,2,1,0:T(8,128)(2,1)}, u32[]{:S(2)}) copy-start(bf16[2,2,160,128]{3,2,1,0:T(8,128)(2,1)} %hidden.3) | copy-start | bytes 491524
  10.9 3.6 %copy-start.3 = (bf16[3,3,256,128]{3,2,1,0:T(8,128)(2,1)S(1)}, bf16[3,3,256,128]{3,2,1,0:T(8,128)(2,1)}, u32[]{:S(2)}) copy-start(bf16[3,3,256,128]{3,2,1,0:T(8,128)(2,1)} %cand_k.3) | copy-start | bytes 1769476
  12.3 5.3 %copy-start.4 = (bf16[128]{0:T(256)(128)(2,1)S(1)}, bf16[128]{0:T(256)(128)(2,1)}, u32[]{:S(2)}) copy-start(bf16[128]{0:T(256)(128)(2,1)} %param.27) | copy-start | bytes 772
  12.3 5.3 %collective-permute-start.6 = (bf16[2,2,176,128]{3,2,1,0:T(8,128)(2,1)S(1)}, bf16[2,2,176,128]{3,2,1,0:T(8,128)(2,1)S(1)}, u32[]{:S(2)}, u32[]{:S(2)}) collective-permute-start(bf16[2,2,176,128]{3,2,1,0:T(8,128)(2,1)S(1)} %shard_map.161.mot), channel_id=1, source_target_pairs={{0,1},{1,0},{2,3},{3,2},{4,8},{5,9},{6,10},{7,11},{8,4},{9,5},{10,... | collective-permute-start | bytes 540680 | tf_op jit(solution)/shard_map/ppermute | solution.py:637
  14.1 3.5 %collective-permute-start.5 = (bf16[2,2,176,128]{3,2,1,0:T(8,128)(2,1)S(1)}, bf16[2,2,176,128]{3,2,1,0:T(8,128)(2,1)S(1)}, u32[]{:S(2)}, u32[]{:S(2)}) collective-permute-start(bf16[2,2,176,128]{3,2,1,0:T(8,128)(2,1)S(1)} %shard_map.161.mot), channel_id=1, source_target_pairs={{0,4},{4,0},{8,12},{12,8},{16,20},{20,16},{24,28},{28,24},{1,5},{5... | collective-permute-start | bytes 540680 | tf_op jit(solution)/shard_map/ppermute | solution.py:638

commit v10 on v8

--- a/solution.py
+++ b/solution.py
@@ -193,7 +193,7 @@
         copy.wait()
 
 
-def weight_kernel(first, bias, w2, motion, w1, w1t, w2t, mw):
+def prepare_weights(first, bias, w2, motion, w1, w1t, w2t, mw):
     w_high, w_low = split(first[...] * 0.5)
     b_high, rest = split(bias[...] * 0.5)
     b_mid, b_low = split(rest)
@@ -222,7 +222,25 @@
 CASES = [(v, y) for v in range(2) for y in range(ROWS)]
 
 
-def close_kernel(own, odd_in, even_in, disp, w1, w1t, w2, w2t, query_out, match_out, depth_out, edge_out):
+def close_kernel(
+    own,
+    odd_in,
+    even_in,
+    disp,
+    first_layer,
+    bias,
+    w2,
+    motion,
+    query_out,
+    match_out,
+    depth_out,
+    edge_out,
+    w1t,
+    w2t,
+    mw,
+    w1,
+):
+    prepare_weights(first_layer, bias, w2, motion, w1, w1t, w2t, mw)
     col = lax.axis_index("col")
     is_even = col % 2 == 0
 
@@ -597,24 +615,21 @@
     even_in = lax.ppermute(even_out, ("row", "col"), even)
     link_in = lax.ppermute(link_out, ("row", "col"), link)
     chip_in = lax.ppermute(chip_out, "row", chip)
-    w1, w1t, w2t, mw = call(
-        weight_kernel,
-        [((128, 512), BF), ((256, 128), BF), ((256, 256), BF), ((128, 128), BF)],
-        flops=10**6,
-        bytes_accessed=2 * 10**6,
-    )(*raw)
-    w2 = raw[2]
-    query, match, depths, edges = call(
+    query, match, depths, edges, w1t, w2t, mw = call(
         close_kernel,
         [
             ((4 * EXT, 256), BF),
             ((256, 4 * CLOSE), BF),
             ((EXT, 8), F32),
             ((2, 16, 256), F32),
+            ((256, 128), BF),
+            ((256, 256), BF),
+            ((128, 128), BF),
         ],
+        scratch=[pltpu.VMEM((128, 512), BF)],
         flops=10**9,
         bytes_accessed=10**6,
-    )(own, odd_in, even_in, disp, w1, w1t, w2, w2t)
+    )(own, odd_in, even_in, disp, *raw)
     (mot,) = call(
         motion_kernel,
         [((2, ROWS, EXT, UNITS), BF)],

time: 19.7 us -> 19.6 us (level)
  transfers between devices with their start and end apart: 7 -> 7, of which waited for: 1 -> 1; matrix products, arithmetic and copies ran while one was open for 0% -> 0% of each run, Pallas kernels for 19% -> 18%
where the time goes in v10:
time: 19.6 us; the launch traced here: 19.5 us
  starting transfers between devices  10 us (51%)
  Pallas kernels  7.13 us (36%)
  waiting for transfers between devices  1.57 us (8%)
  between operations  0.73 us (4%)
    ppermute x1, starting transfers between devices, local(): chip_in = lax.ppermute(chip_out, 'row', chip)  2.84 us
    pallas_call x1, Pallas kernels, local(): call(outer_kernel, [((2, ROWS, TILE, UNITS), BF), ((2, ROWS, TILE), F32)]...  2.2 us
    ppermute x1, starting transfers between devices, local(): odd_in = lax.ppermute(odd_out, 'col', odd)  2.13 us
    ppermute x1, starting transfers between devices, local(): mot_link = lax.ppermute(mot, ('row', 'col'), link)  1.83 us
    ppermute x1, waiting for transfers between devices, local(): mot_link = lax.ppermute(mot, ('row', 'col'), link)  1.56 us
    pallas_call x1, Pallas kernels, local(): call(motion_kernel, [((2, ROWS, EXT, UNITS), BF)], flops=10 ** 9, bytes_a...  1.4 us
    pallas_call x1, Pallas kernels, local(): call(pack_kernel, [((4, 32, 256), BF), ((80, 256), BF), ((80, 256), BF),...  1.38 us
    ppermute x1, starting transfers between devices, local(): even_in = lax.ppermute(even_out, ('row', 'col'), even)  1.3 us
  transfers between devices with their start and end apart: 7, of which 1 were waited for; matrix products, arithmetic and copies ran while one was open for 0% of the time, Pallas kernels for 18%

profile of v10, /device:TPU:1, one launch (start us, length us, event | category | flops | bytes accessed | tf_op | source)
XLA Modules:
  0.0 19.5 jit_solution(6939614543848026010)
XLA Ops:
  0.6 1.4 %shard_map.158 = (bf16[4,32,256]{2,1,0:T(8,128)(2,1)S(1)}, bf16[80,256]{1,0:T(8,128)(2,1)S(1)}, bf16[80,256]{1,0:T(8,128)(2,1)S(1)}, bf16[64,128]{1,0:T(8,128)(2...) custom-call(f32[2,15,2,160]{3,2,1,0:T(2,128)} %vox_h.1, ...), custom_call_target="tpu_custom_call" | custom-call | flops 1000000 | bytes 2000000 | tf_op jit(solution)/shard_map/pallas_call | solution.py:568
  2.0 2.1 %collective-permute-start.3 = (bf16[80,256]{1,0:T(8,128)(2,1)S(1)}, bf16[80,256]{1,0:T(8,128)(2,1)S(1)}, u32[]{:S(2)}, u32[]{:S(2)}) collective-permute-start(bf16[80,256]{1,0:T(8,128)(2,1)S(1)} %get-tuple-element.32), channel_id=1, source_target_pairs={{0,1},{1,0},{2,3},{3,2},{4,5},{5,4},{6,7},{7,6},{8,9},{9,8},{10,11... | collective-permute-start | bytes 122888 | tf_op jit(solution)/shard_map/ppermute | solution.py:614
  4.1 1.3 %collective-permute-start.4 = (bf16[80,256]{1,0:T(8,128)(2,1)S(1)}, bf16[80,256]{1,0:T(8,128)(2,1)S(1)}, u32[]{:S(2)}, u32[]{:S(2)}) collective-permute-start(bf16[80,256]{1,0:T(8,128)(2,1)S(1)} %get-tuple-element.33), channel_id=1, source_target_pairs={{0,4},{1,2},{2,1},{3,7},{4,0},{5,6},{6,5},{7,3},{8,12},{9,10},{10,... | collective-permute-start | bytes 122888 | tf_op jit(solution)/shard_map/ppermute | solution.py:615
  5.4 1.2 %collective-permute-start.2 = (bf16[64,128]{1,0:T(8,128)(2,1)S(1)}, bf16[64,128]{1,0:T(8,128)(2,1)S(1)}, u32[]{:S(2)}, u32[]{:S(2)}) collective-permute-start(bf16[64,128]{1,0:T(8,128)(2,1)S(1)} %get-tuple-element.30), channel_id=1, source_target_pairs={{0,2},{1,3},{2,0},{3,1},{4,6},{5,7},{6,4},{7,5},{8,10},{9,11},{10,... | collective-permute-start | bytes 49160 | tf_op jit(solution)/shard_map/ppermute | solution.py:613
  6.6 2.8 %collective-permute-start = (bf16[2,3,160,128]{3,2,1,0:T(8,128)(2,1)S(1)}, bf16[2,3,160,128]{3,2,1,0:T(8,128)(2,1)S(1)}, u32[]{:S(2)}, u32[]{:S(2)}) collective-permute-start(bf16[2,3,160,128]{3,2,1,0:T(8,128)(2,1)S(1)} %get-tuple-element.28), channel_id=1, source_target_pairs={{0,4},{4,0},{8,12},{12,8},{16,20},{20,16},{24,28},{28,24},{1,5},{5... | collective-permute-start | bytes 737288 | tf_op jit(solution)/shard_map/ppermute | solution.py:617
  9.4 0.0 collective-permute-start.1
  9.4 0.0 collective-permute-done.3.odd_in
  9.4 0.0 collective-permute-done.4.even_in
  9.5 1.0 %shard_map.159 = (bf16[704,256]{1,0:T(8,128)(2,1)S(1)}, bf16[256,1536]{1,0:T(8,128)(2,1)S(1)}, f32[176,8]{1,0:T(8,128)S(1)}, f32[2,16,256]{2,1,0:T(8,128)S(1)}, ...) custom-call(bf16[4,32,256]{2,1,0:T(8,128)(2,1)S(1)} %get-tuple-element.31.own, ...), custom_call_target="tpu_custom_call" | custom-call | flops 1000000000 | bytes 1000000 | tf_op jit(solution)/shard_map/pallas_call | solution.py:618
  10.5 0.0 collective-permute-done.2.far_in
  10.5 0.0 copy-start
  10.5 0.0 copy-start.1
  10.5 0.0 copy-start.2
  10.5 0.0 copy-start.3
  10.5 1.4 %shard_map.160.mot = bf16[2,2,176,128]{3,2,1,0:T(8,128)(2,1)S(1)} custom-call(bf16[64,128]{1,0:T(8,128)(2,1)S(1)} %collective-permute-done.2.far_in, bf16[704,256]{1,0:T(8,128)(2,1)S(1)} %get-tuple-element.39.query, bf16[256,1536]{1,0:T(8,128)(2,1)S(1)} %get-tuple-element.40.match, f32[176,8]{1,0:T(8,128)S(1)} %get-tuple-element.41.depths, ...), custom_call_target="tpu_custom_call" | custom-call | flops 1000000000 | bytes 1000000 | tf_op jit(solution)/shard_map/pallas_call | solution.py:633
  11.9 0.0 copy-start.4
  11.9 1.8 %collective-permute-start.6 = (bf16[2,2,176,128]{3,2,1,0:T(8,128)(2,1)S(1)}, bf16[2,2,176,128]{3,2,1,0:T(8,128)(2,1)S(1)}, u32[]{:S(2)}, u32[]{:S(2)}) collective-permute-start(bf16[2,2,176,128]{3,2,1,0:T(8,128)(2,1)S(1)} %shard_map.160.mot), channel_id=1, source_target_pairs={{0,1},{1,0},{2,3},{3,2},{4,8},{5,9},{6,10},{7,11},{8,4},{9,5},{10,... | collective-permute-start | bytes 540680 | tf_op jit(solution)/shard_map/ppermute | solution.py:639
  13.8 0.8 %collective-permute-start.5 = (bf16[2,2,176,128]{3,2,1,0:T(8,128)(2,1)S(1)}, bf16[2,2,176,128]{3,2,1,0:T(8,128)(2,1)S(1)}, u32[]{:S(2)}, u32[]{:S(2)}) collective-permute-start(bf16[2,2,176,128]{3,2,1,0:T(8,128)(2,1)S(1)} %shard_map.160.mot), channel_id=1, source_target_pairs={{0,4},{4,0},{8,12},{12,8},{16,20},{20,16},{24,28},{28,24},{1,5},{5... | collective-permute-start | bytes 540680 | tf_op jit(solution)/shard_map/ppermute | solution.py:640
  14.6 1.1 %shard_map.161 = (f32[2,2,176,256]{3,2,1,0:T(8,128)S(1)}, f32[2,2,176,128]{3,2,1,0:T(8,128)S(1)}, f32[2,2,160,128]{3,2,1,0:T(8,128)S(1)}, bf16[2,2,176,128]{3,2,1,0:T(8,128)(2,1)S(1)}) custom-call(bf16[2,2,160,128]{3,2,1,0:T(8,128)(2,1)S(1)} %copy-done.2, bf16[2,2,160,384]{3,2,1,0:T(8,128)(2,1)S(1)} %copy-done, bf16[2,2,176,128]{3,2,1,0:T(8,128)(2,1)S(1)} %shard_map.160.mot, ...), custom_call_target="tpu_custom_call" | custom-call | flops 1000000000 | bytes 4000000 | tf_op jit(solution)/shard_map/pallas_call | solution.py:641
  15.7 1.6 %collective-permute-done.6.mot_link = bf16[2,2,176,128]{3,2,1,0:T(8,128)(2,1)S(1)} collective-permute-done((bf16[2,2,176,128]{3,2,1,0:T(8,128)(2,1)S(1)}, bf16[2,2,176,128]{3,2,1,0:T(8,128)(2,1)S(1)}, u32[]{:S(2)}, u32[]{:S(2)}) %collective-permute-start.6) | collective-permute-done | bytes 180256 | tf_op jit(solution)/shard_map/ppermute | solution.py:639
  17.3 0.0 collective-permute-done.5.mot_chip
  17.3 0.0 collective-permute-done.chip_in
  17.3 0.0 collective-permute-done.1.link_in
  17.3 2.2 %shard_map.162 = (bf16[2,2,160,128]{3,2,1,0:T(8,128)(2,1)}, f32[2,2,160]{2,1,0:T(2,128)}) custom-call(bf16[2,2,160,128]{3,2,1,0:T(8,128)(2,1)S(1)} %copy-done.2, bf16[2,2,160,384]{3,2,1,0:T(8,128)(2,1)S(1)} %copy-done, bf16[2,3,160,128]{3,2,1,0:T(8,128)(2,1)S(1)} %collective-permute-done.chip_in, ...), custom_call_target="tpu_custom_call" | custom-call | flops 1000000000 | bytes 4000000 | tf_op jit(solution)/shard_map/pallas_call | solution.py:653
  (5 shorter events, 0.0 us)
Async XLA Ops:
  2.0 7.4 %collective-permute-start.3 = (bf16[80,256]{1,0:T(8,128)(2,1)S(1)}, bf16[80,256]{1,0:T(8,128)(2,1)S(1)}, u32[]{:S(2)}, u32[]{:S(2)}) collective-permute-start(bf16[80,256]{1,0:T(8,128)(2,1)S(1)} %get-tuple-element.32), channel_id=1, source_target_pairs={{0,1},{1,0},{2,3},{3,2},{4,5},{5,4},{6,7},{7,6},{8,9},{9,8},{10,11... | collective-permute-start | bytes 122888 | tf_op jit(solution)/shard_map/ppermute | solution.py:614
  4.1 5.3 %collective-permute-start.4 = (bf16[80,256]{1,0:T(8,128)(2,1)S(1)}, bf16[80,256]{1,0:T(8,128)(2,1)S(1)}, u32[]{:S(2)}, u32[]{:S(2)}) collective-permute-start(bf16[80,256]{1,0:T(8,128)(2,1)S(1)} %get-tuple-element.33), channel_id=1, source_target_pairs={{0,4},{1,2},{2,1},{3,7},{4,0},{5,6},{6,5},{7,3},{8,12},{9,10},{10,... | collective-permute-start | bytes 122888 | tf_op jit(solution)/shard_map/ppermute | solution.py:615
  5.4 5.0 %collective-permute-start.2 = (bf16[64,128]{1,0:T(8,128)(2,1)S(1)}, bf16[64,128]{1,0:T(8,128)(2,1)S(1)}, u32[]{:S(2)}, u32[]{:S(2)}) collective-permute-start(bf16[64,128]{1,0:T(8,128)(2,1)S(1)} %get-tuple-element.30), channel_id=1, source_target_pairs={{0,2},{1,3},{2,0},{3,1},{4,6},{5,7},{6,4},{7,5},{8,10},{9,11},{10,... | collective-permute-start | bytes 49160 | tf_op jit(solution)/shard_map/ppermute | solution.py:613
  6.6 10.7 %collective-permute-start = (bf16[2,3,160,128]{3,2,1,0:T(8,128)(2,1)S(1)}, bf16[2,3,160,128]{3,2,1,0:T(8,128)(2,1)S(1)}, u32[]{:S(2)}, u32[]{:S(2)}) collective-permute-start(bf16[2,3,160,128]{3,2,1,0:T(8,128)(2,1)S(1)} %get-tuple-element.28), channel_id=1, source_target_pairs={{0,4},{4,0},{8,12},{12,8},{16,20},{20,16},{24,28},{28,24},{1,5},{5... | collective-permute-start | bytes 737288 | tf_op jit(solution)/shard_map/ppermute | solution.py:617
  9.4 7.9 %collective-permute-start.1 = (bf16[2,3,160,128]{3,2,1,0:T(8,128)(2,1)S(1)}, bf16[2,3,160,128]{3,2,1,0:T(8,128)(2,1)S(1)}, u32[]{:S(2)}, u32[]{:S(2)}) collective-permute-start(bf16[2,3,160,128]{3,2,1,0:T(8,128)(2,1)S(1)} %get-tuple-element.29), channel_id=1, source_target_pairs={{0,1},{1,0},{2,3},{3,2},{4,8},{5,9},{6,10},{7,11},{8,4},{9,5},{10,... | collective-permute-start | bytes 737288 | tf_op jit(solution)/shard_map/ppermute | solution.py:616
  10.5 4.1 %copy-start = (bf16[2,2,160,384]{3,2,1,0:T(8,128)(2,1)S(1)}, bf16[2,2,160,384]{3,2,1,0:T(8,128)(2,1)}, u32[]{:S(2)}) copy-start(bf16[2,2,160,384]{3,2,1,0:T(8,128)(2,1)} %context.3) | copy-start | bytes 1474564
  10.5 4.1 %copy-start.1 = (bf16[3,3,256,256]{3,2,1,0:T(8,128)(2,1)S(1)}, bf16[3,3,256,256]{3,2,1,0:T(8,128)(2,1)}, u32[]{:S(2)}) copy-start(bf16[3,3,256,256]{3,2,1,0:T(8,128)(2,1)} %gate_k.3) | copy-start | bytes 3538948
  10.5 4.1 %copy-start.2 = (bf16[2,2,160,128]{3,2,1,0:T(8,128)(2,1)S(1)}, bf16[2,2,160,128]{3,2,1,0:T(8,128)(2,1)}, u32[]{:S(2)}) copy-start(bf16[2,2,160,128]{3,2,1,0:T(8,128)(2,1)} %hidden.3) | copy-start | bytes 491524
  10.5 4.1 %copy-start.3 = (bf16[3,3,256,128]{3,2,1,0:T(8,128)(2,1)S(1)}, bf16[3,3,256,128]{3,2,1,0:T(8,128)(2,1)}, u32[]{:S(2)}) copy-start(bf16[3,3,256,128]{3,2,1,0:T(8,128)(2,1)} %cand_k.3) | copy-start | bytes 1769476
  11.9 5.4 %copy-start.4 = (bf16[128]{0:T(256)(128)(2,1)S(1)}, bf16[128]{0:T(256)(128)(2,1)}, u32[]{:S(2)}) copy-start(bf16[128]{0:T(256)(128)(2,1)} %param.27) | copy-start | bytes 772
  11.9 5.4 %collective-permute-start.6 = (bf16[2,2,176,128]{3,2,1,0:T(8,128)(2,1)S(1)}, bf16[2,2,176,128]{3,2,1,0:T(8,128)(2,1)S(1)}, u32[]{:S(2)}, u32[]{:S(2)}) collective-permute-start(bf16[2,2,176,128]{3,2,1,0:T(8,128)(2,1)S(1)} %shard_map.160.mot), channel_id=1, source_target_pairs={{0,1},{1,0},{2,3},{3,2},{4,8},{5,9},{6,10},{7,11},{8,4},{9,5},{10,... | collective-permute-start | bytes 540680 | tf_op jit(solution)/shard_map/ppermute | solution.py:639
  13.8 3.5 %collective-permute-start.5 = (bf16[2,2,176,128]{3,2,1,0:T(8,128)(2,1)S(1)}, bf16[2,2,176,128]{3,2,1,0:T(8,128)(2,1)S(1)}, u32[]{:S(2)}, u32[]{:S(2)}) collective-permute-start(bf16[2,2,176,128]{3,2,1,0:T(8,128)(2,1)S(1)} %shard_map.160.mot), channel_id=1, source_target_pairs={{0,4},{4,0},{8,12},{12,8},{16,20},{20,16},{24,28},{28,24},{1,5},{5... | collective-permute-start | bytes 540680 | tf_op jit(solution)/shard_map/ppermute | solution.py:640
